TPU v7x, 32 devices: a whole 2x2x4 slice. The times are simulated.
32 devices in a mesh: dp: 8 (over y, x, core), seq: 4 (over z).
Axes of the slice: x: 2, y: 2, z: 4, core: 2. Of those that a mesh axis runs over, the one named last changes fastest.
Arguments:
- hidden_in: bfloat16 [16, 1024, 768], P('dp', 'seq'), may hold values from -6 to 6
- seq_len: int32 [16], P('dp'), may hold values from 64 to 1024, as said below
- bucket: int32 [16], P('dp'), may hold values from 0 to 2, as said below
- in_weight: bfloat16 [768, 2304], P('dp'), may hold values from -0.21875 to 0.21875
- in_bias: float32 [2304], replicated, may hold values from -3 to 3
- short_taps: float32 [3, 2304], replicated, may hold values from -3.5 to 3.5
- cond_taps: float32 [3, 768], replicated, may hold values from -3.5 to 3.5
- mode_residue: float32 [4, 768], replicated, may hold values from -3.5 to 3.5
- mode_rate: float32 [4, 768], replicated, may hold values from 0.0001 to 0.02
- out_weight: bfloat16 [768, 768], P('dp'), may hold values from -0.21875 to 0.21875
- out_bias: float32 [768], replicated, may hold values from -3 to 3
- norm1_gain: float32 [768], replicated, may hold values from 0.5 to 1.5
- norm1_bias: float32 [768], replicated, may hold values from -1.75 to 1.75
- gate_weight: bfloat16 [768, 3072], P('dp'), may hold values from -0.21875 to 0.21875
- up_weight: bfloat16 [768, 3072], P('dp'), may hold values from -0.21875 to 0.21875
- down_weight: bfloat16 [3072, 768], P('dp'), may hold values from -0.109375 to 0.109375
- down_bias: float32 [768], replicated, may hold values from -3 to 3
- norm2_gain: float32 [768], replicated, may hold values from 0.5 to 1.5
- norm2_bias: float32 [768], replicated, may hold values from -1.75 to 1.75
- out_cotangent: bfloat16 [16, 1024, 768], P('dp', 'seq'), may hold values from -6 to 6
Outputs:
- layer_out: bfloat16 [16, 1024, 768], P('dp', 'seq')
- grad_hidden: bfloat16 [16, 1024, 768], P('dp', 'seq')
- grad_in_weight: float32 [768, 2304], P('dp')
- grad_in_bias: float32 [2304], replicated
- grad_short_taps: float32 [3, 2304], replicated
- grad_cond_taps: float32 [3, 768], replicated
- grad_mode_residue: float32 [4, 768], replicated
- grad_mode_rate: float32 [4, 768], replicated
- grad_out_weight: float32 [768, 768], P('dp')
- grad_out_bias: float32 [768], replicated
- grad_norm1_gain: float32 [768], replicated
- grad_norm1_bias: float32 [768], replicated
- grad_gate_weight: float32 [768, 3072], P('dp')
- grad_up_weight: float32 [768, 3072], P('dp')
- grad_down_weight: float32 [3072, 768], P('dp')
- grad_down_bias: float32 [768], replicated
- grad_norm2_gain: float32 [768], replicated
- grad_norm2_bias: float32 [768], replicated
Inputs may be any that keep to these rules, and one draw needn't show every extreme that they name: Of the 2 rows 2 * i to 2 * i + 1, one has bucket 2. seq_len[r] lies between 1024 * 2**bucket[r] // 16 and 1024 * 2**bucket[r] // 4; of the 2 rows 2 * i to 2 * i + 1, one has length 1024.
All inputs are finite; a program needn't handle non-finite values.
Results may differ from a plain program's by a relative error of at most 0.019.
Values may be sent and summed in bfloat16 or wider, within the bound.
No kernel may reach another device: no remote copies, remote signals or barrier semaphores. Data moves between devices by JAX's collectives and lax.ppermute only.
A program may use at most 512 MiB of HBM per device.

v0:
```python
import math

import jax
import jax.numpy as jnp
from jax import lax
from jax.sharding import PartitionSpec as P

norm_eps = 1e-05
block_cap = 32


def with_halo(block, sides, width):
    for axis, dim in sides:
        count = lax.axis_size(axis)
        forward = [(i, i + 1) for i in range(count - 1)]
        backward = [(target, source) for source, target in forward]
        low = lax.ppermute(
            lax.slice_in_dim(block, block.shape[dim] - width, None, axis=dim), axis, forward
        )
        high = lax.ppermute(lax.slice_in_dim(block, 0, width, axis=dim), axis, backward)
        block = jnp.concatenate([low, block, high], axis=dim)
    return block


def gelu_tanh(values):
    return jax.nn.gelu(values, approximate=True)


def outer_sum(left_side, right_side):
    return lax.dot_general(
        left_side, right_side, (((0,), (0,)), ((), ())), preferred_element_type=jnp.float32
    )


def back_product(grad_rows, weight_full):
    return lax.dot_general(
        grad_rows, weight_full, (((1,), (1,)), ((), ())), preferred_element_type=jnp.float32
    )


def norm_forward(values, gain_vec, shifts):
    centre = values - jnp.mean(values, axis=-1, keepdims=True)
    inv_dev = lax.rsqrt(jnp.mean(centre * centre, axis=-1, keepdims=True) + norm_eps)
    normed = centre * inv_dev
    return (normed * gain_vec + shifts, normed, inv_dev)


def norm_backward(grad_out, normed, inv_dev, gain_vec):
    grad_normed = grad_out * gain_vec
    grad_in = inv_dev * (
        grad_normed
        - jnp.mean(grad_normed, axis=-1, keepdims=True)
        - normed * jnp.mean(grad_normed * normed, axis=-1, keepdims=True)
    )
    return (grad_in, jnp.sum(grad_out * normed, axis=0), jnp.sum(grad_out, axis=0))


def row_decays(mode_rate, factors):
    return mode_rate[None] * factors[:, None, None]


def mode_weights(mode_residue, decays):
    return mode_residue[None] * jnp.sqrt(1.0 - jnp.exp(-2.0 * decays))


def local_states(source, decays):
    row_count, row_span, model_width = source.shape
    block_len = math.gcd(block_cap, row_span)
    blocks = row_span // block_len
    pieces = source.reshape(row_count, blocks, block_len, model_width)
    offsets = jnp.arange(block_len, dtype=jnp.float32)
    lag_gap = offsets[:, None] - offsets[None, :]
    inner_lag = jnp.where(
        lag_gap[None, None, :, :, None] >= 0.0,
        jnp.exp(-decays[:, :, None, None, :] * jnp.maximum(lag_gap, 0.0)[None, None, :, :, None]),
        0.0,
    )
    within = jnp.einsum("rmijd,rnjd->rmnid", inner_lag, pieces, precision=lax.Precision.HIGHEST)
    block_ends = within[:, :, :, block_len - 1, :]
    block_ids = jnp.arange(blocks, dtype=jnp.float32)
    block_gap = block_ids[:, None] - block_ids[None, :] - 1.0
    across = jnp.where(
        block_gap[None, None, :, :, None] >= 0.0,
        jnp.exp(
            -decays[:, :, None, None, :]
            * (block_len * jnp.maximum(block_gap, 0.0))[None, None, :, :, None]
        ),
        0.0,
    )
    before = jnp.einsum("rmnkd,rmkd->rmnd", across, block_ends, precision=lax.Precision.HIGHEST)
    rising = jnp.exp(-decays[:, :, None, :] * (offsets + 1.0)[None, None, :, None])
    states = within + rising[:, :, None] * before[:, :, :, None]
    return states.reshape(row_count, decays.shape[1], row_span, model_width)


def finish_states(states, entering, decays, weights_mode):
    row_span = states.shape[2]
    offsets = jnp.arange(row_span, dtype=jnp.float32)
    reach_decay = jnp.exp(-decays[:, :, None, :] * (offsets + 1.0)[None, None, :, None])
    totals = states + reach_decay * entering[:, :, None, :]
    return (jnp.sum(weights_mode[:, :, None, :] * totals, axis=1), totals[:, :, row_span - 1, :])


def mixer_local(source, mode_rate, mode_residue, entering, factors):
    decays = row_decays(mode_rate, factors)
    return finish_states(
        local_states(source, decays), entering, decays, mode_weights(mode_residue, decays)
    )


def spread_states(every_state, block_decay, gaps):
    shaped = gaps[:, None, None, None]
    factor_q = jnp.where(shaped >= 0.0, jnp.exp(-block_decay[None] * jnp.maximum(shaped, 0.0)), 0.0)
    return jnp.sum(factor_q * every_state, axis=0)


def local(
    hidden_in,
    seq_len,
    bucket,
    in_weight,
    in_bias,
    short_taps,
    cond_taps,
    mode_residue,
    mode_rate,
    out_weight,
    out_bias,
    norm1_gain,
    norm1_bias,
    gate_weight,
    up_weight,
    down_weight,
    down_bias,
    norm2_gain,
    norm2_bias,
    out_cotangent,
):
    row_count, row_span, model_width = hidden_in.shape
    seq_count = lax.axis_size("seq")
    seq_place = lax.axis_index("seq")
    first_pos = seq_place * row_span
    positions = first_pos + jnp.arange(row_span, dtype=jnp.int32)
    row_mask = (positions[None, :] < seq_len[:, None]).astype(jnp.float32)
    keep_rows = row_mask.reshape(row_count * row_span, 1)
    mask_cube = row_mask[:, :, None]
    factors = jnp.where(bucket == 0, 4.0, jnp.where(bucket == 1, 2.0, 1.0)).astype(jnp.float32)
    full_in, full_out, full_gate, full_up, full_down = (
        lax.all_gather(in_weight, "dp", axis=0, tiled=True),
        lax.all_gather(out_weight, "dp", axis=0, tiled=True),
        lax.all_gather(gate_weight, "dp", axis=0, tiled=True),
        lax.all_gather(up_weight, "dp", axis=0, tiled=True),
        lax.all_gather(down_weight, "dp", axis=0, tiled=True),
    )
    tokens = hidden_in.reshape(row_count * row_span, model_width)
    projected = jnp.dot(tokens, full_in, preferred_element_type=jnp.float32) + in_bias
    rounded = (
        (projected * keep_rows).astype(jnp.bfloat16).reshape(row_count, row_span, 3 * model_width)
    )
    padded = with_halo(rounded, (("seq", 1),), 2).astype(jnp.float32)
    shorted = (
        short_taps[0] * padded[:, :-2]
        + short_taps[1] * padded[:, 1:-1]
        + short_taps[2] * padded[:, 2:]
    )
    ext_pos = first_pos - 1 + jnp.arange(row_span + 2, dtype=jnp.int32)
    inside = ((ext_pos >= 0) & (ext_pos < seq_count * row_span)).astype(jnp.float32)[None, :, None]
    key_pre = shorted[:, :, model_width : 2 * model_width] * inside
    key_part = (
        cond_taps[0] * key_pre[:, :-2]
        + cond_taps[1] * key_pre[:, 1:-1]
        + cond_taps[2] * key_pre[:, 2:]
    )
    queries = shorted[:, 1:-1, :model_width]
    values_part = shorted[:, 1:-1, 2 * model_width :]
    source = key_part * values_part * mask_cube
    decays = row_decays(mode_rate, factors)
    weights_mode = mode_weights(mode_residue, decays)
    states = local_states(source, decays)
    block_decay = decays * row_span
    leaving_own = states[:, :, row_span - 1, :]
    device_ids = jnp.arange(seq_count, dtype=jnp.float32)
    place_float = seq_place.astype(jnp.float32)
    every_state = lax.all_gather(leaving_own[None], "seq", axis=0, tiled=True)
    entering = spread_states(every_state, block_decay, place_float - 1.0 - device_ids)
    long_out, _ = finish_states(states, entering, decays, weights_mode)
    gated_out = (queries * long_out * mask_cube).astype(jnp.bfloat16)
    gated_flat = gated_out.reshape(row_count * row_span, model_width)
    mixer_out = jnp.dot(gated_flat, full_out, preferred_element_type=jnp.float32) + out_bias
    normed_one_out, normed_one, scale_one = norm_forward(
        tokens.astype(jnp.float32) + mixer_out, norm1_gain, norm1_bias
    )
    first_low = normed_one_out.astype(jnp.bfloat16)
    gate_pre = jnp.dot(first_low, full_gate, preferred_element_type=jnp.float32)
    up_pre = jnp.dot(first_low, full_up, preferred_element_type=jnp.float32)
    gelu_out, gelu_pull = jax.vjp(gelu_tanh, gate_pre)
    active = (gelu_out * up_pre).astype(jnp.bfloat16)
    feed_out = jnp.dot(active, full_down, preferred_element_type=jnp.float32) + down_bias
    result_full, normed_two, scale_two = norm_forward(
        normed_one_out + feed_out, norm2_gain, norm2_bias
    )
    layer_out = (
        (result_full * keep_rows).astype(jnp.bfloat16).reshape(row_count, row_span, model_width)
    )
    grad_top = (
        out_cotangent.reshape(row_count * row_span, model_width).astype(jnp.float32) * keep_rows
    )
    grad_pre_two, grad_gain_two, grad_shift_two = norm_backward(
        grad_top, normed_two, scale_two, norm2_gain
    )
    grad_feed = grad_pre_two.astype(jnp.bfloat16)
    grad_down_bias = jnp.sum(grad_feed.astype(jnp.float32), axis=0)
    grad_down = outer_sum(active, grad_feed)
    grad_active = back_product(grad_feed, full_down)
    grad_gate = gelu_pull(grad_active * up_pre)[0].astype(jnp.bfloat16)
    grad_up = (grad_active * gelu_out).astype(jnp.bfloat16)
    grad_gate_w = outer_sum(first_low, grad_gate)
    grad_up_w = outer_sum(first_low, grad_up)
    grad_first = grad_pre_two + back_product(grad_gate, full_gate) + back_product(grad_up, full_up)
    grad_pre_one, grad_gain_one, grad_shift_one = norm_backward(
        grad_first, normed_one, scale_one, norm1_gain
    )
    grad_mixer = grad_pre_one.astype(jnp.bfloat16)
    grad_out_bias = jnp.sum(grad_mixer.astype(jnp.float32), axis=0)
    grad_out_w = outer_sum(gated_flat, grad_mixer)
    grad_gated = (
        back_product(grad_mixer, full_out).reshape(row_count, row_span, model_width) * mask_cube
    )
    grad_queries = grad_gated * long_out
    grad_long = grad_gated * queries

    def mixer_of(source_in, rate_in, residue_in, enter_in):
        return mixer_local(source_in, rate_in, residue_in, enter_in, factors)

    _, mixer_pull = jax.vjp(mixer_of, source, mode_rate, mode_residue, entering)
    grad_source_a, grad_rate_a, grad_residue_a, grad_enter = mixer_pull(
        (grad_long, jnp.zeros_like(entering))
    )
    every_grad = lax.all_gather(grad_enter[None], "seq", axis=0, tiled=True)
    grad_leaving = spread_states(every_grad, block_decay, device_ids - place_float - 1.0)
    grad_source_b, grad_rate_b, grad_residue_b, _ = mixer_pull(
        (jnp.zeros_like(grad_long), grad_leaving)
    )
    grad_source = (grad_source_a + grad_source_b) * mask_cube
    grad_rate = grad_rate_a + grad_rate_b
    grad_residue = grad_residue_a + grad_residue_b
    sent_grads = jnp.concatenate(
        [grad_queries, grad_source * values_part, grad_source * key_part], axis=2
    ).astype(jnp.bfloat16)
    rim_grads = with_halo(sent_grads, (("seq", 1),), 2).astype(jnp.float32)
    grad_key_rim = rim_grads[:, :, model_width : 2 * model_width]
    grad_key_pre = (
        cond_taps[0] * grad_key_rim[:, 2:]
        + cond_taps[1] * grad_key_rim[:, 1:-1]
        + cond_taps[2] * grad_key_rim[:, :-2]
    ) * inside
    own_keys = grad_key_rim[:, 2:-2]
    grad_cond = jnp.stack(
        [
            jnp.sum(own_keys * key_pre[:, offset : offset + row_span], axis=(0, 1))
            for offset in range(3)
        ]
    )
    grad_short_ext = jnp.concatenate(
        [rim_grads[:, 1:-1, :model_width], grad_key_pre, rim_grads[:, 1:-1, 2 * model_width :]],
        axis=2,
    )
    own_short = grad_short_ext[:, 1:-1]
    grad_short = jnp.stack(
        [
            jnp.sum(own_short * padded[:, offset + 1 : offset + 1 + row_span], axis=(0, 1))
            for offset in range(3)
        ]
    )
    grad_rounded = (
        short_taps[0] * grad_short_ext[:, 2:]
        + short_taps[1] * grad_short_ext[:, 1:-1]
        + short_taps[2] * grad_short_ext[:, :-2]
    )
    grad_proj = (grad_rounded.reshape(row_count * row_span, 3 * model_width) * keep_rows).astype(
        jnp.bfloat16
    )
    grad_in_bias = jnp.sum(grad_proj.astype(jnp.float32), axis=0)
    grad_in_w = outer_sum(tokens, grad_proj)
    grad_tokens = (
        (grad_pre_one + back_product(grad_proj, full_in))
        .astype(jnp.bfloat16)
        .reshape(row_count, row_span, model_width)
    )
    (
        sum_in_bias,
        sum_short,
        sum_cond,
        sum_residue,
        sum_rate,
        sum_out_bias,
        sum_gain_one,
        sum_shift_one,
        sum_down_bias,
        sum_gain_two,
        sum_shift_two,
    ) = lax.psum(
        (
            grad_in_bias,
            grad_short,
            grad_cond,
            grad_residue,
            grad_rate,
            grad_out_bias,
            grad_gain_one,
            grad_shift_one,
            grad_down_bias,
            grad_gain_two,
            grad_shift_two,
        ),
        ("dp", "seq"),
    )
    large_grads = (grad_in_w, grad_out_w, grad_gate_w, grad_up_w, grad_down)
    shares = (
        lax.psum_scatter(
            large_grads[0].astype(jnp.bfloat16), "dp", scatter_dimension=0, tiled=True
        ).astype(jnp.float32),
        lax.psum_scatter(
            large_grads[1].astype(jnp.bfloat16), "dp", scatter_dimension=0, tiled=True
        ).astype(jnp.float32),
        lax.psum_scatter(
            large_grads[2].astype(jnp.bfloat16), "dp", scatter_dimension=0, tiled=True
        ).astype(jnp.float32),
        lax.psum_scatter(
            large_grads[3].astype(jnp.bfloat16), "dp", scatter_dimension=0, tiled=True
        ).astype(jnp.float32),
        lax.psum_scatter(
            large_grads[4].astype(jnp.bfloat16), "dp", scatter_dimension=0, tiled=True
        ).astype(jnp.float32),
    )
    shares = (
        lax.psum(shares[0].astype(jnp.bfloat16), "seq").astype(jnp.float32),
        lax.psum(shares[1].astype(jnp.bfloat16), "seq").astype(jnp.float32),
        lax.psum(shares[2].astype(jnp.bfloat16), "seq").astype(jnp.float32),
        lax.psum(shares[3].astype(jnp.bfloat16), "seq").astype(jnp.float32),
        lax.psum(shares[4].astype(jnp.bfloat16), "seq").astype(jnp.float32),
    )
    share_in, share_out, share_gate, share_up, share_down = shares
    return (
        layer_out,
        grad_tokens,
        share_in,
        sum_in_bias,
        sum_short,
        sum_cond,
        sum_residue,
        sum_rate,
        share_out,
        sum_out_bias,
        sum_gain_one,
        sum_shift_one,
        share_gate,
        share_up,
        share_down,
        sum_down_bias,
        sum_gain_two,
        sum_shift_two,
    )


def solution(mesh):
    in_specs = (
        P("dp", "seq", None),
        P("dp"),
        P("dp"),
        P("dp", None),
        P(),
        P(),
        P(),
        P(),
        P(),
        P("dp", None),
        P(),
        P(),
        P(),
        P("dp", None),
        P("dp", None),
        P("dp", None),
        P(),
        P(),
        P(),
        P("dp", "seq", None),
    )
    out_specs = (
        P("dp", "seq", None),
        P("dp", "seq", None),
        P("dp", None),
        P(),
        P(),
        P(),
        P(),
        P(),
        P("dp", None),
        P(),
        P(),
        P(),
        P("dp", None),
        P("dp", None),
        P("dp", None),
        P(),
        P(),
        P(),
    )
    return jax.shard_map(local, mesh=mesh, in_specs=in_specs, out_specs=out_specs, check_vma=False)
```

profile of v0, /device:TPU:0, one launch (start us, length us, event | category | flops | bytes accessed | tf_op | source)
XLA Modules:
  0.0 2086.9 jit_solution(8374242711818871342)
XLA Ops:
  20.4 31.9 %fusion.169 = f32[2,4,32,32,768]{3,2,1,4,0:T(8,128)} fusion(f32[32,32]{1,0:T(8,128)S(1)} %fusion.94, f32[2,4,768]{1,2,0:T(8,128)S(1)} %copy.209, pred[32,32]{1,0:T(8,128)(4,1)S(1)} %fusion.95), kind=kLoop, calls=%fused_computation.7.clone.clone.1 | loop fusion | flops 12582912 | bytes 25195520 | tf_op jit(solution)/shard_map/transpose(jvp(rmijd,rnjd->rmnid))/dot_general | solution.py:78
  77.6 395.2 %fusion.32 = f32[2,4,8,32,768]{3,2,1,4,0:T(8,128)} fusion(f32[2,8,32,768,1]{2,1,4,3,0:T(8,128)} %copy.248, f32[32,32]{1,0:T(8,128)S(1)} %fusion.94, f32[2,4,768]{1,2,0:T(8,128)S(1)} %copy.209, pred[32,32]{1,0:T(8,128)(4,1)S(1)} %fusion.95), kind=kOutput, calls=%fused_computation.44 | convolution fusion | flops 616562688 | bytes 7894016 | tf_op jit(solution)/shard_map/rmijd,rnjd->rmnid/dot_general | solution.py:78
  472.8 19.0 slice.159
  491.8 17.4 copy.276
  511.8 18.9 multiply_add_fusion.2
  530.7 19.4 copy.214
  551.0 13.7 all-gather
  566.1 34.7 %multiply_reduce_fusion.4 = f32[2,8,32,768]{2,1,3,0:T(8,128)} fusion(f32[2,4,768]{1,2,0:T(8,128)} %copy.216, f32[8,32]{1,0:T(8,128)S(1)} %add_add_fusion.3, f32[2,4,768]{1,2,0:T(8,128)} %copy-done.5, f32[2,4,768]{1,2,0:T(8,128)} %copy.208, f32[2,4,8,32,768]{3,2,1,4,0:T(8,128)} %fusion.32, f32[2,4,8,768]{2,1,3,0:T(4,128)S(1)} %bitcast.179, ...), kind=kLoop, calls=%fused_computation.33 | loop fusion | flops 10616832 | bytes 8922112 | tf_op jit(solution)/shard_map/reduce_sum | solution.py:101
  614.4 7.8 fusion.122
  622.1 11.6 multiply_convert_fusion.1
  633.7 6.6 fusion.121
  644.2 12.5 multiply_convert_fusion
  673.7 6.7 fusion.38
  680.4 13.5 all-gather.1
  699.2 7.0 multiply_reduce_fusion.5
  710.7 20.4 copy.222
  731.1 168.0 %multiply_reduce_fusion.1 = (f32[2,4,768]{1,2,0:T(8,128)}, f32[2,4,768]{1,2,0:T(8,128)}, f32[2,4,32,768]{2,1,3,0:T(4,128)}, f32[2,4,8,768]{2,1,3,0:T(4,128)}, f3...) fusion(f32[2,4,768]{1,2,0:T(8,128)} %copy.216, f32[8,32]{1,0:T(8,128)S(1)} %add_add_fusion.3, ...), kind=kLoop, calls=%fused_computation.30 | loop fusion | flops 27807744 | bytes 17228800 | tf_op jit(solution)/shard_map/transpose(jvp())/reduce_sum | solution.py:101
  905.0 6.7 add_bitcast_fusion
  911.7 20.4 copy.224
  932.0 19.8 copy.219
  951.8 19.5 fusion.171
  971.4 125.7 %fusion.5 = f32[2,768,8,32,1]{3,2,4,1,0:T(8,128)} fusion(f32[2,768,8,4,32]{4,2,3,1,0:T(8,128)} %copy.224, f32[2,4,32,32,768]{3,2,1,4,0:T(8,128)} %fusion.169), kind=kOutput, calls=%fused_computation.8 | convolution fusion | flops 603979776 | bytes 33030144 | tf_op jit(solution)/shard_map/transpose(jvp(rmijd,rnjd->rmnid))/dot_general | solution.py:78
  1097.1 127.5 %fusion.46 = f32[2,8,32,768]{2,1,3,0:T(8,128)} fusion(f32[2,768,8,32,1]{3,2,4,1,0:T(8,128)} %fusion.5, f32[32,32]{1,0:T(8,128)S(1)} %copy-done.45, f32[2,4,768]{1,2,0:T(8,128)S(1)} %copy-done.6, pred[32,32]{1,0:T(8,128)(4,1)S(1)} %copy-done.64, f32[2,768,8,4,32]{4,2,3,1,0:T(8,128)} %fusion.171), kind=kOutput, calls=%fused_computation.58 | convolution fusion | flops 616955904 | bytes 9466880 | tf_op jit(solution)/shard_map/transpose(jvp(rmijd,rnjd->rmnid))/dot_general | solution.py:78
  1256.0 5.9 copy.281
  1263.9 7.0 convolution_convert_fusion.1
  1272.1 6.5 convolution_convert_fusion.2
  1278.7 7.2 convolution_convert_fusion
  1285.9 245.9 %fusion.1 = f32[2,4,768]{1,2,0:T(8,128)} fusion(f32[32,32]{1,0:T(8,128)S(1)} %copy-done.45, f32[2,4,768]{1,2,0:T(8,128)S(1)} %copy-done.6, pred[32,32]{1,0:T(8,128)(4,1)S(1)} %copy-done.64, f32[2,768,8,4,32]{4,2,3,1,0:T(8,128)} %copy.224, f32[2,8,32,768,1]{2,1,4,3,0:T(8,128)} %copy.248), kind=kOutput, calls=%fused_computation.2 | convolution fusion | flops 635430912 | bytes 7918592 | tf_op jit(solution)/shard_map/transpose(jvp(rmijd,rnjd->rmnid))/dot_general | solution.py:78
  1532.5 9.9 multiply_reduce_fusion.6
  1550.3 259.3 %fusion.3 = f32[2,4,768]{1,2,0:T(8,128)} fusion(f32[32,32]{1,0:T(8,128)S(1)} %copy-done.45, f32[2,4,768]{1,2,0:T(8,128)S(1)} %copy-done.6, pred[32,32]{1,0:T(8,128)(4,1)S(1)} %copy-done.65, f32[2,8,32,768,1]{2,1,4,3,0:T(8,128)} %copy.248, f32[2,4,8,1,768]{3,2,1,4,0:T(8,128)} %copy.219, f32[2,8,32,768]{2,1,3,0:T(8,128)} %copy.218, f32[2,4,768]{1,2,0:T(8,128)S(1)} %copy-done.16), kind=kOutput, calls=%fused_computation.5 | convolution fusion | flops 638576640 | bytes 3421184 | tf_op jit(solution)/shard_map/transpose(jvp(rmijd,rnjd->rmnid))/dot_general | solution.py:78
  1834.1 126.0 %all-reduce.8.cloned.1.call-done = (f32[2304]{0:T(1024)}, f32[3,2304]{1,0:T(4,128)}, f32[3,768]{1,0:T(4,128)}, f32[4,768]{0,1:T(8,128)}, f32[4,768]{0,1:T(8,128)...) async-done(((f32[2304]{0:T(1024)}, f32[3,2304]{1,0:T(4,128)}, f32[3,768]{1,0:T(4,128)}, ...) | async-done | bytes 89104 | tf_op jit(solution)/shard_map/psum | solution.py:302
  1963.7 101.4 %all-reduce.10.cloned.1.call-done = (bf16[96,2304]{0,1:T(8,128)(2,1)}, bf16[96,768]{1,0:T(8,128)(2,1)}, bf16[96,3072]{1,0:T(8,128)(2,1)}, bf16[96,3072]{1,0:T(8,128)(2,1)}, bf16[384,768]{1,0:T(8,128)(2,1)}) async-done(((bf16[96,2304]{0,1:T(8,128)(2,1)}, bf16[96,768]{1,0:T(8,128)(2,1)}, bf16[96,3072]{1,0:T(8,128)(2,1)}, bf16[96,3072]{1,0:T(8,128)(2,1)}, bf16[384,768]{1,0:T(8,128)(2,1)}), ...) | async-done | bytes 2359312 | tf_op jit(solution)/shard_map/psum | solution.py:337
  (355 shorter events, 178.6 us)
Async XLA Ops:
  7.2 45.1 %all-gather.8.cloned.1.call-start = ((), (), s32[]{:S(2)}) async-start(), calls=%async_computation.5 | async-start | bytes 3981312 | tf_op jit(solution)/shard_map/all_gather | solution.py:149
  7.9 601.4 %all-gather.10.cloned.1.call-start = ((), (), s32[]{:S(2)}) async-start(), calls=%async_computation.6 | async-start | bytes 1327104 | tf_op jit(solution)/shard_map/all_gather | solution.py:150
  8.7 605.7 %all-gather.12.cloned.1.call-start = ((), (), s32[]{:S(2)}) async-start(), calls=%async_computation.7 | async-start | bytes 5308416 | tf_op jit(solution)/shard_map/all_gather | solution.py:151
  9.4 612.7 %all-gather.14.cloned.1.call-start = ((), (), s32[]{:S(2)}) async-start(), calls=%async_computation.8 | async-start | bytes 5308416 | tf_op jit(solution)/shard_map/all_gather | solution.py:152
  10.0 623.7 %all-gather.16.cloned.1.call-start = ((), (), s32[]{:S(2)}) async-start(), calls=%async_computation.9 | async-start | bytes 5308416 | tf_op jit(solution)/shard_map/all_gather | solution.py:153
  10.6 1815.0 %reduce-scatter.16.cloned.1.call-start = ((), (), s32[]{:S(2)}) async-start(), calls=%async_computation.14 | async-start | bytes 3981312
  11.3 892.2 %copy-start.79 = (pred[8,8]{1,0:T(8,128)(4,1)}, pred[8,8]{1,0:T(8,128)(4,1)S(1)}, u32[]{:S(2)}) copy-start(pred[8,8]{1,0:T(8,128)(4,1)S(1)} %fusion.96) | copy-start | bytes 196
  11.9 891.5 %copy-start.62 = (f32[8,8]{1,0:T(8,128)}, f32[8,8]{1,0:T(8,128)S(1)}, u32[]{:S(2)}) copy-start(f32[8,8]{1,0:T(8,128)S(1)} %maximum_multiply_fusion) | copy-start | bytes 772
  13.4 655.1 %copy-start.42 = (f32[2,256]{1,0:T(2,128)}, f32[2,256]{1,0:T(2,128)S(1)}, u32[]{:S(2)}) copy-start(f32[2,256]{1,0:T(2,128)S(1)} %get-tuple-element.238) | copy-start | bytes 6148
  13.4 628.5 %copy-start.57 = (f32[1,2,2,128]{3,1,2,0:T(2,128)}, f32[1,2,2,128]{3,1,2,0:T(2,128)S(1)}, u32[]{:S(2)}) copy-start(f32[1,2,2,128]{3,1,2,0:T(2,128)S(1)} %copy.292) | copy-start | bytes 6148
  16.7 682.4 %copy-start.29 = (f32[2,4,768]{2,1,0:T(4,128)}, f32[2,4,768]{2,1,0:T(4,128)S(1)}, u32[]{:S(2)}) copy-start(f32[2,4,768]{2,1,0:T(4,128)S(1)} %get-tuple-element.234) | copy-start | bytes 73732
  56.6 8.1 collective-permute-start
  61.6 5.7 collective-permute-start.1
  971.4 125.7 %copy-start.6 = (f32[2,4,768]{1,2,0:T(8,128)S(1)}, f32[2,4,768]{1,2,0:T(8,128)}, u32[]{:S(2)}) copy-start(f32[2,4,768]{1,2,0:T(8,128)} %copy-done.5) | copy-start | bytes 73732
  971.4 125.7 %copy-start.45 = (f32[32,32]{1,0:T(8,128)S(1)}, f32[32,32]{1,0:T(8,128)}, u32[]{:S(2)}) copy-start(f32[32,32]{1,0:T(8,128)} %copy-done.44) | copy-start | bytes 12292
  971.4 125.7 %copy-start.64 = (pred[32,32]{1,0:T(8,128)(4,1)S(1)}, pred[32,32]{1,0:T(8,128)(4,1)}, u32[]{:S(2)}) copy-start(pred[32,32]{1,0:T(8,128)(4,1)} %copy-done.63) | copy-start | bytes 3076
  1232.8 3.3 collective-permute-start.2
  1234.6 5.7 collective-permute-start.3
  1262.0 565.7 %reduce-scatter.8.cloned.1.call-start = ((), (), s32[]{:S(2)}) async-start(), calls=%async_computation.10 | async-start | bytes 1327104 | tf_op jit(solution)/shard_map/reduce_scatter | solution.py:323
  1263.9 563.8 %reduce-scatter.12.cloned.1.call-start = ((), (), s32[]{:S(2)}) async-start(), calls=%async_computation.12 | async-start | bytes 5308416 | tf_op jit(solution)/shard_map/reduce_scatter | solution.py:329
  1270.9 556.8 %reduce-scatter.10.cloned.1.call-start = ((), (), s32[]{:S(2)}) async-start(), calls=%async_computation.11 | async-start | bytes 5308416 | tf_op jit(solution)/shard_map/reduce_scatter | solution.py:326
  1278.7 549.0 %reduce-scatter.14.cloned.1.call-start = ((), (), s32[]{:S(2)}) async-start(), calls=%async_computation.13 | async-start | bytes 5308416 | tf_op jit(solution)/shard_map/reduce_scatter | solution.py:332
  1531.8 428.3 %all-reduce.8.cloned.1.call-start = ((), (), s32[]{:S(2)}) async-start(), calls=%async_computation.15 | async-start | bytes 1744896 | tf_op jit(solution)/shard_map/psum | solution.py:302
  1550.2 261.4 %copy-start.26 = (f32[2,4,768,8]{2,3,1,0:T(8,128)S(1)}, f32[2,4,768,8]{2,3,1,0:T(8,128)}, u32[]{:S(2)}) copy-start(f32[2,4,768,8]{2,3,1,0:T(8,128)} %copy-done.25) | copy-start | bytes 589828
  1550.2 261.4 %copy-start.30 = (f32[2,4,768]{2,1,0:T(4,128)S(1)}, f32[2,4,768]{2,1,0:T(4,128)}, u32[]{:S(2)}) copy-start(f32[2,4,768]{2,1,0:T(4,128)} %copy-done.29) | copy-start | bytes 73732
  1550.2 263.3 %copy-start.38 = (f32[2,4,768]{2,1,0:T(4,128)S(1)}, f32[2,4,768]{2,1,0:T(4,128)}, u32[]{:S(2)}) copy-start(f32[2,4,768]{2,1,0:T(4,128)} %get-tuple-element.232) | copy-start | bytes 73732
  1825.5 239.5 %all-reduce.10.cloned.1.call-start = ((), (), s32[]{:S(2)}) async-start(), calls=%async_computation.16 | async-start | bytes 5013504 | tf_op jit(solution)/shard_map/psum | solution.py:337
  1960.1 116.7 %copy-start.74 = (f32[768]{0:T(1024)S(1)}, f32[768]{0:T(1024)}, u32[]{:S(2)}) copy-start(f32[768]{0:T(1024)} %get-tuple-element.259) | copy-start | bytes 9220
  1960.1 117.3 %copy-start.73 = (f32[768]{0:T(1024)S(1)}, f32[768]{0:T(1024)}, u32[]{:S(2)}) copy-start(f32[768]{0:T(1024)} %get-tuple-element.260) | copy-start | bytes 9220
  1960.1 117.9 %copy-start.72 = (f32[768]{0:T(1024)S(1)}, f32[768]{0:T(1024)}, u32[]{:S(2)}) copy-start(f32[768]{0:T(1024)} %get-tuple-element.264) | copy-start | bytes 9220
  1960.1 118.5 %copy-start.71 = (f32[768]{0:T(1024)S(1)}, f32[768]{0:T(1024)}, u32[]{:S(2)}) copy-start(f32[768]{0:T(1024)} %get-tuple-element.265) | copy-start | bytes 9220
  1960.2 119.1 %copy-start.70 = (f32[768]{0:T(1024)S(1)}, f32[768]{0:T(1024)}, u32[]{:S(2)}) copy-start(f32[768]{0:T(1024)} %get-tuple-element.266) | copy-start | bytes 9220
  (81 other events, 1664.6 us)
Sparse Core Ops, SparseCore 0:
  9.9 36.6 all-gather.7
  48.5 24.0 all-gather.9
  74.5 38.9 all-gather.11
  115.2 38.9 all-gather.13
  155.9 38.9 all-gather.15
  1262.1 48.1 reduce-scatter.15
  1314.1 36.7 reduce-scatter.7
  1354.7 53.9 reduce-scatter.11
  1412.1 53.8 reduce-scatter.9
  1532.0 53.8 reduce-scatter.13
  1825.7 134.3 all-reduce.7
  1963.5 101.4 all-reduce.9
where the time goes:
time: 2100 us; the launch traced here: 2090 us
  matrix products  1240 us (59%)
  other arithmetic  360 us (17%)
  waiting for transfers between devices  238 us (11%)
  local copies, waits for them, and re-layouts  200 us (10%)
  blocking collectives  27.2 us (1%)
    dot_general x5, matrix products, local_states(): jnp.einsum('rmijd,rnjd->rmnid', inner_lag, pieces, precision=lax.Precisio...  1150 us
    reduce_sum x1, other arithmetic, finish_states(): weights_mode[:, :, None, :] * totals  168 us
    psum x1, waiting for transfers between devices, local(): lax.psum((grad_in_bias, grad_short, grad_cond, grad_residue, grad_rate, g...  126 us
    psum x1, waiting for transfers between devices, local(): lax.psum(shares[0].astype(jnp.bfloat16), 'seq').astype(jnp.float32)  101 us
    unnamed x217, local copies, waits for them, and re-layouts  57.6 us
    dot_general x2, other arithmetic, local_states(): jnp.einsum('rmijd,rnjd->rmnid', inner_lag, pieces, precision=lax.Precisio...  51.5 us
  transfers between devices with their start and end apart: 16, of which 5 were waited for; matrix products, arithmetic and copies ran while one was open for 56% of the time, Pallas kernels for 0%

commit v1 on v0

v1 whole, which is shorter than its diff:
```python
import jax
import jax.numpy as jnp
from jax import lax
from jax.experimental import pallas as pl
from jax.experimental.pallas import tpu as pltpu
from jax.sharding import PartitionSpec as P

norm_eps = 1e-05
f32 = jnp.float32
bf16 = jnp.bfloat16
segs = 8
lane_block = 256
vmem_cap = 56 * 1024 * 1024


def iota(shape, dim):
    return lax.broadcasted_iota(jnp.int32, shape, dim)


def factor_of(info, rows, r):
    b = info[rows + r]
    return jnp.where(b == 0, 4.0, jnp.where(b == 1, 2.0, 1.0)).astype(f32)


def order_matrix(span):
    seg = span // segs
    o, n = iota((span, span), 0), iota((span, span), 1)
    return (n == (o & (segs - 1)) * seg + lax.shift_right_logical(o, 3)).astype(f32).astype(bf16)


def fill_edges(ext, r, seg, halo, cols):
    n = cols[1]
    c = pl.ds(cols[0], n)
    sub = iota((segs, n), 0)
    for h, (dst, src, shift, edge) in enumerate(
        ((0, seg, 1, 0), (1, seg + 1, 1, 0), (seg + 2, 2, segs - 1, segs - 1), (seg + 3, 3, segs - 1, segs - 1))
    ):
        rolled = pltpu.roll(ext[r, src, :, c], shift, 0)
        ext[r, dst, :, c] = jnp.where(sub == edge, halo[pl.ds(4 * r + h, 1), c], rolled)


def fetch_parts(where, parts, full, sems):
    depth = parts[0].shape[0]
    return [
        pltpu.make_async_copy(
            part, full.at[pl.ds(pl.multiple_of(where[k] * depth, 16), depth)], sems.at[k]
        )
        for k, part in enumerate(parts)
    ]


def start_all(copies):
    for copy in copies:
        copy.start()


def wait_all(copies):
    for copy in copies:
        copy.wait()


def send_parts(where, full, outs, sems, cols=None):
    per, depth = outs[0].shape[0], outs[0].shape[1]
    copies = []
    for k in range(per * len(outs)):
        rows_of = pl.ds(pl.multiple_of(where[k] * depth, 16), depth)
        src, dst = full.at[rows_of], outs[k // per].at[k % per]
        if cols is not None:
            src, dst = full.at[rows_of, cols], outs[k // per].at[k % per, :, cols]
        copies.append(pltpu.make_async_copy(src, dst, sems.at[k]))
    return copies


def enter_kernel(rows, span, seq_count, count, info, where, x, cot, xh, bias, st, ct, rate, *refs):
    parts, refs = refs[:count], refs[count:]
    xp, xpt, cp, ext, q, keys, vals, ends, dev_end, mask, hal, w, sems = refs
    copies = fetch_parts(where, parts, w, sems)
    start_all(copies)
    width = x.shape[2]
    seg = span // segs
    place = info[2 * rows]
    base = place * span
    order = order_matrix(span)
    for r in range(rows):
        moved = jnp.dot(order, x[r], preferred_element_type=f32).astype(bf16)
        xp[pl.ds(r * span, span), :] = moved
        xpt[:, pl.ds(r * span, span)] = moved.T
        cp[pl.ds(r * span, span), :] = jnp.dot(order, cot[r], preferred_element_type=f32).astype(bf16)
        n = iota((span, 128), 0)
        pos = base + (n & (segs - 1)) * seg + lax.shift_right_logical(n, 3)
        mask[pl.ds(r * span, span), :] = (pos < info[r]).astype(f32)
    hn = iota((16, 128), 0)
    hk = hn & 3
    hpos = base + jnp.where(hk < 2, hk - 2, span + hk - 2)
    hlim = jnp.where(lax.shift_right_logical(hn, 2) == 0, info[0], info[1])
    hmask = ((hpos >= 0) & (hpos < hlim)).astype(f32)
    wait_all(copies)

    @pl.loop(0, 3 * width // lane_block)
    def _(t):
        cols = pl.ds(pl.multiple_of(t * lane_block, lane_block), lane_block)
        part = jnp.dot(xp[...], w[:, cols], preferred_element_type=f32) + bias[:, cols]
        rim = jnp.dot(xh[...], w[:, cols], preferred_element_type=f32) + bias[:, cols]
        for s in range(lane_block // 128):
            sub = slice(s * 128, (s + 1) * 128)
            scol = pl.ds(pl.multiple_of(t * lane_block + s * 128, 128), 128)
            low = (part[:, sub] * mask[...]).astype(bf16).astype(f32)
            for r in range(rows):
                ext[r, pl.ds(2, seg), :, scol] = low[r * span : (r + 1) * span].reshape(seg, segs, 128)
            hal[:, scol] = (rim[:, sub] * hmask).astype(bf16).astype(f32)

    sub = iota((segs, lane_block), 0)
    first = (place == 0).astype(f32)
    last = (place == seq_count - 1).astype(f32)
    in_low = 1.0 - first * (sub == 0).astype(f32)
    in_high = 1.0 - last * (sub == segs - 1).astype(f32)
    for r in range(rows):
        factor = factor_of(info, rows, r)
        for t in range(3 * width // lane_block):
            fill_edges(ext, r, seg, hal, (t * lane_block, lane_block))
        for t in range(width // lane_block):
            cq = pl.ds(t * lane_block, lane_block)
            ck = pl.ds(width + t * lane_block, lane_block)
            cv = pl.ds(2 * width + t * lane_block, lane_block)
            modes = rate.shape[0]
            fade = [jnp.exp(-rate[pl.ds(m, 1), cq] * factor) for m in range(modes)]
            far = [jnp.exp(-rate[pl.ds(m, 1), cq] * (factor * seg)) for m in range(modes)]

            def tap3(cols, e):
                return (
                    st[pl.ds(0, 1), cols] * ext[r, e - 1, :, cols]
                    + st[pl.ds(1, 1), cols] * ext[r, e, :, cols]
                    + st[pl.ds(2, 1), cols] * ext[r, e + 1, :, cols]
                )

            def step(j, carry):
                kp_prev, kp_cur, states = carry
                kp_next = tap3(ck, j + 3)
                kp_next = jnp.where(j == seg - 1, kp_next * in_high, kp_next)
                key = (
                    ct[pl.ds(0, 1), cq] * kp_prev
                    + ct[pl.ds(1, 1), cq] * kp_cur
                    + ct[pl.ds(2, 1), cq] * kp_next
                )
                val = tap3(cv, j + 2)
                q[r, j, :, cq] = tap3(cq, j + 2)
                keys[r, j, :, cq] = key
                vals[r, j, :, cq] = val
                live = (base + sub * seg + j < info[r]).astype(f32)
                src = key * val * live
                return (kp_cur, kp_next, tuple(f * h + src for f, h in zip(fade, states)))

            zero = jnp.zeros((segs, lane_block), f32)
            start = (tap3(ck, 1) * in_low, tap3(ck, 2), (zero,) * modes)
            _, _, states = lax.fori_loop(0, seg, step, start)
            for m in range(modes):
                ends[r, m, :, cq] = states[m]
                total = jnp.zeros((1, lane_block), f32)
                for i in range(segs):
                    total = far[m] * total + states[m][i : i + 1]
                dev_end[r, pl.ds(m, 1), cq] = total


def vm(shape, dtype=f32):
    return jax.ShapeDtypeStruct(shape, dtype)


def vmem_specs(n):
    return [pl.BlockSpec(memory_space=pltpu.VMEM)] * n


def smem_spec():
    return [pl.BlockSpec(memory_space=pltpu.SMEM)]


def cost(flops, nbytes):
    return pl.CostEstimate(flops=int(flops), bytes_accessed=int(nbytes), transcendentals=0)


def any_specs(n):
    return [pl.BlockSpec(memory_space=pl.ANY)] * n


def mixer_enter(info, where, hidden, cot, halo, bias, st, ct, rate, parts, seq_count):
    rows, span, width = hidden.shape
    seg, modes, tokens = span // segs, rate.shape[0], rows * span
    body = (rows, seg, segs, width)
    return pl.pallas_call(
        lambda *refs: enter_kernel(rows, span, seq_count, len(parts), *refs),
        out_shape=(
            vm((tokens, width), bf16),
            vm((width, tokens), bf16),
            vm((tokens, width), bf16),
            vm((rows, seg + 4, segs, 3 * width)),
            vm(body),
            vm(body),
            vm(body),
            vm((rows, modes, segs, width)),
            vm((rows, modes, width)),
        ),
        in_specs=smem_spec() * 2 + vmem_specs(7) + any_specs(len(parts)),
        out_specs=tuple(vmem_specs(9)),
        scratch_shapes=[
            pltpu.VMEM((tokens, 128), f32),
            pltpu.VMEM((16, 3 * width), f32),
            pltpu.VMEM((width, 3 * width), bf16),
            pltpu.SemaphoreType.DMA((len(parts),)),
        ],
        compiler_params=pltpu.CompilerParams(vmem_limit_bytes=vmem_cap),
        cost_estimate=cost(2 * tokens * width * width * 3, 20e6),
        name="mixer_enter",
    )(info, where, hidden, cot, halo, bias, st, ct, rate, *parts)


def carry_in(parts, fade_span):
    total = parts[0]
    scale = fade_span
    for p in parts[1:]:
        total = total + scale * p
        scale = scale * fade_span
    return total


def settle_kernel(rows, span, others, count, info, where, *refs):
    gath, refs = refs[:others], refs[others:]
    parts, refs = refs[:count], refs[count:]
    ends, q, keys, vals, rate, res, xp, ob, long_out, gated_t, carry_out, n1, s1, gsc, wo, sems = refs
    copies = fetch_parts(where, parts, wo, sems)
    start_all(copies)
    seg = span // segs
    width = q.shape[3]
    modes = rate.shape[0]
    base = info[2 * rows] * span
    sub = iota((segs, lane_block), 0)
    for r in range(rows):
        factor = factor_of(info, rows, r)
        for t in range(width // lane_block):
            c = pl.ds(t * lane_block, lane_block)
            fade, mix, start = [], [], []
            for m in range(modes):
                d = rate[pl.ds(m, 1), c] * factor
                fade.append(jnp.exp(-d))
                mix.append(res[pl.ds(m, 1), c] * jnp.sqrt(1.0 - jnp.exp(-2.0 * d)))
                far = jnp.exp(-d * seg)
                cur = carry_in([g[r, pl.ds(m, 1), c] for g in gath], jnp.exp(-d * span))
                tile = jnp.zeros((segs, lane_block), f32)
                end = ends[r, m, :, c]
                for i in range(segs):
                    tile = jnp.where(sub == i, cur, tile)
                    cur = far * cur + end[i : i + 1]
                carry_out[r, m, :, c] = tile
                start.append(tile)

            def step(j, states):
                live = (base + sub * seg + j < info[r]).astype(f32)
                src = keys[r, j, :, c] * vals[r, j, :, c] * live
                states = tuple(f * h + src for f, h in zip(fade, states))
                out = mix[0] * states[0]
                for m in range(1, modes):
                    out = out + mix[m] * states[m]
                long_out[r, j, :, c] = out
                gsc[r, j, :, c] = q[r, j, :, c] * out * live
                return states

            lax.fori_loop(0, seg, step, tuple(start))
    wait_all(copies)
    for r in range(rows):
        tok = pl.ds(r * span, span)
        low = gsc[r].reshape(span, width).astype(bf16)
        gated_t[:, tok] = low.T
        n1[tok, :] = xp[tok, :].astype(f32) + jnp.dot(low, wo[...], preferred_element_type=f32) + ob[...]

    @pl.loop(0, rows * span // 16)
    def _(k):
        tok = pl.ds(pl.multiple_of(k * 16, 16), 16)
        v = n1[tok, :]
        centre = v - jnp.mean(v, axis=-1, keepdims=True)
        inv = lax.rsqrt(jnp.mean(centre * centre, axis=-1, keepdims=True) + norm_eps)
        n1[tok, :] = centre * inv
        s1[tok, :] = jnp.broadcast_to(inv, (16, 128))


def mixer_settle(info, where, gath, ends, q, keys, vals, rate, res, xp, ob, parts):
    rows, seg, _, width = q.shape
    span = seg * segs
    tokens, modes = rows * span, rate.shape[0]
    return pl.pallas_call(
        lambda *refs: settle_kernel(rows, span, len(gath), len(parts), *refs),
        out_shape=(
            vm(q.shape),
            vm((width, tokens), bf16),
            vm(ends.shape),
            vm((tokens, width)),
            vm((tokens, 128)),
        ),
        in_specs=smem_spec() * 2 + vmem_specs(len(gath)) + any_specs(len(parts)) + vmem_specs(8),
        out_specs=tuple(vmem_specs(5)),
        scratch_shapes=[
            pltpu.VMEM(q.shape, f32),
            pltpu.VMEM((width, width), bf16),
            pltpu.SemaphoreType.DMA((len(parts),)),
        ],
        compiler_params=pltpu.CompilerParams(vmem_limit_bytes=vmem_cap),
        cost_estimate=cost(2 * tokens * width * width, 12e6),
        name="mixer_settle",
    )(info, where, *gath, *parts, ends, q, keys, vals, rate, res, xp, ob)


def gelu_kernel(count, where, n1, gain, shift, *refs):
    gate_parts, up_parts, refs = refs[:count], refs[count : 2 * count], refs[2 * count :]
    low_t, act, act_t, pull, gel, wg, wu, low, gs, us, sems = refs
    tile = act.shape[1]
    i = pl.program_id(0)

    @pl.when(i == 0)
    def _():
        gate_copies = fetch_parts(where, gate_parts, wg, sems.at[0])
        up_copies = fetch_parts(where, up_parts, wu, sems.at[1])
        start_all(gate_copies)
        start_all(up_copies)
        low[...] = (n1[...] * gain[...] + shift[...]).astype(bf16)
        low_t[...] = low[...].T
        wait_all(gate_copies)
        wait_all(up_copies)

    cols = pl.ds(pl.multiple_of(i * tile, tile), tile)
    gs[...] = jnp.dot(low[...], wg[:, cols], preferred_element_type=f32)
    us[...] = jnp.dot(low[...], wu[:, cols], preferred_element_type=f32)
    scale = 0.7978845608028654

    @pl.loop(0, act.shape[0] // 16)
    def _(k):
        tok = pl.ds(pl.multiple_of(k * 16, 16), 16)
        g, u = gs[tok, :], us[tok, :]
        sq = g * g
        th = jnp.tanh(g * (scale + (scale * 0.044715) * sq))
        half = 0.5 + 0.5 * th
        gelu = g * half
        slope = half + (0.5 * g) * (1.0 - th * th) * (scale + (3.0 * scale * 0.044715) * sq)
        act[tok, :] = (gelu * u).astype(bf16)
        pull[tok, :] = (u * slope).astype(bf16)
        gel[tok, :] = gelu.astype(bf16)

    act_t[...] = act[...].T


def feed_gelu(where, n1, gain, shift, gate_parts, up_parts, hidden):
    tokens, width = n1.shape
    tile = 512
    block = pl.BlockSpec((tokens, tile), lambda i: (0, i))
    count = len(gate_parts)

    def fixed(shape):
        return pl.BlockSpec(shape, lambda i: (0,) * len(shape))

    return pl.pallas_call(
        lambda *refs: gelu_kernel(count, *refs),
        grid=(hidden // tile,),
        out_shape=(
            vm((width, tokens), bf16),
            vm((tokens, hidden), bf16),
            vm((hidden, tokens), bf16),
            vm((tokens, hidden), bf16),
            vm((tokens, hidden), bf16),
        ),
        in_specs=smem_spec()
        + [fixed((tokens, width)), fixed((1, width)), fixed((1, width))]
        + any_specs(2 * count),
        out_specs=(
            fixed((width, tokens)),
            block,
            pl.BlockSpec((tile, tokens), lambda i: (i, 0)),
            block,
            block,
        ),
        scratch_shapes=[
            pltpu.VMEM((width, hidden), bf16),
            pltpu.VMEM((width, hidden), bf16),
            pltpu.VMEM((tokens, width), bf16),
            pltpu.VMEM((tokens, tile), f32),
            pltpu.VMEM((tokens, tile), f32),
            pltpu.SemaphoreType.DMA((2, count)),
        ],
        compiler_params=pltpu.CompilerParams(vmem_limit_bytes=vmem_cap),
        cost_estimate=cost(4 * tokens * width * hidden, 24e6),
        name="feed_gelu",
    )(where, n1, gain, shift, *gate_parts, *up_parts)


def row_mean(v):
    return jnp.mean(v, axis=-1, keepdims=True)


def fold(v):
    return v[:8] + v[8:]


def down_kernel(rows, span, count, outs, info, where, slots, *refs):
    parts, refs = refs[:count], refs[count:]
    act, act_t, n1, gain1, shift1, bias, gain2, shift2, cp = refs[:9]
    layer, pre2, feed, sums = refs[9:13]
    dws, refs = refs[13 : 13 + outs], refs[13 + outs :]
    wd, acc, low, dw, sems, out_sems = refs
    copies = fetch_parts(where, parts, wd, sems)
    start_all(copies)
    hidden, width = wd.shape
    wait_all(copies)
    for t in range(width // lane_block):
        c = pl.ds(t * lane_block, lane_block)
        acc[:, c] = jnp.dot(act[...], wd[:, c], preferred_element_type=f32)
    zero = jnp.zeros((8, width), f32)
    base = info[2 * rows] * span
    seg = span // segs

    def step(k, loop):
        tok = pl.ds(pl.multiple_of(k * 16, 16), 16)
        n = iota((16, width), 0) + k * 16
        r = lax.shift_right_logical(n, span.bit_length() - 1)
        n = n & (span - 1)
        pos = base + (n & (segs - 1)) * seg + lax.shift_right_logical(n, 3)
        limit = jnp.where(k * 16 >= span, info[1], info[0])
        keep = (pos < limit).astype(f32)
        v = n1[tok, :] * gain1[...] + shift1[...] + acc[tok, :] + bias[...]
        centre = v - row_mean(v)
        inv = lax.rsqrt(row_mean(centre * centre) + norm_eps)
        n2 = centre * inv
        low[tok, :] = ((n2 * gain2[...] + shift2[...]) * keep).astype(bf16)
        top = cp[tok, :].astype(f32) * keep
        e = top * gain2[...]
        grad = inv * (e - row_mean(e) - n2 * row_mean(e * n2))
        pre2[tok, :] = grad
        cut = grad.astype(bf16)
        feed[tok, :] = cut
        return (
            loop[0] + fold(cut.astype(f32)),
            loop[1] + fold(top * n2),
            loop[2] + fold(top),
        )

    totals = lax.fori_loop(0, rows * span // 16, step, (zero, zero, zero))
    for k in range(3):
        sums[pl.ds(k, 1), :] = jnp.sum(totals[k], axis=0, keepdims=True)
    o, n = iota((span, span), 0), iota((span, span), 1)
    back = (o == (n & (segs - 1)) * seg + lax.shift_right_logical(n, 3)).astype(f32).astype(bf16)
    block = 512
    for b in range(hidden // block):
        c = pl.ds(b * block, block)
        dw[c, :] = jnp.dot(act_t[c, :], feed[...], preferred_element_type=f32).astype(bf16)
    sends = send_parts(slots, dw, dws, out_sems)
    start_all(sends)
    for r in range(rows):
        layer[r] = jnp.dot(back, low[pl.ds(r * span, span), :], preferred_element_type=f32).astype(bf16)
    wait_all(sends)


def feed_down(info, where, slots, act, act_t, n1, gain1, shift1, bias, gain2, shift2, cp, parts, rows, dw_shapes):
    tokens, width = n1.shape
    span, hidden = tokens // rows, act.shape[1]
    count, outs = len(parts), len(dw_shapes)
    return pl.pallas_call(
        lambda *refs: down_kernel(rows, span, count, outs, *refs),
        out_shape=(
            vm((rows, span, width), bf16),
            vm((tokens, width)),
            vm((tokens, width), bf16),
            vm((8, width)),
        )
        + tuple(vm(s, bf16) for s in dw_shapes),
        in_specs=smem_spec() * 3 + any_specs(count) + vmem_specs(9),
        out_specs=tuple(vmem_specs(4)) + tuple(any_specs(outs)),
        scratch_shapes=[
            pltpu.VMEM((hidden, width), bf16),
            pltpu.VMEM((tokens, width), f32),
            pltpu.VMEM((tokens, width), bf16),
            pltpu.VMEM((hidden, width), bf16),
            pltpu.SemaphoreType.DMA((count,)),
            pltpu.SemaphoreType.DMA((outs * dw_shapes[0][0],)),
        ],
        compiler_params=pltpu.CompilerParams(vmem_limit_bytes=vmem_cap),
        cost_estimate=cost(4 * tokens * width * hidden, 24e6),
        name="feed_down",
    )(info, where, slots, *parts, act, act_t, n1, gain1, shift1, bias, gain2, shift2, cp)


def contract_last(a, b):
    return lax.dot_general(a, b, (((1,), (1,)), ((), ())), preferred_element_type=f32)


def inner_kernel(count, outs, where, slots, *refs):
    down, gate, up = (refs[k * count : (k + 1) * count] for k in range(3))
    refs = refs[3 * count :]
    feed, low_t, pre2, pull, gel = refs[:5]
    first = refs[5]
    dgs, dus = refs[6 : 6 + outs], refs[6 + outs : 6 + 2 * outs]
    wd, wg, wu, dg, du, sems, out_sems = refs[6 + 2 * outs :]
    i, steps = pl.program_id(0), pl.num_programs(0)
    tile = pull.shape[1]

    def weights(which):
        return [
            copy
            for k, parts, full in ((0, down, wd), (1, gate, wg), (2, up, wu))
            if k in which
            for copy in fetch_parts(where, parts, full, sems.at[k])
        ]

    @pl.when(i == 0)
    def _():
        start_all(weights((0, 1, 2)))
        first[...] = pre2[...]
        wait_all(weights((0,)))

    cols = pl.ds(pl.multiple_of(i * tile, tile), tile)
    act = contract_last(feed[...], wd[cols, :])
    g = (act * pull[...].astype(f32)).astype(bf16)
    u = (act * gel[...].astype(f32)).astype(bf16)
    dg[:, cols] = jnp.dot(low_t[...], g, preferred_element_type=f32).astype(bf16)
    du[:, cols] = jnp.dot(low_t[...], u, preferred_element_type=f32).astype(bf16)

    @pl.when(i == 0)
    def _():
        wait_all(weights((1, 2)))

    first[...] += contract_last(g, wg[:, cols]) + contract_last(u, wu[:, cols])

    @pl.when(i == steps - 1)
    def _():
        sends = send_parts(slots, dg, dgs, out_sems.at[0]) + send_parts(slots, du, dus, out_sems.at[1])
        start_all(sends)
        wait_all(sends)


def feed_inner(where, slots, down, gate, up, feed, low_t, pre2, pull, gel, dw_shapes):
    tokens, width = pre2.shape
    hidden = pull.shape[1]
    tile = 384
    count, outs = len(down), len(dw_shapes)
    block = pl.BlockSpec((tokens, tile), lambda i: (0, i))

    def fixed(shape):
        return pl.BlockSpec(shape, lambda i: (0,) * len(shape))

    return pl.pallas_call(
        lambda *refs: inner_kernel(count, outs, *refs),
        grid=(hidden // tile,),
        out_shape=(vm((tokens, width)),) + tuple(vm(s, bf16) for s in dw_shapes * 2),
        in_specs=smem_spec() * 2
        + any_specs(3 * count)
        + [fixed((tokens, width)), fixed((width, tokens)), fixed((tokens, width)), block, block],
        out_specs=(fixed((tokens, width)),) + tuple(any_specs(2 * outs)),
        scratch_shapes=[
            pltpu.VMEM((hidden, width), bf16),
            pltpu.VMEM((width, hidden), bf16),
            pltpu.VMEM((width, hidden), bf16),
            pltpu.VMEM((width, hidden), bf16),
            pltpu.VMEM((width, hidden), bf16),
            pltpu.SemaphoreType.DMA((3, count)),
            pltpu.SemaphoreType.DMA((2, outs * dw_shapes[0][0])),
        ],
        compiler_params=pltpu.CompilerParams(vmem_limit_bytes=vmem_cap),
        cost_estimate=cost(10 * tokens * width * hidden, 32e6),
        name="feed_inner",
    )(where, slots, *down, *gate, *up, feed, low_t, pre2, pull, gel)


def back_kernel(rows, span, count, outs, info, where, slots, *refs):
    parts, refs = refs[:count], refs[count:]
    first, n1, s1, gain, gated_t, q, rate = refs[:7]
    pre1, gg, ends, dev_end, sums = refs[7:12]
    dws = refs[12 : 12 + outs]
    wo, mix, dw, sems, out_sems = refs[12 + outs :]
    copies = fetch_parts(where, parts, wo, sems)
    start_all(copies)
    seg = span // segs
    width, modes = q.shape[3], rate.shape[0]
    base = info[2 * rows] * span
    zero = jnp.zeros((8, width), f32)

    def norm_step(k, loop):
        tok = pl.ds(pl.multiple_of(k * 16, 16), 16)
        top, n = first[tok, :], n1[tok, :]
        e = top * gain[...]
        grad = s1[tok, 0:1] * (e - row_mean(e) - n * row_mean(e * n))
        pre1[tok, :] = grad
        cut = grad.astype(bf16)
        mix[tok, :] = cut
        return (
            loop[0] + fold(cut.astype(f32)),
            loop[1] + fold(top * n),
            loop[2] + fold(top),
        )

    totals = lax.fori_loop(0, rows * span // 16, norm_step, (zero, zero, zero))
    for k in range(3):
        sums[pl.ds(k, 1), :] = jnp.sum(totals[k], axis=0, keepdims=True)
    dw[...] = jnp.dot(gated_t[...], mix[...], preferred_element_type=f32).astype(bf16)
    sends = send_parts(slots, dw, dws, out_sems)
    start_all(sends)
    wait_all(copies)
    for r in range(rows):
        gg[r] = contract_last(mix[pl.ds(r * span, span), :], wo[...]).reshape(seg, segs, width)
    sub = iota((segs, lane_block), 0)
    for r in range(rows):
        factor = factor_of(info, rows, r)
        for t in range(width // lane_block):
            c = pl.ds(t * lane_block, lane_block)
            fade = [jnp.exp(-rate[pl.ds(m, 1), c] * factor) for m in range(modes)]
            far = [jnp.exp(-rate[pl.ds(m, 1), c] * (factor * seg)) for m in range(modes)]

            def step(k, states):
                j = seg - 1 - k
                live = (base + sub * seg + j < info[r]).astype(f32)
                grad = gg[r, j, :, c] * live
                gg[r, j, :, c] = grad
                g = grad * q[r, j, :, c]
                return tuple(f * h + g for f, h in zip(fade, states))

            blank = jnp.zeros((segs, lane_block), f32)
            states = lax.fori_loop(0, seg, step, (blank,) * modes)
            for m in range(modes):
                ends[r, m, :, c] = states[m]
                total = jnp.zeros((1, lane_block), f32)
                for i in reversed(range(segs)):
                    total = far[m] * total + states[m][i : i + 1]
                dev_end[r, pl.ds(m, 1), c] = total
    wait_all(sends)


def mixer_back(info, where, slots, parts, first, n1, s1, gain, gated_t, q, rate, dw_shapes):
    rows, seg, _, width = q.shape
    modes = rate.shape[0]
    tokens = rows * seg * segs
    count, outs = len(parts), len(dw_shapes)
    return pl.pallas_call(
        lambda *refs: back_kernel(rows, seg * segs, count, outs, *refs),
        out_shape=(
            vm((tokens, width)),
            vm(q.shape),
            vm((rows, modes, segs, width)),
            vm((rows, modes, width)),
            vm((8, width)),
        )
        + tuple(vm(s, bf16) for s in dw_shapes),
        in_specs=smem_spec() * 3 + any_specs(count) + vmem_specs(7),
        out_specs=tuple(vmem_specs(5)) + tuple(any_specs(outs)),
        scratch_shapes=[
            pltpu.VMEM((width, width), bf16),
            pltpu.VMEM((tokens, width), bf16),
            pltpu.VMEM((width, width), bf16),
            pltpu.SemaphoreType.DMA((count,)),
            pltpu.SemaphoreType.DMA((outs * dw_shapes[0][0],)),
        ],
        compiler_params=pltpu.CompilerParams(vmem_limit_bytes=vmem_cap),
        cost_estimate=cost(4 * tokens * width * width, 12e6),
        name="mixer_back",
    )(info, where, slots, *parts, first, n1, s1, gain, gated_t, q, rate)


def source_kernel(rows, span, others, info, *refs):
    gath = refs[:others]
    (ends, carry, gg, q, long_out, keys, vals, rate, res, gm, rim, gres, grate, hist) = refs[others:]
    seg = span // segs
    width, modes = q.shape[3], rate.shape[0]
    base = info[2 * rows] * span
    sub = iota((segs, lane_block), 0)
    for t in range(width // lane_block):
        c = pl.ds(t * lane_block, lane_block)
        sum_res = [jnp.zeros((1, lane_block), f32) for _ in range(modes)]
        sum_rate = [jnp.zeros((1, lane_block), f32) for _ in range(modes)]
        for r in range(rows):
            factor = factor_of(info, rows, r)
            fade, mix, start, root, ebb = [], [], [], [], []
            for m in range(modes):
                d = rate[pl.ds(m, 1), c] * factor
                fade.append(jnp.exp(-d))
                ebb.append(jnp.exp(-2.0 * d))
                root.append(jnp.sqrt(1.0 - ebb[m]))
                mix.append(res[pl.ds(m, 1), c] * root[m])
                far = jnp.exp(-d * seg)
                cur = carry_in([g[r, pl.ds(m, 1), c] for g in gath], jnp.exp(-d * span))
                tile = jnp.zeros((segs, lane_block), f32)
                end = ends[r, m, :, c]
                for i in reversed(range(segs)):
                    tile = jnp.where(sub == i, cur, tile)
                    cur = far * cur + end[i : i + 1]
                start.append(tile)

            def ahead(j, loop):
                states, sums = loop
                live = (base + sub * seg + j < info[r]).astype(f32)
                src = keys[r, j, :, c] * vals[r, j, :, c] * live
                g = gg[r, j, :, c] * q[r, j, :, c]
                past = tuple(f * h for f, h in zip(fade, states))
                for m in range(modes):
                    hist[m, j] = past[m]
                states = tuple(p + src for p in past)
                return (states, tuple(s + g * h for s, h in zip(sums, states)))

            zero = jnp.zeros((segs, lane_block), f32)
            init = tuple(carry[r, m, :, c] for m in range(modes))
            _, with_state = lax.fori_loop(0, seg, ahead, (init, (zero,) * modes))

            def behind(k, loop):
                states, sums = loop
                j = seg - 1 - k
                live = (base + sub * seg + j < info[r]).astype(f32)
                grad = gg[r, j, :, c]
                g = grad * q[r, j, :, c]
                states = tuple(f * h + g for f, h in zip(fade, states))
                gs = mix[0] * states[0]
                for m in range(1, modes):
                    gs = gs + mix[m] * states[m]
                gs = gs * live
                for b, part in enumerate(
                    (grad * long_out[r, j, :, c], gs * vals[r, j, :, c], gs * keys[r, j, :, c])
                ):
                    gm[r, j + 2, :, pl.ds(b * width + t * lane_block, lane_block)] = part.astype(bf16).astype(f32)
                return (states, tuple(s + h * hist[m, j] for m, (s, h) in enumerate(zip(sums, states))))

            _, with_lag = lax.fori_loop(0, seg, behind, (tuple(start), (zero,) * modes))
            for m in range(modes):
                u = jnp.sum(with_state[m], axis=0, keepdims=True)
                v = jnp.sum(with_lag[m], axis=0, keepdims=True)
                sum_res[m] = sum_res[m] + root[m] * u
                sum_rate[m] = sum_rate[m] + factor * res[pl.ds(m, 1), c] * (ebb[m] / root[m] * u - root[m] * v)
        for m in range(modes):
            gres[pl.ds(m, 1), c] = sum_res[m]
            grate[pl.ds(m, 1), c] = sum_rate[m]
    for r in range(rows):
        for h, (j, i) in enumerate(((0, 0), (1, 0), (seg - 2, segs - 1), (seg - 1, segs - 1))):
            rim[pl.ds(4 * r + h, 1), :] = gm[r, j + 2, pl.ds(i, 1), :]


def mixer_source(info, gath, ends, carry, gg, q, long_out, keys, vals, rate, res):
    rows, seg, _, width = q.shape
    modes = rate.shape[0]
    return pl.pallas_call(
        lambda *refs: source_kernel(rows, seg * segs, len(gath), *refs),
        out_shape=(
            vm((rows, seg + 4, segs, 3 * width)),
            vm((4 * rows, 3 * width)),
            vm((modes, width)),
            vm((modes, width)),
        ),
        in_specs=smem_spec() + vmem_specs(9 + len(gath)),
        out_specs=tuple(vmem_specs(4)),
        scratch_shapes=[pltpu.VMEM((modes, seg, segs, lane_block), f32)],
        compiler_params=pltpu.CompilerParams(vmem_limit_bytes=vmem_cap),
        cost_estimate=cost(1e6, 16e6),
        name="mixer_source",
    )(info, *gath, ends, carry, gg, q, long_out, keys, vals, rate, res)


def taps_kernel(rows, span, seq_count, count, outs, info, where, slots, gm_in, *refs):
    parts, refs = refs[:count], refs[count:]
    halo, ext, st, ct, xpt, pre1, hidden_grad, gshort, gcond, gbias = refs[:10]
    dws, refs = refs[10 : 10 + outs], refs[10 + outs :]
    gsc, gm, gp, w, dw, low, sem, sems, out_sems = refs
    seg = span // segs
    fetch = pltpu.make_async_copy(gm_in, gm, sem)
    fetch.start()
    copies = fetch_parts(where, parts, w, sems)
    start_all(copies)
    fetch.wait()
    width = ct.shape[1]
    place = info[2 * rows]
    base = place * span
    sub = iota((segs, lane_block), 0)
    in_low = 1.0 - (place == 0).astype(f32) * (sub == 0).astype(f32)
    in_high = 1.0 - (place == seq_count - 1).astype(f32) * (sub == segs - 1).astype(f32)
    zero = jnp.zeros((segs, lane_block), f32)
    for r in range(rows):
        for t in range(3 * width // lane_block):
            fill_edges(gm, r, seg, halo, (t * lane_block, lane_block))
    for block in range(3):
        for t in range(width // lane_block):
            at = block * width + t * lane_block
            c = pl.ds(at, lane_block)
            cc = pl.ds(t * lane_block, lane_block)
            sums = tuple(zero for _ in range(4))
            csums = tuple(zero for _ in range(3))
            for r in range(rows):

                def tap3(e):
                    return (
                        st[pl.ds(0, 1), c] * ext[r, e - 1, :, c]
                        + st[pl.ds(1, 1), c] * ext[r, e, :, c]
                        + st[pl.ds(2, 1), c] * ext[r, e + 1, :, c]
                    )

                def back3(e):
                    return (
                        ct[pl.ds(0, 1), cc] * gm[r, e + 1, :, c]
                        + ct[pl.ds(1, 1), cc] * gm[r, e, :, c]
                        + ct[pl.ds(2, 1), cc] * gm[r, e - 1, :, c]
                    )

                def grad_at(e):
                    return back3(e) if block == 1 else gm[r, e, :, c]

                def step(j, loop):
                    prev, cur, kp_prev, kp_cur, sums, csums = loop
                    nxt = grad_at(j + 3)
                    if block == 1:
                        nxt = jnp.where(j == seg - 1, nxt * in_high, nxt)
                        kp_next = tap3(j + 3)
                        kp_next = jnp.where(j == seg - 1, kp_next * in_high, kp_next)
                        own = gm[r, j + 2, :, c]
                        csums = tuple(s + own * k for s, k in zip(csums, (kp_prev, kp_cur, kp_next)))
                    else:
                        kp_next = kp_cur
                    live = (base + sub * seg + j < info[r]).astype(f32)
                    full = (
                        st[pl.ds(0, 1), c] * nxt + st[pl.ds(1, 1), c] * cur + st[pl.ds(2, 1), c] * prev
                    ) * live
                    full = full.astype(bf16).astype(f32)
                    gsc[r, j] = full
                    sums = (
                        sums[0] + cur * ext[r, j + 1, :, c],
                        sums[1] + cur * ext[r, j + 2, :, c],
                        sums[2] + cur * ext[r, j + 3, :, c],
                        sums[3] + full,
                    )
                    return (cur, nxt, kp_cur, kp_next, sums, csums)

                if block == 1:
                    start = (grad_at(1) * in_low, grad_at(2), tap3(1) * in_low, tap3(2), sums, csums)
                else:
                    start = (grad_at(1), grad_at(2), zero, zero, sums, csums)
                _, _, _, _, sums, csums = lax.fori_loop(0, seg, step, start)
                gp[pl.ds(r * span, span), c] = gsc[r].reshape(span, lane_block).astype(bf16)
            for k in range(3):
                gshort[pl.ds(k, 1), c] = jnp.sum(sums[k], axis=0, keepdims=True)
            gbias[:, c] = jnp.sum(sums[3], axis=0, keepdims=True)
            if block == 1:
                for k in range(3):
                    gcond[pl.ds(k, 1), cc] = jnp.sum(csums[k], axis=0, keepdims=True)


    for t in range(3 * width // 768):
        c = pl.ds(t * 768, 768)
        dw[:, c] = jnp.dot(xpt[...], gp[:, c], preferred_element_type=f32).astype(bf16)
    sends = send_parts(slots, dw, dws, out_sems)
    start_all(sends)
    wait_all(copies)
    low[...] = (contract_last(gp[...], w[...]) + pre1[...]).astype(bf16)
    o, n = iota((span, span), 0), iota((span, span), 1)
    back = (o == (n & (segs - 1)) * seg + lax.shift_right_logical(n, 3)).astype(f32).astype(bf16)
    for r in range(rows):
        moved = jnp.dot(back, low[pl.ds(r * span, span), :], preferred_element_type=f32)
        hidden_grad[r] = moved.astype(bf16)
    wait_all(sends)


def mixer_taps(info, where, slots, gm, parts, halo, ext, st, ct, xpt, pre1, seq_count, dw_shapes):
    rows, padded, _, wide = ext.shape
    seg, width = padded - 4, wide // 3
    tokens = rows * seg * segs
    count, outs = len(parts), len(dw_shapes)
    return pl.pallas_call(
        lambda *refs: taps_kernel(rows, seg * segs, seq_count, count, outs, *refs),
        out_shape=(
            vm((rows, seg * segs, width), bf16),
            vm((3, wide)),
            vm((3, width)),
            vm((1, wide)),
        )
        + tuple(vm(s, bf16) for s in dw_shapes),
        in_specs=smem_spec() * 3 + any_specs(1 + count) + vmem_specs(6),
        out_specs=tuple(vmem_specs(4)) + tuple(any_specs(outs)),
        scratch_shapes=[
            pltpu.VMEM((rows, seg, segs, lane_block), f32),
            pltpu.VMEM(gm.shape, f32),
            pltpu.VMEM((tokens, wide), bf16),
            pltpu.VMEM((width, wide), bf16),
            pltpu.VMEM((width, wide), bf16),
            pltpu.VMEM((tokens, width), bf16),
            pltpu.SemaphoreType.DMA,
            pltpu.SemaphoreType.DMA((count,)),
            pltpu.SemaphoreType.DMA((outs * dw_shapes[0][0],)),
        ],
        compiler_params=pltpu.CompilerParams(vmem_limit_bytes=vmem_cap),
        cost_estimate=cost(4 * tokens * width * wide, 20e6),
        name="mixer_taps",
    )(info, where, slots, gm, *parts, halo, ext, st, ct, xpt, pre1)


def chip_pairs(count):
    first = [(d, d ^ (2 if d % 2 == 0 else 4)) for d in range(count)]
    second = [(d, d ^ (4 if d % 2 == 0 else 2)) for d in range(count)]
    core = [(d, d ^ 1) for d in range(count)]
    return core, first, second


def gather_shards(shard):
    core, first, second = chip_pairs(8)
    p1 = lax.ppermute(shard, "dp", first)
    p2 = lax.ppermute(shard, "dp", second)
    p3 = lax.ppermute(p1, "dp", second)
    near = [shard, p1, p2, p3]
    return near + [lax.ppermute(p, "dp", core) for p in near]


def shard_order(me):
    even = (me & 1) == 0
    f = jnp.where(even, 2, 4)
    g = jnp.where(even, 4, 2)
    near = [me, me ^ f, me ^ g, me ^ 6]
    far = [me ^ 1, me ^ 1 ^ g, me ^ 1 ^ f, me ^ 7]
    return jnp.stack(near + far).astype(jnp.int32)


def slot_order(me):
    even = (me & 1) == 0
    f = jnp.where(even, 2, 4)
    g = jnp.where(even, 4, 2)
    mine = [me, me ^ g, me ^ f, me ^ 6]
    theirs = [me ^ 1, me ^ 1 ^ f, me ^ 1 ^ g, me ^ 7]
    return jnp.stack(mine + theirs).astype(jnp.int32)


def scatter_sum(mine, theirs):
    core, first, second = chip_pairs(8)
    got = lax.ppermute(theirs, "dp", core)
    send = (mine[2:].astype(f32) + got[2:].astype(f32)).astype(bf16)
    got1 = lax.ppermute(send, "dp", first)
    keep = mine[:2].astype(f32) + got[:2].astype(f32) + got1.astype(f32)
    got2 = lax.ppermute(keep[1].astype(bf16), "dp", second)
    return (keep[0] + got2.astype(f32)).astype(bf16)


def line_sum(own):
    odd = (lax.axis_index("seq") & 1) == 1
    half = own.shape[0] // 2
    low, high = own[:half], own[half:]
    keep, send = jnp.where(odd, high, low), jnp.where(odd, low, high)
    near = [(i, i ^ 1) for i in range(4)]
    h1 = lax.ppermute(send, "seq", near)
    part = (keep.astype(f32) + h1.astype(f32)).astype(bf16)
    h2 = lax.ppermute(part, "seq", [(i, i ^ 2) for i in range(4)])
    total = (part.astype(f32) + h2.astype(f32)).astype(bf16)
    h3 = lax.ppermute(total, "seq", near)
    return jnp.concatenate([jnp.where(odd, h3, total), jnp.where(odd, total, h3)]).astype(f32)


def small_sum(flat):
    for bit in (1, 2, 4):
        flat = flat + lax.ppermute(flat, "dp", [(d, d ^ bit) for d in range(8)])
    for bit in (1, 2):
        flat = flat + lax.ppermute(flat, "seq", [(d, d ^ bit) for d in range(4)])
    return flat


def local(
    hidden_in,
    seq_len,
    bucket,
    in_weight,
    in_bias,
    short_taps,
    cond_taps,
    mode_residue,
    mode_rate,
    out_weight,
    out_bias,
    norm1_gain,
    norm1_bias,
    gate_weight,
    up_weight,
    down_weight,
    down_bias,
    norm2_gain,
    norm2_bias,
    out_cotangent,
):
    rows, span, width = hidden_in.shape
    tokens, seg = rows * span, span // segs
    dp_count, seq_count = lax.axis_size("dp"), lax.axis_size("seq")
    me, place = lax.axis_index("dp"), lax.axis_index("seq")
    info = jnp.concatenate([seq_len, bucket, place[None]]).astype(jnp.int32)
    chips = dp_count == 8
    up_line = [(i, i + 1) for i in range(seq_count - 1)]
    down_line = [(i + 1, i) for i in range(seq_count - 1)]

    def rims(low, high):
        before = lax.ppermute(high, "seq", up_line)
        after = lax.ppermute(low, "seq", down_line)
        return jnp.concatenate([before, after], axis=1).reshape(rows * 4, -1)

    def whole(shard):
        if not chips:
            return [lax.all_gather(shard, "dp", axis=0, tiled=True)]
        return gather_shards(shard)

    def dw_shapes(shard):
        depth, wide = shard.shape
        return ((4, depth, wide),) * 2 if chips else ((1, depth * dp_count, wide),)

    def line(vec):
        return vec[None]

    where = shard_order(me) if chips else jnp.zeros((1,), jnp.int32)
    slots = slot_order(me) if chips else where
    halo = rims(hidden_in[:, :2], hidden_in[:, span - 2 :])
    halo = jnp.pad(halo, ((0, 16 - rows * 4), (0, 0)))
    in_parts = whole(in_weight)
    out_parts = whole(out_weight)
    gate_parts = whole(gate_weight)
    up_parts = whole(up_weight)
    down_parts = whole(down_weight)

    xp, xpt, cp, ext, q, keys, vals, ends, dev_end = mixer_enter(
        info, where, hidden_in, out_cotangent, halo, line(in_bias), short_taps, cond_taps, mode_rate,
        in_parts, seq_count,
    )
    gath = [
        lax.ppermute(dev_end, "seq", [(i, i + k) for i in range(seq_count - k)])
        for k in range(1, seq_count)
    ]
    long_out, gated_t, carry, n1, s1 = mixer_settle(
        info, where, gath, ends, q, keys, vals, mode_rate, mode_residue, xp, line(out_bias), out_parts
    )
    low_t, act, act_t, pull, gel = feed_gelu(
        where, n1, line(norm1_gain), line(norm1_bias), gate_parts, up_parts, gate_weight.shape[1]
    )
    layer_out, pre2, feed, sums_two, *g_down = feed_down(
        info, where, slots, act, act_t, n1, line(norm1_gain), line(norm1_bias), line(down_bias),
        line(norm2_gain), line(norm2_bias), cp, down_parts, rows, dw_shapes(down_weight),
    )
    first, *g_inner = feed_inner(
        where, slots, down_parts, gate_parts, up_parts, feed, low_t, pre2, pull, gel, dw_shapes(gate_weight)
    )
    g_gate, g_up = g_inner[: len(g_inner) // 2], g_inner[len(g_inner) // 2 :]
    pre1, gg, back_ends, back_dev, sums_one, *g_out = mixer_back(
        info, where, slots, out_parts, first, n1, s1, line(norm1_gain), gated_t, q, mode_rate,
        dw_shapes(out_weight),
    )
    back_gath = [
        lax.ppermute(back_dev, "seq", [(i + k, i) for i in range(seq_count - k)])
        for k in range(1, seq_count)
    ]
    gm, rim, g_res, g_rate = mixer_source(
        info, back_gath, back_ends, carry, gg, q, long_out, keys, vals, mode_rate, mode_residue
    )
    rim = rim.astype(bf16).reshape(rows, 4, 3 * width)
    g_halo = rims(rim[:, :2], rim[:, 2:]).astype(f32)
    grad_hidden, g_short, g_cond, g_in_bias, *g_in = mixer_taps(
        info, where, slots, gm, in_parts, g_halo, ext, short_taps, cond_taps, xpt, pre1, seq_count,
        dw_shapes(in_weight),
    )

    small = (g_in_bias[0], g_short, g_cond, g_res, g_rate, sums_one[:3], sums_two[:3])
    flat = jnp.concatenate([s.reshape(-1, width) for s in small])
    if chips and seq_count == 4:
        flat = small_sum(flat)
    else:
        flat = lax.psum(flat, ("dp", "seq"))
    sums, at = [], 0
    for s in small:
        n = s.size // width
        sums.append(flat[at : at + n].reshape(s.shape))
        at += n

    def share(grad):
        if chips:
            own = scatter_sum(*grad)
        else:
            own = lax.psum_scatter(grad[0][0], "dp", scatter_dimension=0, tiled=True)
        if seq_count == 4:
            return line_sum(own)
        return lax.psum(own, "seq").astype(f32)

    share_down, share_gate, share_up, share_out, share_in = map(share, (g_down, g_gate, g_up, g_out, g_in))
    return (
        layer_out, grad_hidden, share_in, sums[0], sums[1], sums[2], sums[3], sums[4], share_out,
        sums[5][0], sums[5][1], sums[5][2], share_gate, share_up, share_down, sums[6][0], sums[6][1],
        sums[6][2],
    )


def solution(mesh):
    split, weight, full = P("dp", "seq", None), P("dp", None), P()
    in_specs = (
        split, P("dp"), P("dp"), weight, full, full, full, full, full, weight,
        full, full, full, weight, weight, weight, full, full, full, split,
    )
    out_specs = (
        split, split, weight, full, full, full, full, full, weight, full,
        full, full, weight, weight, weight, full, full, full,
    )
    return jax.shard_map(local, mesh=mesh, in_specs=in_specs, out_specs=out_specs, check_vma=False)
```

time: 2100 us -> 464 us (0.22)
  matrix products: 1240 us -> 0 us
  other arithmetic: 360 us -> 23.5 us
  local copies, waits for them, and re-layouts: 200 us -> 18.7 us
  Pallas kernels: 0 us -> 158 us
  starting transfers between devices: 9.86 us -> 65.4 us
  waiting for transfers between devices: 238 us -> 196 us
  blocking collectives: 27.2 us -> 0 us
    dot_general x20 -> x0, matrix products: 1240 us -> none  [the longest x5 1150 us: local_states(): jnp.einsum('rmijd,rnjd->rmnid', inner_lag, pieces, precision=lax.Precisio...]
    reduce_sum x17 -> x0, other arithmetic: 244 us -> none  [the longest x1 168 us: finish_states(): weights_mode[:, :, None, :] * totals]
    psum x2 -> x0, waiting for transfers between devices: 227 us -> none  [the longest x1 126 us: local(): lax.psum((grad_in_bias, grad_short, grad_cond, grad_residue, grad_rate, g...]
    ppermute x4 -> x80, waiting for transfers between devices: 6.92 us -> 196 us  [the longest x5 35.4 us: gather_shards(): p1 = lax.ppermute(shard, 'dp', first)]
    pallas_call x0 -> x8, Pallas kernels: none -> 158 us  [the longest x1 34.4 us: feed_inner(): pl.pallas_call(lambda *refs: inner_kernel(count, outs, *refs), grid=(hidd...]
    ppermute x4 -> x80, starting transfers between devices: 9.38 us -> 65.4 us  [the longest x3 8.14 us: local(): lax.ppermute(dev_end, 'seq', [(i, i + k) for i in range(seq_count - k)])]
    unnamed x217 -> x98, local copies, waits for them, and re-layouts: 57.6 us -> 4.26 us
    dot_general x3 -> x0, other arithmetic: 52.7 us -> none  [the longest x2 51.5 us: local_states(): jnp.einsum('rmijd,rnjd->rmnid', inner_lag, pieces, precision=lax.Precisio...]
  transfers between devices with their start and end apart: 16 -> 80, of which waited for: 5 -> 37; matrix products, arithmetic and copies ran while one was open for 56% -> 8% of each run, Pallas kernels for 0% -> 16%
where the time goes in v1:
time: 464 us; the launch traced here: 463 us
  waiting for transfers between devices  196 us (42%)
  Pallas kernels  158 us (34%)
  starting transfers between devices  65.4 us (14%)
  other arithmetic  23.5 us (5%)
  local copies, waits for them, and re-layouts  18.7 us (4%)
    ppermute x5, waiting for transfers between devices, gather_shards(): p1 = lax.ppermute(shard, 'dp', first)  35.4 us
    ppermute x5, waiting for transfers between devices, line_sum(): h1 = lax.ppermute(send, 'seq', near)  34.9 us
    pallas_call x1, Pallas kernels, feed_inner(): pl.pallas_call(lambda *refs: inner_kernel(count, outs, *refs), grid=(hidd...  34.4 us
    ppermute x5, waiting for transfers between devices, scatter_sum(): got1 = lax.ppermute(send, 'dp', first)  28.3 us
    pallas_call x1, Pallas kernels, feed_down(): pl.pallas_call(lambda *refs: down_kernel(rows, span, count, outs, *refs),...  25.5 us
    pallas_call x1, Pallas kernels, mixer_taps(): pl.pallas_call(lambda *refs: taps_kernel(rows, seg * segs, seq_count, cou...  22.5 us
    ppermute x5, waiting for transfers between devices, gather_shards(): p3 = lax.ppermute(p1, 'dp', second)  21.2 us
    pallas_call x1, Pallas kernels, feed_gelu(): pl.pallas_call(lambda *refs: gelu_kernel(count, *refs), grid=(hidden // t...  19.6 us
  transfers between devices with their start and end apart: 80, of which 37 were waited for; matrix products, arithmetic and copies ran while one was open for 8% of the time, Pallas kernels for 16%

profile of v1, /device:TPU:0, one launch (start us, length us, event | category | flops | bytes accessed | tf_op | source)
XLA Modules:
  0.0 463.0 jit_solution(16699973315787954505)
XLA Ops:
  6.5 3.5 collective-permute-start.7
  12.6 4.5 collective-permute-done.8
  19.6 7.5 %collective-permute-done.21.refs_8_.refs_6_ = bf16[96,768]{1,0:T(8,128)(2,1)S(1)} collective-permute-done((bf16[96,768]{1,0:T(8,128)(2,1)S(1)}, bf16[96,768]{1,0:T(8,128)(2,1)S(1)}, u32[]{:S(2)}, u32[]{:S(2)}) %collective-permute-start.21) | collective-permute-done | bytes 147488 | tf_op jit(solution)/shard_map/ppermute | solution.py:899
  32.2 10.5 %collective-permute-done.26.refs_5_.refs_11_ = bf16[96,3072]{1,0:T(8,128)(2,1)S(1)} collective-permute-done((bf16[96,3072]{1,0:T(8,128)(2,1)}, bf16[96,3072]{1,0:T(8,128)(2,1)S(1)}, u32[]{:S(2)}, u32[]{:S(2)}) %collective-permute-start.26) | collective-permute-done | bytes 589856 | tf_op jit(solution)/shard_map/ppermute | solution.py:897
  42.7 12.6 %collective-permute-done.33.refs_13_.refs_19_ = bf16[96,3072]{1,0:T(8,128)(2,1)S(1)} collective-permute-done((bf16[96,3072]{1,0:T(8,128)(2,1)}, bf16[96,3072]{1,0:T(8,128)(2,1)S(1)}, u32[]{:S(2)}, u32[]{:S(2)}) %collective-permute-start.33) | collective-permute-done | bytes 589856 | tf_op jit(solution)/shard_map/ppermute | solution.py:897
  59.8 12.2 %collective-permute-done.refs_4_.refs_3_ = bf16[384,768]{1,0:T(8,128)(2,1)} collective-permute-done((bf16[384,768]{1,0:T(8,128)(2,1)}, bf16[384,768]{1,0:T(8,128)(2,1)}, u32[]{:S(2)}, u32[]{:S(2)}) %collective-permute-start) | collective-permute-done | bytes 589856 | tf_op jit(solution)/shard_map/ppermute | solution.py:897
  74.6 7.3 %collective-permute-done.28.refs_7_.refs_13_ = bf16[96,3072]{1,0:T(8,128)(2,1)} collective-permute-done((bf16[96,3072]{1,0:T(8,128)(2,1)S(1)}, bf16[96,3072]{1,0:T(8,128)(2,1)}, u32[]{:S(2)}, u32[]{:S(2)}) %collective-permute-start.28) | collective-permute-done | bytes 589856 | tf_op jit(solution)/shard_map/ppermute | solution.py:899
  81.9 6.3 %collective-permute-done.35.refs_15_.refs_21_ = bf16[96,3072]{1,0:T(8,128)(2,1)} collective-permute-done((bf16[96,3072]{1,0:T(8,128)(2,1)S(1)}, bf16[96,3072]{1,0:T(8,128)(2,1)}, u32[]{:S(2)}, u32[]{:S(2)}) %collective-permute-start.35) | collective-permute-done | bytes 589856 | tf_op jit(solution)/shard_map/ppermute | solution.py:899
  94.9 16.0 %mixer_enter.1 = (bf16[512,768]{1,0:T(8,128)(2,1)}, bf16[768,512]{1,0:T(8,128)(2,1)}, bf16[512,768]{1,0:T(8,128)(2,1)}, f32[2,36,8,2304]{3,2,1,0:T(8,128)}, f32[...) custom-call(s32[5]{0:T(128)} %pad_add_fusion.refs_0_, ...), custom_call_target="tpu_custom_call" | custom-call | flops 1811939328 | bytes 20000000 | tf_op jit(solution)/shard_map/mixer_enter/pallas_call | solution.py:188
  110.9 3.9 collective-permute-start.16
  125.5 14.5 %mixer_settle.1 = (f32[2,32,8,768]{3,2,1,0:T(8,128)}, bf16[768,512]{1,0:T(8,128)(2,1)}, f32[2,4,8,768]{3,2,1,0:T(8,128)}, f32[512,768]{1,0:T(8,128)}, f32[512,128]{1,0:T(8,128)}) custom-call(s32[5]{0:T(128)} %pad_add_fusion.refs_0_, s32[8]{0:T(128)} %stack.46.refs_1_.refs_0_, f32[2,4,768]{2,1,0:T(4,128)} %copy-done.22, f32[2,4,768]{2,1,0:T(4,128)} %copy-done.23, ...), custom_call_target="tpu_custom_call" | custom-call | flops 603979776 | bytes 12000000 | tf_op jit(solution)/shard_map/mixer_settle/pallas_call | solution.py:287
  140.0 19.6 %feed_gelu.1 = (bf16[768,512]{1,0:T(8,128)(2,1)}, bf16[512,3072]{1,0:T(8,128)(2,1)}, bf16[3072,512]{1,0:T(8,128)(2,1)}, bf16[512,3072]{1,0:T(8,128)(2,1)}, bf16[512,3072]{1,0:T(8,128)(2,1)}) custom-call(s32[8]{0:T(128)} %stack.46.refs_1_.refs_0_, f32[512,768]{1,0:T(8,128)} %get-tuple-element.71.refs_1_.refs_13_.refs_12_, ...), custom_call_target="tpu_custom_call" | custom-call | flops 4831838208 | bytes 24000000 | tf_op jit(solution)/shard_map/feed_gelu/pallas_call | solution.py:356
  161.0 25.5 %feed_down.1 = (bf16[2,256,768]{2,1,0:T(8,128)(2,1)}, f32[512,768]{1,0:T(8,128)}, bf16[512,768]{1,0:T(8,128)(2,1)}, f32[8,768]{1,0:T(8,128)}, bf16[4,384,768]{2,...) custom-call(s32[5]{0:T(128)} %pad_add_fusion.refs_0_, s32[8]{0:T(128)} %stack.46.refs_1_.refs_0_, s32[8]{0:T(128)} %stack.47.refs_2_.refs_1_, ...), custom_call_target="tpu_custom_call" | custom-call | flops 4831838208 | bytes 24000000 | tf_op jit(solution)/shard_map/feed_down/pallas_call | solution.py:460
  186.6 34.4 %feed_inner.1 = (f32[512,768]{1,0:T(8,128)}, bf16[4,96,3072]{2,1,0:T(8,128)(2,1)}, bf16[4,96,3072]{2,1,0:T(8,128)(2,1)}, bf16[4,96,3072]{2,1,0:T(8,128)(2,1)}, bf16[4,96,3072]{2,1,0:T(8,128)(2,1)}) custom-call(s32[8]{0:T(128)} %stack.46.refs_1_.refs_0_, s32[8]{0:T(128)} %stack.47.refs_2_.refs_1_, bf16[384,768]{1,0:T(8,128)(2,1)} %refs_2_.3, ...), custom_call_target="tpu_custom_call" | custom-call | flops 12079595520 | bytes 32000000 | tf_op jit(solution)/shard_map/feed_inner/pallas_call | solution.py:543
  221.0 12.2 %mixer_back.1 = (f32[512,768]{1,0:T(8,128)}, f32[2,32,8,768]{3,2,1,0:T(8,128)}, f32[2,4,8,768]{3,2,1,0:T(8,128)}, f32[2,4,768]{2,1,0:T(4,128)}, f32[8,768]{1,0:T...) custom-call(s32[5]{0:T(128)} %pad_add_fusion.refs_0_, s32[8]{0:T(128)} %stack.46.refs_1_.refs_0_, ...), custom_call_target="tpu_custom_call" | custom-call | flops 1207959552 | bytes 12000000 | tf_op jit(solution)/shard_map/mixer_back/pallas_call | solution.py:634
  241.3 3.4 collective-permute-done.42.refs_3_
  245.3 13.3 %mixer_source.1 = (f32[2,36,8,2304]{3,2,1,0:T(8,128)}, f32[8,2304]{1,0:T(8,128)}, f32[4,768]{1,0:T(4,128)}, f32[4,768]{1,0:T(4,128)}) custom-call(s32[5]{0:T(128)} %pad_add_fusion.refs_0_, f32[2,4,768]{2,1,0:T(4,128)} %copy-done.25, f32[2,4,768]{2,1,0:T(4,128)} %copy-done.26, f32[2,4,768]{2,1,0:T(4,128)} %copy-done.27, ...), custom_call_target="tpu_custom_call" | custom-call | flops 1000000 | bytes 16000000 | tf_op jit(solution)/shard_map/mixer_source/pallas_call | solution.py:737
  262.3 4.2 collective-permute-done.44
  267.2 22.5 %mixer_taps.1 = (bf16[2,256,768]{2,1,0:T(8,128)(2,1)}, f32[3,2304]{1,0:T(4,128)}, f32[3,768]{1,0:T(4,128)}, f32[1,2304]{1,0:T(1,128)}, bf16[4,96,2304]{2,1,0:T(8,128)(2,1)}, /*index=5*/bf16[4,96,2304]{2,1,0:T(8,128)(2,1)}) custom-call(s32[5]{0:T(128)} %pad_add_fusion.refs_0_, s32[8]{0:T(128)} %stack.46.refs_1_.refs_0_, s32[8]{0:T(128)} %stack.47.refs_2_.refs_1_, ...), custom_call_target="tpu_custom_call" | custom-call | flops 3623878656 | bytes 20000000 | tf_op jit(solution)/shard_map/mixer_taps/pallas_call | solution.py:860
  299.4 4.0 collective-permute-done.53
  303.6 4.5 collective-permute-done.54
  309.6 4.6 %collective-permute-done.55 = f32[29,768]{1,0:T(8,128)S(1)} collective-permute-done((f32[29,768]{1,0:T(8,128)S(1)}, f32[29,768]{1,0:T(8,128)S(1)}, u32[]{:S(2)}, u32[]{:S(2)}) %collective-permute-start.55) | collective-permute-done | bytes 89120 | tf_op jit(solution)/shard_map/ppermute | solution.py:950
  347.5 9.3 %collective-permute-done.47 = bf16[96,2304]{1,0:T(8,128)(2,1)S(1)} collective-permute-done((bf16[96,2304]{1,0:T(8,128)(2,1)S(1)}, bf16[96,2304]{1,0:T(8,128)(2,1)S(1)}, u32[]{:S(2)}, u32[]{:S(2)}) %collective-permute-start.47) | collective-permute-done | bytes 442400 | tf_op jit(solution)/shard_map/ppermute | solution.py:928
  358.8 4.4 collective-permute-done.48
  363.3 4.0 collective-permute-start.49
  370.6 9.6 %collective-permute-done.69 = bf16[2,96,3072]{2,1,0:T(8,128)(2,1)S(1)} collective-permute-done((bf16[2,96,3072]{2,1,0:T(8,128)(2,1)S(1)}, bf16[2,96,3072]{2,1,0:T(8,128)(2,1)S(1)}, u32[]{:S(2)}, u32[]{:S(2)}) %collective-permute-start.69) | collective-permute-done | bytes 1179680 | tf_op jit(solution)/shard_map/ppermute | solution.py:926
  383.7 17.3 %collective-permute-done.63 = bf16[2,96,3072]{2,1,0:T(8,128)(2,1)S(1)} collective-permute-done((bf16[2,96,3072]{2,1,0:T(8,128)(2,1)S(1)}, bf16[2,96,3072]{2,1,0:T(8,128)(2,1)S(1)}, u32[]{:S(2)}, u32[]{:S(2)}) %collective-permute-start.63) | collective-permute-done | bytes 1179680 | tf_op jit(solution)/shard_map/ppermute | solution.py:926
  403.4 9.8 %collective-permute-done.50 = bf16[48,2304]{1,0:T(8,128)(2,1)S(1)} collective-permute-done((bf16[48,2304]{1,0:T(8,128)(2,1)S(1)}, bf16[48,2304]{1,0:T(8,128)(2,1)S(1)}, u32[]{:S(2)}, u32[]{:S(2)}) %collective-permute-start.50) | collective-permute-done | bytes 221216 | tf_op jit(solution)/shard_map/ppermute | solution.py:942
  417.0 10.2 %collective-permute-done.77 = bf16[192,768]{1,0:T(8,128)(2,1)S(1)} collective-permute-done((bf16[192,768]{1,0:T(8,128)(2,1)S(1)}, bf16[192,768]{1,0:T(8,128)(2,1)S(1)}, u32[]{:S(2)}, u32[]{:S(2)}) %collective-permute-start.77) | collective-permute-done | bytes 294944 | tf_op jit(solution)/shard_map/ppermute | solution.py:938
  427.3 10.0 %collective-permute-done.71 = bf16[48,3072]{1,0:T(8,128)(2,1)S(1)} collective-permute-done((bf16[48,3072]{1,0:T(8,128)(2,1)S(1)}, bf16[48,3072]{1,0:T(8,128)(2,1)S(1)}, u32[]{:S(2)}, u32[]{:S(2)}) %collective-permute-start.71) | collective-permute-done | bytes 294944 | tf_op jit(solution)/shard_map/ppermute | solution.py:938
  437.5 7.8 %collective-permute-done.65 = bf16[48,3072]{1,0:T(8,128)(2,1)S(1)} collective-permute-done((bf16[48,3072]{1,0:T(8,128)(2,1)S(1)}, bf16[48,3072]{1,0:T(8,128)(2,1)S(1)}, u32[]{:S(2)}, u32[]{:S(2)}) %collective-permute-start.65) | collective-permute-done | bytes 294944 | tf_op jit(solution)/shard_map/ppermute | solution.py:938
  448.3 6.5 %collective-permute-done.66 = bf16[48,3072]{1,0:T(8,128)(2,1)S(1)} collective-permute-done((bf16[48,3072]{1,0:T(8,128)(2,1)S(1)}, bf16[48,3072]{1,0:T(8,128)(2,1)S(1)}, u32[]{:S(2)}, u32[]{:S(2)}) %collective-permute-start.66) | collective-permute-done | bytes 294944 | tf_op jit(solution)/shard_map/ppermute | solution.py:940
  (315 shorter events, 125.1 us)
Async XLA Ops:
  0.7 16.9 %collective-permute-start.19 = (bf16[96,768]{1,0:T(8,128)(2,1)}, bf16[96,768]{1,0:T(8,128)(2,1)S(1)}, u32[]{:S(2)}, u32[]{:S(2)}) collective-permute-start(bf16[96,768]{1,0:T(8,128)(2,1)} %refs_3_.5), channel_id=1, source_target_pairs={{0,8},{4,20},{8,0},{12,28},{16,24},{20,4},{24,16},{28,12},{1,9},{5... | collective-permute-start | bytes 442376 | tf_op jit(solution)/shard_map/ppermute | solution.py:897
  5.2 24.9 %collective-permute-start.9 = (bf16[96,2304]{1,0:T(8,128)(2,1)}, bf16[96,2304]{1,0:T(8,128)(2,1)S(1)}, u32[]{:S(2)}, u32[]{:S(2)}) collective-permute-start(bf16[96,2304]{1,0:T(8,128)(2,1)} %refs_4_.3), channel_id=1, source_target_pairs={{0,8},{4,20},{8,0},{12,28},{16,24},{20,4},{24,16},{28,12},{1,9},{5... | collective-permute-start | bytes 1327112 | tf_op jit(solution)/shard_map/ppermute | solution.py:897
  28.8 26.6 %collective-permute-start.33 = (bf16[96,3072]{1,0:T(8,128)(2,1)}, bf16[96,3072]{1,0:T(8,128)(2,1)S(1)}, u32[]{:S(2)}, u32[]{:S(2)}) collective-permute-start(bf16[96,3072]{1,0:T(8,128)(2,1)} %refs_18_.3), channel_id=1, source_target_pairs={{0,8},{4,20},{8,0},{12,28},{16,24},{20,4},{24,16},{28,12},{1,9},{5... | collective-permute-start | bytes 1769480 | tf_op jit(solution)/shard_map/ppermute | solution.py:897
  30.1 26.8 %collective-permute-start.27 = (bf16[96,3072]{1,0:T(8,128)(2,1)}, bf16[96,3072]{1,0:T(8,128)(2,1)}, u32[]{:S(2)}, u32[]{:S(2)}) collective-permute-start(bf16[96,3072]{1,0:T(8,128)(2,1)} %refs_10_.1), channel_id=1, source_target_pairs={{0,16},{4,12},{8,24},{12,4},{16,0},{20,28},{24,8},{28,20},{1,17},{... | collective-permute-start | bytes 1769480 | tf_op jit(solution)/shard_map/ppermute | solution.py:898
  30.6 26.3 %collective-permute-start.34 = (bf16[96,3072]{1,0:T(8,128)(2,1)}, bf16[96,3072]{1,0:T(8,128)(2,1)}, u32[]{:S(2)}, u32[]{:S(2)}) collective-permute-start(bf16[96,3072]{1,0:T(8,128)(2,1)} %refs_18_.3), channel_id=1, source_target_pairs={{0,16},{4,12},{8,24},{12,4},{16,0},{20,28},{24,8},{28,20},{1,17},{... | collective-permute-start | bytes 1769480 | tf_op jit(solution)/shard_map/ppermute | solution.py:898
  32.2 26.7 %collective-permute-start.29 = (bf16[96,3072]{1,0:T(8,128)(2,1)}, bf16[96,3072]{1,0:T(8,128)(2,1)S(1)}, u32[]{:S(2)}, u32[]{:S(2)}) collective-permute-start(bf16[96,3072]{1,0:T(8,128)(2,1)} %refs_10_.1), channel_id=1, source_target_pairs={{0,4},{4,0},{8,12},{12,8},{16,20},{20,16},{24,28},{28,24},{1,5},{5... | collective-permute-start | bytes 1769480 | tf_op jit(solution)/shard_map/ppermute | solution.py:901
  42.7 17.0 %collective-permute-start.36 = (bf16[96,3072]{1,0:T(8,128)(2,1)}, bf16[96,3072]{1,0:T(8,128)(2,1)S(1)}, u32[]{:S(2)}, u32[]{:S(2)}) collective-permute-start(bf16[96,3072]{1,0:T(8,128)(2,1)} %refs_18_.3), channel_id=1, source_target_pairs={{0,4},{4,0},{8,12},{12,8},{16,20},{20,16},{24,28},{28,24},{1,5},{5... | collective-permute-start | bytes 1769480 | tf_op jit(solution)/shard_map/ppermute | solution.py:901
  56.9 17.1 %collective-permute-start.11 = (bf16[96,2304]{1,0:T(8,128)(2,1)S(1)}, bf16[96,2304]{1,0:T(8,128)(2,1)S(1)}, u32[]{:S(2)}, u32[]{:S(2)}) collective-permute-start(bf16[96,2304]{1,0:T(8,128)(2,1)S(1)} %collective-permute-done.9.refs_10_.refs_5_), channel_id=1, source_target_pairs={{0,16},{4,12},{8,24},{12,4},{16,0},{20,28},{24,8},{28,20},{1,17},{... | collective-permute-start | bytes 1327112 | tf_op jit(solution)/shard_map/ppermute | solution.py:899
  81.9 29.0 %collective-permute-start.31 = (bf16[96,3072]{1,0:T(8,128)(2,1)}, bf16[96,3072]{1,0:T(8,128)(2,1)}, u32[]{:S(2)}, u32[]{:S(2)}) collective-permute-start(bf16[96,3072]{1,0:T(8,128)(2,1)} %collective-permute-done.27.refs_6_.refs_12_), channel_id=1, source_target_pairs={{0,4},{4,0},{8,12},{12,8},{16,20},{20,16},{24,28},{28,24},{1,5},{5... | collective-permute-start | bytes 1769480 | tf_op jit(solution)/shard_map/ppermute | solution.py:901
  88.3 26.6 %collective-permute-start.38 = (bf16[96,3072]{1,0:T(8,128)(2,1)}, bf16[96,3072]{1,0:T(8,128)(2,1)}, u32[]{:S(2)}, u32[]{:S(2)}) collective-permute-start(bf16[96,3072]{1,0:T(8,128)(2,1)} %collective-permute-done.34.refs_14_.refs_20_), channel_id=1, source_target_pairs={{0,4},{4,0},{8,12},{12,8},{16,20},{20,16},{24,28},{28,24},{1,5},{5... | collective-permute-start | bytes 1769480 | tf_op jit(solution)/shard_map/ppermute | solution.py:901
  88.3 29.5 %collective-permute-start.2 = (bf16[384,768]{1,0:T(8,128)(2,1)}, bf16[384,768]{1,0:T(8,128)(2,1)}, u32[]{:S(2)}, u32[]{:S(2)}) collective-permute-start(bf16[384,768]{1,0:T(8,128)(2,1)} %collective-permute-done.refs_4_.refs_3_), channel_id=1, source_target_pairs={{0,16},{4,12},{8,24},{12,4},{16,0},{20,28},{24,8},{28,20},{1,17},{... | collective-permute-start | bytes 1769480 | tf_op jit(solution)/shard_map/ppermute | solution.py:899
  88.4 32.4 %collective-permute-start.32 = (bf16[96,3072]{1,0:T(8,128)(2,1)}, bf16[96,3072]{1,0:T(8,128)(2,1)}, u32[]{:S(2)}, u32[]{:S(2)}) collective-permute-start(bf16[96,3072]{1,0:T(8,128)(2,1)} %collective-permute-done.28.refs_7_.refs_13_), channel_id=1, source_target_pairs={{0,4},{4,0},{8,12},{12,8},{16,20},{20,16},{24,28},{28,24},{1,5},{5... | collective-permute-start | bytes 1769480 | tf_op jit(solution)/shard_map/ppermute | solution.py:901
  90.0 50.0 %collective-permute-start.39 = (bf16[96,3072]{1,0:T(8,128)(2,1)}, bf16[96,3072]{1,0:T(8,128)(2,1)}, u32[]{:S(2)}, u32[]{:S(2)}) collective-permute-start(bf16[96,3072]{1,0:T(8,128)(2,1)} %collective-permute-done.35.refs_15_.refs_21_), channel_id=1, source_target_pairs={{0,4},{4,0},{8,12},{12,8},{16,20},{20,16},{24,28},{28,24},{1,5},{5... | collective-permute-start | bytes 1769480 | tf_op jit(solution)/shard_map/ppermute | solution.py:901
  119.1 40.5 %collective-permute-start.3 = (bf16[384,768]{1,0:T(8,128)(2,1)}, bf16[384,768]{1,0:T(8,128)(2,1)S(1)}, u32[]{:S(2)}, u32[]{:S(2)}) collective-permute-start(bf16[384,768]{1,0:T(8,128)(2,1)} %refs_2_.3), channel_id=1, source_target_pairs={{0,4},{4,0},{8,12},{12,8},{16,20},{20,16},{24,28},{28,24},{1,5},{5... | collective-permute-start | bytes 1769480 | tf_op jit(solution)/shard_map/ppermute | solution.py:901
  119.5 40.1 %collective-permute-start.4 = (bf16[384,768]{1,0:T(8,128)(2,1)}, bf16[384,768]{1,0:T(8,128)(2,1)S(1)}, u32[]{:S(2)}, u32[]{:S(2)}) collective-permute-start(bf16[384,768]{1,0:T(8,128)(2,1)} %collective-permute-done.refs_4_.refs_3_), channel_id=1, source_target_pairs={{0,4},{4,0},{8,12},{12,8},{16,20},{20,16},{24,28},{28,24},{1,5},{5... | collective-permute-start | bytes 1769480 | tf_op jit(solution)/shard_map/ppermute | solution.py:901
  120.8 38.8 %collective-permute-start.5 = (bf16[384,768]{1,0:T(8,128)(2,1)}, bf16[384,768]{1,0:T(8,128)(2,1)S(1)}, u32[]{:S(2)}, u32[]{:S(2)}) collective-permute-start(bf16[384,768]{1,0:T(8,128)(2,1)} %collective-permute-done.1.refs_5_.refs_4_), channel_id=1, source_target_pairs={{0,4},{4,0},{8,12},{12,8},{16,20},{20,16},{24,28},{28,24},{1,5},{5... | collective-permute-start | bytes 1769480 | tf_op jit(solution)/shard_map/ppermute | solution.py:901
  120.8 38.8 %collective-permute-start.6 = (bf16[384,768]{1,0:T(8,128)(2,1)}, bf16[384,768]{1,0:T(8,128)(2,1)S(1)}, u32[]{:S(2)}, u32[]{:S(2)}) collective-permute-start(bf16[384,768]{1,0:T(8,128)(2,1)} %collective-permute-done.2.refs_6_.refs_5_), channel_id=1, source_target_pairs={{0,4},{4,0},{8,12},{12,8},{16,20},{20,16},{24,28},{28,24},{1,5},{5... | collective-permute-start | bytes 1769480 | tf_op jit(solution)/shard_map/ppermute | solution.py:901
  262.2 32.2 %collective-permute-start.56 = (bf16[4,96,768]{2,1,0:T(8,128)(2,1)S(1)}, bf16[4,96,768]{2,1,0:T(8,128)(2,1)S(1)}, u32[]{:S(2)}, u32[]{:S(2)}) collective-permute-start(bf16[4,96,768]{2,1,0:T(8,128)(2,1)S(1)} %copy-done.44), channel_id=1, source_target_pairs={{0,4},{4,0},{8,12},{12,8},{16,20},{20,16},{24,28},{28,24},{1,5},{5... | collective-permute-start | bytes 1769480 | tf_op jit(solution)/shard_map/ppermute | solution.py:924
  295.2 20.6 %collective-permute-start.57 = (bf16[2,96,768]{2,1,0:T(8,128)(2,1)}, bf16[2,96,768]{2,1,0:T(8,128)(2,1)}, u32[]{:S(2)}, u32[]{:S(2)}) collective-permute-start(bf16[2,96,768]{2,1,0:T(8,128)(2,1)} %add_convert_fusion.10), channel_id=1, source_target_pairs={{0,8},{4,20},{8,0},{12,28},{16,24},{20,4},{24,16},{28,12},{1,9},{5... | collective-permute-start | bytes 884744 | tf_op jit(solution)/shard_map/ppermute | solution.py:926
  303.5 23.6 %collective-permute-start.45 = (bf16[4,96,2304]{2,1,0:T(8,128)(2,1)}, bf16[4,96,2304]{2,1,0:T(8,128)(2,1)}, u32[]{:S(2)}, u32[]{:S(2)}) collective-permute-start(bf16[4,96,2304]{2,1,0:T(8,128)(2,1)} %get-tuple-element.96), channel_id=1, source_target_pairs={{0,4},{4,0},{8,12},{12,8},{16,20},{20,16},{24,28},{28,24},{1,5},{5... | collective-permute-start | bytes 5308424 | tf_op jit(solution)/shard_map/ppermute | solution.py:924
  309.0 28.4 %collective-permute-start.74 = (bf16[4,384,768]{2,1,0:T(8,128)(2,1)}, bf16[4,384,768]{2,1,0:T(8,128)(2,1)}, u32[]{:S(2)}, u32[]{:S(2)}) collective-permute-start(bf16[4,384,768]{2,1,0:T(8,128)(2,1)} %get-tuple-element.111), channel_id=1, source_target_pairs={{0,4},{4,0},{8,12},{12,8},{16,20},{20,16},{24,28},{28,24},{1,5},{5... | collective-permute-start | bytes 7077896 | tf_op jit(solution)/shard_map/ppermute | solution.py:924
  309.1 35.8 %collective-permute-start.68 = (bf16[4,96,3072]{2,1,0:T(8,128)(2,1)}, bf16[4,96,3072]{2,1,0:T(8,128)(2,1)}, u32[]{:S(2)}, u32[]{:S(2)}) collective-permute-start(bf16[4,96,3072]{2,1,0:T(8,128)(2,1)} %get-tuple-element.109), channel_id=1, source_target_pairs={{0,4},{4,0},{8,12},{12,8},{16,20},{20,16},{24,28},{28,24},{1,5},{5... | collective-permute-start | bytes 7077896 | tf_op jit(solution)/shard_map/ppermute | solution.py:924
  314.9 42.1 %collective-permute-start.62 = (bf16[4,96,3072]{2,1,0:T(8,128)(2,1)}, bf16[4,96,3072]{2,1,0:T(8,128)(2,1)S(1)}, u32[]{:S(2)}, u32[]{:S(2)}) collective-permute-start(bf16[4,96,3072]{2,1,0:T(8,128)(2,1)} %get-tuple-element.107), channel_id=1, source_target_pairs={{0,4},{4,0},{8,12},{12,8},{16,20},{20,16},{24,28},{28,24},{1,5},{5... | collective-permute-start | bytes 7077896 | tf_op jit(solution)/shard_map/ppermute | solution.py:924
  339.2 28.2 %collective-permute-start.75 = (bf16[2,384,768]{2,1,0:T(8,128)(2,1)S(1)}, bf16[2,384,768]{2,1,0:T(8,128)(2,1)S(1)}, u32[]{:S(2)}, u32[]{:S(2)}) collective-permute-start(bf16[2,384,768]{2,1,0:T(8,128)(2,1)S(1)} %add_convert_fusion), channel_id=1, source_target_pairs={{0,8},{4,20},{8,0},{12,28},{16,24},{20,4},{24,16},{28,12},{1,9},{5... | collective-permute-start | bytes 3538952 | tf_op jit(solution)/shard_map/ppermute | solution.py:926
  346.6 33.7 %collective-permute-start.69 = (bf16[2,96,3072]{2,1,0:T(8,128)(2,1)S(1)}, bf16[2,96,3072]{2,1,0:T(8,128)(2,1)S(1)}, u32[]{:S(2)}, u32[]{:S(2)}) collective-permute-start(bf16[2,96,3072]{2,1,0:T(8,128)(2,1)S(1)} %add_convert_fusion.1), channel_id=1, source_target_pairs={{0,8},{4,20},{8,0},{12,28},{16,24},{20,4},{24,16},{28,12},{1,9},{5... | collective-permute-start | bytes 3538952 | tf_op jit(solution)/shard_map/ppermute | solution.py:926
  357.3 43.7 %collective-permute-start.63 = (bf16[2,96,3072]{2,1,0:T(8,128)(2,1)S(1)}, bf16[2,96,3072]{2,1,0:T(8,128)(2,1)S(1)}, u32[]{:S(2)}, u32[]{:S(2)}) collective-permute-start(bf16[2,96,3072]{2,1,0:T(8,128)(2,1)S(1)} %add_convert_fusion.2), channel_id=1, source_target_pairs={{0,8},{4,20},{8,0},{12,28},{16,24},{20,4},{24,16},{28,12},{1,9},{5... | collective-permute-start | bytes 3538952 | tf_op jit(solution)/shard_map/ppermute | solution.py:926
  363.3 38.2 %collective-permute-start.49 = (bf16[48,2304]{1,0:T(8,128)(2,1)S(1)}, bf16[48,2304]{1,0:T(8,128)(2,1)S(1)}, u32[]{:S(2)}, u32[]{:S(2)}) collective-permute-start(bf16[48,2304]{1,0:T(8,128)(2,1)S(1)} %add_convert_fusion.12), channel_id=1, source_target_pairs={{0,2},{1,3},{2,0},{3,1},{4,6},{5,7},{6,4},{7,5},{8,10},{9,11},{10,... | collective-permute-start | bytes 663560 | tf_op jit(solution)/shard_map/ppermute | solution.py:940
  369.1 45.1 %collective-permute-start.76 = (bf16[384,768]{1,0:T(8,128)(2,1)S(1)}, bf16[384,768]{1,0:T(8,128)(2,1)S(1)}, u32[]{:S(2)}, u32[]{:S(2)}) collective-permute-start(bf16[384,768]{1,0:T(8,128)(2,1)S(1)} %fusion.10), channel_id=1, source_target_pairs={{0,16},{4,12},{8,24},{12,4},{16,0},{20,28},{24,8},{28,20},{1,17},{... | collective-permute-start | bytes 1769480 | tf_op jit(solution)/shard_map/ppermute | solution.py:928
  382.1 32.4 %collective-permute-start.70 = (bf16[96,3072]{1,0:T(8,128)(2,1)S(1)}, bf16[96,3072]{1,0:T(8,128)(2,1)S(1)}, u32[]{:S(2)}, u32[]{:S(2)}) collective-permute-start(bf16[96,3072]{1,0:T(8,128)(2,1)S(1)} %fusion.9), channel_id=1, source_target_pairs={{0,16},{4,12},{8,24},{12,4},{16,0},{20,28},{24,8},{28,20},{1,17},{... | collective-permute-start | bytes 1769480 | tf_op jit(solution)/shard_map/ppermute | solution.py:928
  414.6 22.7 %collective-permute-start.71 = (bf16[48,3072]{1,0:T(8,128)(2,1)S(1)}, bf16[48,3072]{1,0:T(8,128)(2,1)S(1)}, u32[]{:S(2)}, u32[]{:S(2)}) collective-permute-start(bf16[48,3072]{1,0:T(8,128)(2,1)S(1)} %broadcast_select_fusion.5), channel_id=1, source_target_pairs={{0,1},{1,0},{2,3},{3,2},{4,5},{5,4},{6,7},{7,6},{8,9},{9,8},{10,11... | collective-permute-start | bytes 884744 | tf_op jit(solution)/shard_map/ppermute | solution.py:938
  416.9 28.5 %collective-permute-start.65 = (bf16[48,3072]{1,0:T(8,128)(2,1)S(1)}, bf16[48,3072]{1,0:T(8,128)(2,1)S(1)}, u32[]{:S(2)}, u32[]{:S(2)}) collective-permute-start(bf16[48,3072]{1,0:T(8,128)(2,1)S(1)} %broadcast_select_fusion.8), channel_id=1, source_target_pairs={{0,1},{1,0},{2,3},{3,2},{4,5},{5,4},{6,7},{7,6},{8,9},{9,8},{10,11... | collective-permute-start | bytes 884744 | tf_op jit(solution)/shard_map/ppermute | solution.py:938
  427.2 18.3 %collective-permute-start.78 = (bf16[192,768]{1,0:T(8,128)(2,1)S(1)}, bf16[192,768]{1,0:T(8,128)(2,1)S(1)}, u32[]{:S(2)}, u32[]{:S(2)}) collective-permute-start(bf16[192,768]{1,0:T(8,128)(2,1)S(1)} %add_convert_fusion.5), channel_id=1, source_target_pairs={{0,2},{1,3},{2,0},{3,1},{4,6},{5,7},{6,4},{7,5},{8,10},{9,11},{10,... | collective-permute-start | bytes 884744 | tf_op jit(solution)/shard_map/ppermute | solution.py:940
  (97 other events, 1781.9 us)

commit v2 on v1

v2 whole, which is shorter than its diff:
```python
import jax
import jax.numpy as jnp
from jax import lax
from jax.experimental import pallas as pl
from jax.experimental.pallas import tpu as pltpu
from jax.sharding import PartitionSpec as P

norm_eps = 1e-05
f32 = jnp.float32
bf16 = jnp.bfloat16
segs = 8
lane_block = 256
vmem_cap = 58 * 1024 * 1024


def iota(shape, dim):
    return lax.broadcasted_iota(jnp.int32, shape, dim)


def factor_of(info, rows, r):
    b = info[rows + r]
    return jnp.where(b == 0, 4.0, jnp.where(b == 1, 2.0, 1.0)).astype(f32)


def order_matrix(span):
    seg = span // segs
    o, n = iota((span, span), 0), iota((span, span), 1)
    return (n == (o & (segs - 1)) * seg + lax.shift_right_logical(o, 3)).astype(f32).astype(bf16)


def fill_edges(ext, r, seg, halo, cols):
    n = cols[1]
    c = pl.ds(cols[0], n)
    sub = iota((segs, n), 0)
    for h, (dst, src, shift, edge) in enumerate(
        ((0, seg, 1, 0), (1, seg + 1, 1, 0), (seg + 2, 2, segs - 1, segs - 1), (seg + 3, 3, segs - 1, segs - 1))
    ):
        rolled = pltpu.roll(ext[r, src, :, c], shift, 0)
        ext[r, dst, :, c] = jnp.where(sub == edge, halo[pl.ds(4 * r + h, 1), c], rolled)


def fetch_parts(where, parts, full, sems, at=0, cols=None):
    depth, wide = parts[0].shape[0], full.shape[1] if cols is None else cols.size
    copies = []
    for k, part in enumerate(parts):
        src = part if part.shape[1] == wide else part.at[:, pl.ds(at, wide)]
        dst = full.at[pl.ds(pl.multiple_of(where[k] * depth, 8), depth)]
        if cols is not None:
            dst = full.at[pl.ds(pl.multiple_of(where[k] * depth, 8), depth), cols]
        copies.append(pltpu.make_async_copy(src, dst, sems.at[k]))
    return copies


def start_all(copies):
    for copy in copies:
        copy.start()


def wait_all(copies):
    for copy in copies:
        copy.wait()


def send_parts(where, full, outs, sems, cols=None, into=None):
    per, depth = outs[0].shape[0], outs[0].shape[1]
    copies = []
    for k in range(per * len(outs)):
        rows_of = pl.ds(pl.multiple_of(where[k] * depth, 8), depth)
        src, dst = full.at[rows_of], outs[k // per].at[k % per]
        if cols is not None:
            src, dst = full.at[rows_of, cols], outs[k // per].at[k % per, :, cols]
        if into is not None:
            dst = outs[k // per].at[k % per, :, into]
        copies.append(pltpu.make_async_copy(src, dst, sems.at[k]))
    return copies


def join_rims(rows, before, after, rim):
    rim[...] = jnp.zeros_like(rim)
    low, high = before[...].astype(f32), after[...].astype(f32)
    for r in range(rows):
        for k in range(2):
            rim[pl.ds(4 * r + k, 1), :] = low[2 * r + k : 2 * r + k + 1]
            rim[pl.ds(4 * r + 2 + k, 1), :] = high[2 * r + k : 2 * r + k + 1]


def enter_kernel(rows, span, seq_count, count, info, where, x, cot, before, after, bias, st, ct, rate, *refs):
    parts, refs = refs[:count], refs[count:]
    xp, xpt, cp, ext, q, keys, vals, ends, dev_end, mask, hal, xh, w, sems = refs
    copies = fetch_parts(where, parts, w, sems)
    start_all(copies)
    width = x.shape[2]
    seg = span // segs
    place = info[2 * rows]
    base = place * span
    order = order_matrix(span)
    for r in range(rows):
        moved = jnp.dot(order, x[r], preferred_element_type=f32).astype(bf16)
        xp[pl.ds(r * span, span), :] = moved
        xpt[:, pl.ds(r * span, span)] = moved.T
        cp[pl.ds(r * span, span), :] = jnp.dot(order, cot[r], preferred_element_type=f32).astype(bf16)
        n = iota((span, 128), 0)
        pos = base + (n & (segs - 1)) * seg + lax.shift_right_logical(n, 3)
        mask[pl.ds(r * span, span), :] = (pos < info[r]).astype(f32)
    join_rims(rows, before, after, xh)
    edge_rows = xh[...].astype(bf16)
    hn = iota((16, 128), 0)
    hk = hn & 3
    hpos = base + jnp.where(hk < 2, hk - 2, span + hk - 2)
    hlim = jnp.where(lax.shift_right_logical(hn, 2) == 0, info[0], info[1])
    hmask = ((hpos >= 0) & (hpos < hlim)).astype(f32)
    wait_all(copies)

    @pl.loop(0, 3 * width // lane_block)
    def _(t):
        cols = pl.ds(pl.multiple_of(t * lane_block, lane_block), lane_block)
        part = jnp.dot(xp[...], w[:, cols], preferred_element_type=f32) + bias[:, cols]
        rim = jnp.dot(edge_rows, w[:, cols], preferred_element_type=f32) + bias[:, cols]
        for s in range(lane_block // 128):
            sub = slice(s * 128, (s + 1) * 128)
            scol = pl.ds(pl.multiple_of(t * lane_block + s * 128, 128), 128)
            low = (part[:, sub] * mask[...]).astype(bf16).astype(f32)
            for r in range(rows):
                ext[r, pl.ds(2, seg), :, scol] = low[r * span : (r + 1) * span].reshape(seg, segs, 128)
            hal[:, scol] = (rim[:, sub] * hmask).astype(bf16).astype(f32)

    sub = iota((segs, lane_block), 0)
    first = (place == 0).astype(f32)
    last = (place == seq_count - 1).astype(f32)
    in_low = 1.0 - first * (sub == 0).astype(f32)
    in_high = 1.0 - last * (sub == segs - 1).astype(f32)
    for r in range(rows):
        factor = factor_of(info, rows, r)
        for t in range(3 * width // lane_block):
            fill_edges(ext, r, seg, hal, (t * lane_block, lane_block))
        for t in range(width // lane_block):
            cq = pl.ds(t * lane_block, lane_block)
            ck = pl.ds(width + t * lane_block, lane_block)
            cv = pl.ds(2 * width + t * lane_block, lane_block)
            modes = rate.shape[0]
            fade = [jnp.exp(-rate[pl.ds(m, 1), cq] * factor) for m in range(modes)]
            far = [jnp.exp(-rate[pl.ds(m, 1), cq] * (factor * seg)) for m in range(modes)]

            def tap3(cols, e):
                return (
                    st[pl.ds(0, 1), cols] * ext[r, e - 1, :, cols]
                    + st[pl.ds(1, 1), cols] * ext[r, e, :, cols]
                    + st[pl.ds(2, 1), cols] * ext[r, e + 1, :, cols]
                )

            def step(j, carry):
                kp_prev, kp_cur, states = carry
                kp_next = tap3(ck, j + 3)
                kp_next = jnp.where(j == seg - 1, kp_next * in_high, kp_next)
                key = (
                    ct[pl.ds(0, 1), cq] * kp_prev
                    + ct[pl.ds(1, 1), cq] * kp_cur
                    + ct[pl.ds(2, 1), cq] * kp_next
                )
                val = tap3(cv, j + 2)
                q[r, j, :, cq] = tap3(cq, j + 2)
                keys[r, j, :, cq] = key
                vals[r, j, :, cq] = val
                live = (base + sub * seg + j < info[r]).astype(f32)
                src = key * val * live
                return (kp_cur, kp_next, tuple(f * h + src for f, h in zip(fade, states)))

            zero = jnp.zeros((segs, lane_block), f32)
            start = (tap3(ck, 1) * in_low, tap3(ck, 2), (zero,) * modes)
            _, _, states = lax.fori_loop(0, seg, step, start, unroll=4)
            for m in range(modes):
                ends[r, m, :, cq] = states[m]
                total = jnp.zeros((1, lane_block), f32)
                for i in range(segs):
                    total = far[m] * total + states[m][i : i + 1]
                dev_end[r, pl.ds(m, 1), cq] = total


def vm(shape, dtype=f32):
    return jax.ShapeDtypeStruct(shape, dtype)


def vmem_specs(n):
    return [pl.BlockSpec(memory_space=pltpu.VMEM)] * n


def smem_spec():
    return [pl.BlockSpec(memory_space=pltpu.SMEM)]


def spent(us):
    return pl.CostEstimate(flops=int(us * 1.1e9), bytes_accessed=1_000_000, transcendentals=0)


def any_specs(n):
    return [pl.BlockSpec(memory_space=pl.ANY)] * n


def hbm_specs(n):
    return [pl.BlockSpec(memory_space=pltpu.HBM)] * n


def mixer_enter(info, where, hidden, cot, before, after, bias, st, ct, rate, parts, seq_count):
    rows, span, width = hidden.shape
    seg, modes, tokens = span // segs, rate.shape[0], rows * span
    body = (rows, seg, segs, width)
    return pl.pallas_call(
        lambda *refs: enter_kernel(rows, span, seq_count, len(parts), *refs),
        out_shape=(
            vm((tokens, width), bf16),
            vm((width, tokens), bf16),
            vm((tokens, width), bf16),
            vm((rows, seg + 4, segs, 3 * width)),
            vm(body),
            vm(body),
            vm(body),
            vm((rows, modes, segs, width)),
            vm((rows, modes, width)),
        ),
        in_specs=smem_spec() * 2 + vmem_specs(8) + hbm_specs(len(parts)),
        out_specs=tuple(vmem_specs(9)),
        scratch_shapes=[
            pltpu.VMEM((tokens, 128), f32),
            pltpu.VMEM((16, 3 * width), f32),
            pltpu.VMEM((16, width), f32),
            pltpu.VMEM((width, 3 * width), bf16),
            pltpu.SemaphoreType.DMA((len(parts),)),
        ],
        compiler_params=pltpu.CompilerParams(vmem_limit_bytes=vmem_cap),
        cost_estimate=spent(1),
        name="mixer_enter",
    )(info, where, hidden, cot, before, after, bias, st, ct, rate, *parts)


def carry_in(parts, fade_span):
    total = parts[0]
    scale = fade_span
    for p in parts[1:]:
        total = total + scale * p
        scale = scale * fade_span
    return total


def settle_kernel(rows, span, others, count, info, where, *refs):
    gath, refs = refs[:others], refs[others:]
    parts, refs = refs[:count], refs[count:]
    ends, q, keys, vals, rate, res, xp, ob, gain, shift, long_out, gated_t, carry_out, n1, s1, low, low_t, gsc, wo, sems = refs
    copies = fetch_parts(where, parts, wo, sems, parts[0].shape[1] - wo.shape[1])
    start_all(copies)
    seg = span // segs
    width = q.shape[3]
    modes = rate.shape[0]
    base = info[2 * rows] * span
    sub = iota((segs, lane_block), 0)
    for r in range(rows):
        factor = factor_of(info, rows, r)
        for t in range(width // lane_block):
            c = pl.ds(t * lane_block, lane_block)
            fade, mix, start = [], [], []
            for m in range(modes):
                d = rate[pl.ds(m, 1), c] * factor
                fade.append(jnp.exp(-d))
                mix.append(res[pl.ds(m, 1), c] * jnp.sqrt(1.0 - jnp.exp(-2.0 * d)))
                far = jnp.exp(-d * seg)
                cur = carry_in([g[r, pl.ds(m, 1), c] for g in gath], jnp.exp(-d * span))
                tile = jnp.zeros((segs, lane_block), f32)
                end = ends[r, m, :, c]
                for i in range(segs):
                    tile = jnp.where(sub == i, cur, tile)
                    cur = far * cur + end[i : i + 1]
                carry_out[r, m, :, c] = tile
                start.append(tile)

            def step(j, states):
                live = (base + sub * seg + j < info[r]).astype(f32)
                src = keys[r, j, :, c] * vals[r, j, :, c] * live
                states = tuple(f * h + src for f, h in zip(fade, states))
                out = mix[0] * states[0]
                for m in range(1, modes):
                    out = out + mix[m] * states[m]
                long_out[r, j, :, c] = out
                gsc[r, j, :, c] = q[r, j, :, c] * out * live
                return states

            lax.fori_loop(0, seg, step, tuple(start), unroll=4)
    wait_all(copies)
    for r in range(rows):
        tok = pl.ds(r * span, span)
        cut = gsc[r].reshape(span, width).astype(bf16)
        gated_t[:, tok] = cut.T
        n1[tok, :] = xp[tok, :].astype(f32) + jnp.dot(cut, wo[...], preferred_element_type=f32) + ob[...]

    @pl.loop(0, rows * span // 16, unroll=4)
    def _(k):
        tok = pl.ds(pl.multiple_of(k * 16, 16), 16)
        v = n1[tok, :]
        centre = v - jnp.mean(v, axis=-1, keepdims=True)
        inv = lax.rsqrt(jnp.mean(centre * centre, axis=-1, keepdims=True) + norm_eps)
        n = centre * inv
        n1[tok, :] = n
        s1[tok, :] = jnp.broadcast_to(inv, (16, 128))
        low[tok, :] = (n * gain[...] + shift[...]).astype(bf16)

    low_t[...] = low[...].T


def mixer_settle(info, where, gath, ends, q, keys, vals, rate, res, xp, ob, gain, shift, parts):
    rows, seg, _, width = q.shape
    span = seg * segs
    tokens, modes = rows * span, rate.shape[0]
    return pl.pallas_call(
        lambda *refs: settle_kernel(rows, span, len(gath), len(parts), *refs),
        out_shape=(
            vm(q.shape),
            vm((width, tokens), bf16),
            vm(ends.shape),
            vm((tokens, width)),
            vm((tokens, 128)),
            vm((tokens, width), bf16),
            vm((width, tokens), bf16),
        ),
        in_specs=smem_spec() * 2 + vmem_specs(len(gath)) + hbm_specs(len(parts)) + vmem_specs(10),
        out_specs=tuple(vmem_specs(7)),
        scratch_shapes=[
            pltpu.VMEM(q.shape, f32),
            pltpu.VMEM((width, width), bf16),
            pltpu.SemaphoreType.DMA((len(parts),)),
        ],
        compiler_params=pltpu.CompilerParams(vmem_limit_bytes=vmem_cap),
        cost_estimate=spent(1),
        name="mixer_settle",
    )(info, where, *gath, *parts, ends, q, keys, vals, rate, res, xp, ob, gain, shift)


def row_mean(v):
    return jnp.mean(v, axis=-1, keepdims=True)


def fold(v):
    return v[:8] + v[8:]


def contract_last(a, b):
    return lax.dot_general(a, b, (((1,), (1,)), ((), ())), preferred_element_type=f32)


hidden_tile = 512


def core_kernel(rows, span, count, outs, info, where, slots, *refs):
    w_parts, d_parts, o_parts, refs = refs[:count], refs[count : 2 * count], refs[2 * count : 3 * count], refs[3 * count :]
    low_h, low_th, gated_th, n1_h, s1_h, cp_h, q_h, gain1, shift1, bias, gain2, shift2, rate, layer = refs[:14]
    refs = refs[14:]
    down_out, first_out, second_out, refs = refs[:outs], refs[outs : 2 * outs], refs[2 * outs : 3 * outs], refs[3 * outs :]
    pre1_h, gg_h, ends, dev_end, sums_two, sums_one, w, wd, wo, act, pull, gel, low, low_t, gated_t = refs[:15]
    n1, s1, cp, q, acc, first, feed, out_low, mix, gs, us, dd, dwg, dwu, dwo = refs[15:30]
    in_sems, w_sems, d_sems, o_sems, dd_sems, dw_sems, end_sems = refs[30:]
    hidden, width = wd.shape
    tile, seg, modes = hidden_tile, span // segs, rate.shape[0]
    tiles, tokens = hidden // tile, rows * span
    base = info[2 * rows] * span

    def bring(k, src, dst):
        return pltpu.make_async_copy(src, dst, in_sems.at[k])

    w_in = [
        [
            copy
            for k, at in enumerate((t * tile, hidden + t * tile))
            for copy in fetch_parts(where, w_parts, w, w_sems.at[k, t], at, pl.ds(at, tile))
        ]
        for t in range(tiles)
    ]
    d_in = fetch_parts(where, d_parts, wd, d_sems)
    o_in = fetch_parts(where, o_parts, wo, o_sems, o_parts[0].shape[1] - width)
    low_in = bring(0, low_h, low)
    norm_in = [bring(1, n1_h, n1), bring(2, cp_h, cp)]
    late_in = [bring(3, low_th, low_t), bring(4, s1_h, s1), bring(5, q_h, q), bring(6, gated_th, gated_t)]
    start_all([low_in] + w_in[0] + w_in[1])
    low_in.wait()
    scale = 0.7978845608028654
    for t in range(tiles):
        if t + 2 < tiles:
            start_all(w_in[t + 2])
        if t == 1:
            start_all(d_in)
        if t == 3:
            start_all(norm_in)
        wait_all(w_in[t])
        cols, up_cols = pl.ds(t * tile, tile), pl.ds(hidden + t * tile, tile)
        gs[...] = jnp.dot(low[...], w[:, cols], preferred_element_type=f32)
        us[...] = jnp.dot(low[...], w[:, up_cols], preferred_element_type=f32)

        @pl.loop(0, tokens // 16, unroll=2)
        def _(k):
            tok = pl.ds(pl.multiple_of(k * 16, 16), 16)
            g, u = gs[tok, :], us[tok, :]
            sq = g * g
            th = jnp.tanh(g * (scale + (scale * 0.044715) * sq))
            side = 0.5 + 0.5 * th
            gelu = g * side
            slope = side + (0.5 * g) * (1.0 - th * th) * (scale + (3.0 * scale * 0.044715) * sq)
            act[tok, cols] = (gelu * u).astype(bf16)
            pull[tok, cols] = (u * slope).astype(bf16)
            gel[tok, cols] = gelu.astype(bf16)

    wait_all(d_in)
    for t in range(width // lane_block):
        c = pl.ds(t * lane_block, lane_block)
        acc[:, c] = jnp.dot(act[...], wd[:, c], preferred_element_type=f32)
    zero = jnp.zeros((8, width), f32)
    wait_all(norm_in)
    start_all(late_in + o_in)

    def outer_norm(k, loop):
        tok = pl.ds(pl.multiple_of(k * 16, 16), 16)
        n = iota((16, width), 0) + k * 16
        n = n & (span - 1)
        pos = base + (n & (segs - 1)) * seg + lax.shift_right_logical(n, 3)
        limit = jnp.where(k * 16 >= span, info[1], info[0])
        keep = (pos < limit).astype(f32)
        v = n1[tok, :] * gain1[...] + shift1[...] + acc[tok, :] + bias[...]
        centre = v - row_mean(v)
        inv = lax.rsqrt(row_mean(centre * centre) + norm_eps)
        n2 = centre * inv
        out_low[tok, :] = ((n2 * gain2[...] + shift2[...]) * keep).astype(bf16)
        top = cp[tok, :].astype(f32) * keep
        e = top * gain2[...]
        grad = inv * (e - row_mean(e) - n2 * row_mean(e * n2))
        first[tok, :] = grad
        cut = grad.astype(bf16)
        feed[tok, :] = cut
        return (
            loop[0] + fold(cut.astype(f32)),
            loop[1] + fold(top * n2),
            loop[2] + fold(top),
        )

    totals = lax.fori_loop(0, tokens // 16, outer_norm, (zero, zero, zero), unroll=4)
    for k in range(3):
        sums_two[pl.ds(k, 1), :] = jnp.sum(totals[k], axis=0, keepdims=True)

    blocks = 8
    span_d = hidden // blocks
    d_sends = []
    for k in range(blocks):
        if k >= 2:
            d_sends[k - 2].wait()
        which = k if outs == 1 else slots[k]
        c = pl.ds(pl.multiple_of(which * span_d, 128), span_d)
        dd[k % 2] = jnp.dot(act[:, c].T, feed[...], preferred_element_type=f32).astype(bf16)
        per = down_out[0].shape[0]
        dst = down_out[0].at[0, pl.ds(k * span_d, span_d)] if outs == 1 else down_out[k // per].at[k % per]
        d_sends.append(pltpu.make_async_copy(dd.at[k % 2], dst, dd_sems.at[k]))
        d_sends[k].start()
    o, n = iota((span, span), 0), iota((span, span), 1)
    back = (o == (n & (segs - 1)) * seg + lax.shift_right_logical(n, 3)).astype(f32).astype(bf16)
    for r in range(rows):
        layer[r] = jnp.dot(back, out_low[pl.ds(r * span, span), :], preferred_element_type=f32).astype(bf16)
    wait_all(late_in)
    sends = []
    half_tiles = tiles // 2
    for t in range(tiles):
        cols, up_cols = pl.ds(t * tile, tile), pl.ds(hidden + t * tile, tile)
        grad = contract_last(feed[...], wd[cols, :])
        g = (grad * pull[:, cols].astype(f32)).astype(bf16)
        u = (grad * gel[:, cols].astype(f32)).astype(bf16)
        if t >= 2:
            wait_all(sends[t - 2])
        dwg[t % 2] = jnp.dot(low_t[...], g, preferred_element_type=f32).astype(bf16)
        dwu[t % 2] = jnp.dot(low_t[...], u, preferred_element_type=f32).astype(bf16)
        into, at, own = (first_out, 0, t) if t < half_tiles else (second_out, width, t - half_tiles)
        g_at, u_at = at + own * tile, at + (half_tiles + own) * tile
        sends.append(
            send_parts(slots, dwg.at[t % 2], into, dw_sems.at[0, t], None, pl.ds(g_at, tile))
            + send_parts(slots, dwu.at[t % 2], into, dw_sems.at[1, t], None, pl.ds(u_at, tile))
        )
        start_all(sends[t])
        first[...] += contract_last(g, w[:, cols]) + contract_last(u, w[:, up_cols])

    def put(k, src, dst):
        return pltpu.make_async_copy(src, dst, end_sems.at[k])

    def inner_norm(k, loop):
        tok = pl.ds(pl.multiple_of(k * 16, 16), 16)
        top, n = first[tok, :], n1[tok, :]
        e = top * gain1[...]
        grad = s1[tok, 0:1] * (e - row_mean(e) - n * row_mean(e * n))
        acc[tok, :] = grad
        cut = grad.astype(bf16)
        mix[tok, :] = cut
        return (
            loop[0] + fold(cut.astype(f32)),
            loop[1] + fold(top * n),
            loop[2] + fold(top),
        )

    totals = lax.fori_loop(0, tokens // 16, inner_norm, (zero, zero, zero), unroll=4)
    finals = [put(0, acc, pre1_h)]
    finals[0].start()
    for k in range(3):
        sums_one[pl.ds(k, 1), :] = jnp.sum(totals[k], axis=0, keepdims=True)
    dwo[...] = jnp.dot(gated_t[...], mix[...], preferred_element_type=f32).astype(bf16)
    o_sends = send_parts(slots, dwo, second_out, dw_sems.at[2, 0], None, pl.ds(0, width))
    start_all(o_sends)
    wait_all(o_in)
    for t in range(width // lane_block):
        c = pl.ds(t * lane_block, lane_block)
        first[:, c] = contract_last(mix[...], wo[c, :])
    sub = iota((segs, lane_block), 0)
    for r in range(rows):
        factor = factor_of(info, rows, r)
        for t in range(width // lane_block):
            c = pl.ds(t * lane_block, lane_block)
            fade = [jnp.exp(-rate[pl.ds(m, 1), c] * factor) for m in range(modes)]
            far = [jnp.exp(-rate[pl.ds(m, 1), c] * (factor * seg)) for m in range(modes)]

            def step(k, states):
                j = seg - 1 - k
                live = (base + sub * seg + j < info[r]).astype(f32)
                tok = pl.ds(pl.multiple_of(r * span + j * segs, segs), segs)
                grad = first[tok, c] * live
                first[tok, c] = grad
                g = grad * q[r, j, :, c]
                return tuple(f * h + g for f, h in zip(fade, states))

            blank = jnp.zeros((segs, lane_block), f32)
            states = lax.fori_loop(0, seg, step, (blank,) * modes, unroll=4)
            for m in range(modes):
                ends[r, m, :, c] = states[m]
                total = jnp.zeros((1, lane_block), f32)
                for i in reversed(range(segs)):
                    total = far[m] * total + states[m][i : i + 1]
                dev_end[r, pl.ds(m, 1), c] = total
    finals.append(put(1, first, gg_h))
    finals[1].start()
    for copies in [d_sends[-2:]] + sends[-2:] + [o_sends, finals]:
        wait_all(copies)


def feed_core(
    info, where, slots, w_parts, d_parts, o_parts, low, low_t, gated_t, n1, s1, cp, q, gain1, shift1, bias,
    gain2, shift2, rate, down_shapes, first_shapes, second_shapes,
):
    tokens, width = n1.shape
    rows, seg = q.shape[:2]
    modes, count, outs = rate.shape[0], len(w_parts), len(first_shapes)
    hidden, tile, pieces = w_parts[0].shape[1] // 2, hidden_tile, first_shapes[0][0] * outs
    shapes = tuple(down_shapes) + tuple(first_shapes) + tuple(second_shapes)
    return pl.pallas_call(
        lambda *refs: core_kernel(rows, seg * segs, count, outs, *refs),
        out_shape=(vm((rows, seg * segs, width), bf16),)
        + tuple(vm(s, bf16) for s in shapes)
        + (
            vm((tokens, width)),
            vm((tokens, width)),
            vm((rows, modes, segs, width)),
            vm((rows, modes, width)),
            vm((8, width)),
            vm((8, width)),
        ),
        in_specs=smem_spec() * 3 + hbm_specs(3 * count + 7) + vmem_specs(6),
        out_specs=tuple(vmem_specs(1) + hbm_specs(3 * outs + 2) + vmem_specs(4)),
        scratch_shapes=[
            pltpu.VMEM((width, 2 * hidden), bf16),
            pltpu.VMEM((hidden, width), bf16),
            pltpu.VMEM((width, width), bf16),
            pltpu.VMEM((tokens, hidden), bf16),
            pltpu.VMEM((tokens, hidden), bf16),
            pltpu.VMEM((tokens, hidden), bf16),
            pltpu.VMEM((tokens, width), bf16),
            pltpu.VMEM((width, tokens), bf16),
            pltpu.VMEM((width, tokens), bf16),
            pltpu.VMEM((tokens, width), f32),
            pltpu.VMEM((tokens, 128), f32),
            pltpu.VMEM((tokens, width), bf16),
            pltpu.VMEM(q.shape, f32),
            pltpu.VMEM((tokens, width), f32),
            pltpu.VMEM((tokens, width), f32),
            pltpu.VMEM((tokens, width), bf16),
            pltpu.VMEM((tokens, width), bf16),
            pltpu.VMEM((tokens, width), bf16),
            pltpu.VMEM((tokens, tile), f32),
            pltpu.VMEM((tokens, tile), f32),
            pltpu.VMEM((2, hidden // 8, width), bf16),
            pltpu.VMEM((2, width, tile), bf16),
            pltpu.VMEM((2, width, tile), bf16),
            pltpu.VMEM((width, width), bf16),
            pltpu.SemaphoreType.DMA((7,)),
            pltpu.SemaphoreType.DMA((2, hidden // tile, count)),
            pltpu.SemaphoreType.DMA((count,)),
            pltpu.SemaphoreType.DMA((count,)),
            pltpu.SemaphoreType.DMA((8,)),
            pltpu.SemaphoreType.DMA((3, hidden // tile, pieces)),
            pltpu.SemaphoreType.DMA((2,)),
        ],
        compiler_params=pltpu.CompilerParams(vmem_limit_bytes=vmem_cap),
        cost_estimate=spent(1),
        name="feed_core",
    )(
        info, where, slots, *w_parts, *d_parts, *o_parts, low, low_t, gated_t, n1, s1, cp, q, gain1, shift1,
        bias, gain2, shift2, rate,
    )


def split_rims(rows, seg, at, rim, low, high):
    for r in range(rows):
        for k in range(2):
            rim[pl.ds(2 * r + k, 1), :] = at(r, k, pl.ds(0, 1))
            rim[pl.ds(2 * (rows + r) + k, 1), :] = at(r, seg - 2 + k, pl.ds(segs - 1, 1))
    low[...] = rim[: 2 * rows].astype(bf16)
    high[...] = rim[2 * rows : 4 * rows].astype(bf16)


def source_kernel(rows, span, others, info, *refs):
    gath = refs[:others]
    ends, carry, rate, res, refs = *refs[others : others + 4], refs[others + 4 :]
    streams, refs = refs[:5], refs[5:]
    gm_h, rim_low, rim_high, gres, grate, gg, q, long_out, keys, vals, gm, hist, rim, in_sems, out_sems = refs
    seg = span // segs
    width, modes = q.shape[3], rate.shape[0]
    blocks = width // lane_block
    ins = [
        [
            pltpu.make_async_copy(
                src.at[:, :, :, pl.ds(t * lane_block, lane_block)],
                dst.at[:, :, :, pl.ds(t * lane_block, lane_block)],
                in_sems.at[t, k],
            )
            for k, (src, dst) in enumerate(zip(streams, (gg, q, long_out, keys, vals)))
        ]
        for t in range(blocks)
    ]
    sends = [
        [
            pltpu.make_async_copy(
                gm.at[:, :, :, pl.ds(b * width + t * lane_block, lane_block)],
                gm_h.at[:, pl.ds(2, seg), :, pl.ds(b * width + t * lane_block, lane_block)],
                out_sems.at[t, b],
            )
            for b in range(3)
        ]
        for t in range(blocks)
    ]
    for t in range(blocks):
        start_all(ins[t])
    base = info[2 * rows] * span
    sub = iota((segs, lane_block), 0)
    for t in range(blocks):
        wait_all(ins[t])
        c = pl.ds(t * lane_block, lane_block)
        sum_res = [jnp.zeros((1, lane_block), f32) for _ in range(modes)]
        sum_rate = [jnp.zeros((1, lane_block), f32) for _ in range(modes)]
        for r in range(rows):
            factor = factor_of(info, rows, r)
            fade, mix, start, root, ebb = [], [], [], [], []
            for m in range(modes):
                d = rate[pl.ds(m, 1), c] * factor
                fade.append(jnp.exp(-d))
                ebb.append(jnp.exp(-2.0 * d))
                root.append(jnp.sqrt(1.0 - ebb[m]))
                mix.append(res[pl.ds(m, 1), c] * root[m])
                far = jnp.exp(-d * seg)
                cur = carry_in([g[r, pl.ds(m, 1), c] for g in gath], jnp.exp(-d * span))
                tile = jnp.zeros((segs, lane_block), f32)
                end = ends[r, m, :, c]
                for i in reversed(range(segs)):
                    tile = jnp.where(sub == i, cur, tile)
                    cur = far * cur + end[i : i + 1]
                start.append(tile)

            def ahead(j, loop):
                states, sums = loop
                live = (base + sub * seg + j < info[r]).astype(f32)
                src = keys[r, j, :, c] * vals[r, j, :, c] * live
                g = gg[r, j, :, c] * q[r, j, :, c]
                past = tuple(f * h for f, h in zip(fade, states))
                for m in range(modes):
                    hist[m, j] = past[m]
                states = tuple(p + src for p in past)
                return (states, tuple(s + g * h for s, h in zip(sums, states)))

            zero = jnp.zeros((segs, lane_block), f32)
            init = tuple(carry[r, m, :, c] for m in range(modes))
            _, with_state = lax.fori_loop(0, seg, ahead, (init, (zero,) * modes), unroll=4)

            def behind(k, loop):
                states, sums = loop
                j = seg - 1 - k
                live = (base + sub * seg + j < info[r]).astype(f32)
                grad = gg[r, j, :, c]
                g = grad * q[r, j, :, c]
                states = tuple(f * h + g for f, h in zip(fade, states))
                gs = mix[0] * states[0]
                for m in range(1, modes):
                    gs = gs + mix[m] * states[m]
                gs = gs * live
                for b, part in enumerate(
                    (grad * long_out[r, j, :, c], gs * vals[r, j, :, c], gs * keys[r, j, :, c])
                ):
                    gm[r, j, :, pl.ds(b * width + t * lane_block, lane_block)] = part.astype(bf16).astype(f32)
                return (states, tuple(s + h * hist[m, j] for m, (s, h) in enumerate(zip(sums, states))))

            _, with_lag = lax.fori_loop(0, seg, behind, (tuple(start), (zero,) * modes), unroll=4)
            for m in range(modes):
                u = jnp.sum(with_state[m], axis=0, keepdims=True)
                v = jnp.sum(with_lag[m], axis=0, keepdims=True)
                sum_res[m] = sum_res[m] + root[m] * u
                sum_rate[m] = sum_rate[m] + factor * res[pl.ds(m, 1), c] * (ebb[m] / root[m] * u - root[m] * v)
        for m in range(modes):
            gres[pl.ds(m, 1), c] = sum_res[m]
            grate[pl.ds(m, 1), c] = sum_rate[m]
        start_all(sends[t])
    split_rims(rows, seg, lambda r, j, i: gm[r, j, i, :], rim, rim_low, rim_high)
    for t in range(blocks):
        wait_all(sends[t])


def mixer_source(info, gath, ends, carry, gg, q, long_out, keys, vals, rate, res):
    rows, seg, _, width = q.shape
    modes = rate.shape[0]
    return pl.pallas_call(
        lambda *refs: source_kernel(rows, seg * segs, len(gath), *refs),
        out_shape=(
            vm((rows, seg + 4, segs, 3 * width)),
            vm((2 * rows, 3 * width), bf16),
            vm((2 * rows, 3 * width), bf16),
            vm((modes, width)),
            vm((modes, width)),
        ),
        in_specs=smem_spec() + vmem_specs(4 + len(gath)) + hbm_specs(5),
        out_specs=tuple(hbm_specs(1) + vmem_specs(4)),
        scratch_shapes=[pltpu.VMEM(q.shape, f32)] * 5
        + [
            pltpu.VMEM((rows, seg, segs, 3 * width), f32),
            pltpu.VMEM((modes, seg, segs, lane_block), f32),
            pltpu.VMEM((4 * rows, 3 * width), f32),
            pltpu.SemaphoreType.DMA((width // lane_block, 5)),
            pltpu.SemaphoreType.DMA((width // lane_block, 3)),
        ],
        compiler_params=pltpu.CompilerParams(vmem_limit_bytes=vmem_cap),
        cost_estimate=spent(1),
        name="mixer_source",
    )(info, *gath, ends, carry, rate, res, gg, q, long_out, keys, vals)


def taps_blocks(rows, span, seq_count, info, gm, halo, ext, st, ct, gp, put, gsc, ready, done):
    seg = span // segs
    width = ct.shape[1]
    place = info[2 * rows]
    base = place * span
    sub = iota((segs, lane_block), 0)
    in_low = 1.0 - (place == 0).astype(f32) * (sub == 0).astype(f32)
    in_high = 1.0 - (place == seq_count - 1).astype(f32) * (sub == segs - 1).astype(f32)
    zero = jnp.zeros((segs, lane_block), f32)
    for block in range(3):
        for t in range(width // lane_block):
            ready(block * (width // lane_block) + t)
            for r in range(rows):
                fill_edges(gm, r, seg, halo, (block * width + t * lane_block, lane_block))
            c = pl.ds(block * width + t * lane_block, lane_block)
            lanes = pl.ds(t * lane_block, lane_block)
            sums = tuple(zero for _ in range(4))
            csums = tuple(zero for _ in range(3))
            for r in range(rows):

                def tap3(e):
                    return (
                        st[pl.ds(0, 1), c] * ext[r, e - 1, :, c]
                        + st[pl.ds(1, 1), c] * ext[r, e, :, c]
                        + st[pl.ds(2, 1), c] * ext[r, e + 1, :, c]
                    )

                def grad_at(e):
                    if block != 1:
                        return gm[r, e, :, c]
                    return (
                        ct[pl.ds(0, 1), lanes] * gm[r, e + 1, :, c]
                        + ct[pl.ds(1, 1), lanes] * gm[r, e, :, c]
                        + ct[pl.ds(2, 1), lanes] * gm[r, e - 1, :, c]
                    )

                def step(j, loop):
                    prev, cur, kp_prev, kp_cur, sums, csums = loop
                    nxt = grad_at(j + 3)
                    if block == 1:
                        nxt = jnp.where(j == seg - 1, nxt * in_high, nxt)
                        kp_next = tap3(j + 3)
                        kp_next = jnp.where(j == seg - 1, kp_next * in_high, kp_next)
                        own = gm[r, j + 2, :, c]
                        csums = tuple(s + own * k for s, k in zip(csums, (kp_prev, kp_cur, kp_next)))
                    else:
                        kp_next = kp_cur
                    live = (base + sub * seg + j < info[r]).astype(f32)
                    full = (
                        st[pl.ds(0, 1), c] * nxt + st[pl.ds(1, 1), c] * cur + st[pl.ds(2, 1), c] * prev
                    ) * live
                    full = full.astype(bf16).astype(f32)
                    gsc[r, j] = full
                    sums = (
                        sums[0] + cur * ext[r, j + 1, :, c],
                        sums[1] + cur * ext[r, j + 2, :, c],
                        sums[2] + cur * ext[r, j + 3, :, c],
                        sums[3] + full,
                    )
                    return (cur, nxt, kp_cur, kp_next, sums, csums)

                if block == 1:
                    start = (grad_at(1) * in_low, grad_at(2), tap3(1) * in_low, tap3(2), sums, csums)
                else:
                    start = (grad_at(1), grad_at(2), zero, zero, sums, csums)
                _, _, _, _, sums, csums = lax.fori_loop(0, seg, step, start, unroll=4)
                gp[pl.ds(r * span, span), c] = gsc[r].reshape(span, lane_block).astype(bf16)
            for k in range(3):
                put("short", k, block, lanes, jnp.sum(sums[k], axis=0, keepdims=True))
            put("bias", 0, block, lanes, jnp.sum(sums[3], axis=0, keepdims=True))
            if block == 1:
                for k in range(3):
                    put("cond", k, block, lanes, jnp.sum(csums[k], axis=0, keepdims=True))
        done(block)


row_bias, row_short, row_cond, row_res, row_rate, row_one, row_two, small_rows = 0, 3, 12, 15, 19, 23, 26, 32


def small_put(small):
    def put(kind, k, block, lanes, value):
        row = {"bias": row_bias + block, "short": row_short + 3 * k + block, "cond": row_cond + k}[kind]
        small[pl.ds(row, 1), lanes] = value

    return put


def taps_kernel(rows, span, seq_count, count, outs, info, where, slots, *refs):
    parts, refs = refs[:count], refs[count:]
    gm_h, ext_h, xpt_h, pre1_h, before, after, st, ct, gres, grate, sums_one, sums_two = refs[:12]
    hidden_grad, small = refs[12:14]
    dws, refs = refs[14 : 14 + outs], refs[14 + outs :]
    gsc, gm, ext, xpt, pre1, gp, halo, w, dw, low, stream_sems, in_sems, sems, out_sems = refs
    width = ct.shape[1]
    groups = 3 * width // lane_block
    streams = [
        [
            pltpu.make_async_copy(
                src.at[:, :, :, pl.ds(n * lane_block, lane_block)],
                dst.at[:, :, :, pl.ds(n * lane_block, lane_block)],
                stream_sems.at[k, n],
            )
            for k, (src, dst) in enumerate(((gm_h, gm), (ext_h, ext)))
        ]
        for n in range(groups)
    ]
    late = [pltpu.make_async_copy(xpt_h, xpt, in_sems.at[0]), pltpu.make_async_copy(pre1_h, pre1, in_sems.at[1])]
    copies = fetch_parts(where, parts, w, sems)
    for n in range(groups):
        start_all(streams[n])
        if n == 2:
            late[0].start()
    start_all(copies + late[1:])
    small[...] = jnp.zeros_like(small)
    modes = gres.shape[0]
    small[pl.ds(row_res, modes), :] = gres[...]
    small[pl.ds(row_rate, modes), :] = grate[...]
    small[pl.ds(row_one, 3), :] = sums_one[pl.ds(0, 3), :]
    small[pl.ds(row_two, 3), :] = sums_two[pl.ds(0, 3), :]
    join_rims(rows, before, after, halo)
    sends = []

    def done(block):
        c = pl.ds(block * width, width)
        if block == 0:
            late[0].wait()
        dw[:, c] = jnp.dot(xpt[...], gp[:, c], preferred_element_type=f32).astype(bf16)
        sends.extend(send_parts(slots, dw, dws, out_sems.at[block], c))
        start_all(sends[-outs * dws[0].shape[0] :])

    taps_blocks(
        rows, span, seq_count, info, gm, halo, ext, st, ct, gp, small_put(small), gsc,
        lambda n: wait_all(streams[n]), done,
    )
    wait_all(copies + late[1:])
    low[...] = (contract_last(gp[...], w[...]) + pre1[...]).astype(bf16)
    o, n = iota((span, span), 0), iota((span, span), 1)
    seg = span // segs
    back = (o == (n & (segs - 1)) * seg + lax.shift_right_logical(n, 3)).astype(f32).astype(bf16)
    for r in range(rows):
        moved = jnp.dot(back, low[pl.ds(r * span, span), :], preferred_element_type=f32)
        hidden_grad[r] = moved.astype(bf16)
    wait_all(sends)


def mixer_taps(
    info, where, slots, gm, parts, before, after, ext, st, ct, xpt, pre1, gres, grate, sums_one, sums_two,
    seq_count, dw_shapes,
):
    rows, padded, _, wide = ext.shape
    seg, width = padded - 4, wide // 3
    tokens = rows * seg * segs
    count, outs = len(parts), len(dw_shapes)
    return pl.pallas_call(
        lambda *refs: taps_kernel(rows, seg * segs, seq_count, count, outs, *refs),
        out_shape=(vm((rows, seg * segs, width), bf16), vm((small_rows, width)))
        + tuple(vm(s, bf16) for s in dw_shapes),
        in_specs=smem_spec() * 3 + hbm_specs(count + 4) + vmem_specs(8),
        out_specs=tuple(vmem_specs(2)) + tuple(any_specs(outs)),
        scratch_shapes=[
            pltpu.VMEM((rows, seg, segs, lane_block), f32),
            pltpu.VMEM(gm.shape, f32),
            pltpu.VMEM(ext.shape, f32),
            pltpu.VMEM(xpt.shape, bf16),
            pltpu.VMEM(pre1.shape, f32),
            pltpu.VMEM((tokens, wide), bf16),
            pltpu.VMEM((16, wide), f32),
            pltpu.VMEM((width, wide), bf16),
            pltpu.VMEM((width, wide), bf16),
            pltpu.VMEM((tokens, width), bf16),
            pltpu.SemaphoreType.DMA((2, wide // lane_block)),
            pltpu.SemaphoreType.DMA((2,)),
            pltpu.SemaphoreType.DMA((count,)),
            pltpu.SemaphoreType.DMA((3, outs * dw_shapes[0][0])),
        ],
        compiler_params=pltpu.CompilerParams(vmem_limit_bytes=vmem_cap),
        cost_estimate=spent(1),
        name="mixer_taps",
    )(
        info, where, slots, *parts, gm, ext, xpt, pre1, before, after, st, ct, gres, grate, sums_one, sums_two
    )


def chip_pairs(count):
    first = [(d, d ^ (2 if d % 2 == 0 else 4)) for d in range(count)]
    second = [(d, d ^ (4 if d % 2 == 0 else 2)) for d in range(count)]
    core = [(d, d ^ 1) for d in range(count)]
    return core, first, second


def tie(value, *needs):
    return lax.optimization_barrier((value, needs))[0]


def cross(block, pairs):
    return lax.ppermute(block, "dp", pairs)


def shard_order(me):
    even = (me & 1) == 0
    f = jnp.where(even, 2, 4)
    g = jnp.where(even, 4, 2)
    near = [me, me ^ f, me ^ g, me ^ 6]
    far = [me ^ 1, me ^ 1 ^ g, me ^ 1 ^ f, me ^ 7]
    return jnp.stack(near + far).astype(jnp.int32)


def slot_order(me):
    even = (me & 1) == 0
    f = jnp.where(even, 2, 4)
    g = jnp.where(even, 4, 2)
    mine = [me, me ^ g, me ^ f, me ^ 6]
    theirs = [me ^ 1, me ^ 1 ^ f, me ^ 1 ^ g, me ^ 7]
    return jnp.stack(mine + theirs).astype(jnp.int32)


class Gather:
    def __init__(self, shard, name):
        self.shard, self.name = shard, name
        self.core, self.first, self.second = chip_pairs(8)

    def one(self, *needs):
        with jax.named_scope(self.name + "_one"):
            self.p1 = cross(tie(self.shard, *needs), self.first)
        return self.p1

    def two(self, *needs):
        with jax.named_scope(self.name + "_two"):
            self.p2 = cross(tie(self.shard, *needs), self.second)
        return self.p2

    def three(self, *needs):
        with jax.named_scope(self.name + "_three"):
            self.p3 = cross(tie(self.p1, *needs), self.second)
        return self.p3

    def share(self, early=(), late=()):
        near = [self.shard, self.p1, self.p2, self.p3]
        with jax.named_scope(self.name + "_core"):
            sent = [tie(p, *early) for p in near[:3]] + [tie(near[3], *late)]
            self.parts = near + [cross(p, self.core) for p in sent]
        return self.parts


class Scatter:
    steps = 6

    def __init__(self, mine, theirs, name):
        self.mine, self.theirs, self.name, self.at = mine, theirs, name, 0
        self.core, self.first, self.second = chip_pairs(8)
        self.odd = lax.axis_index("seq") & 1
        self.near = [(i, i ^ 1) for i in range(4)]

    def step(self, *needs):
        self.at += 1
        with jax.named_scope(f"{self.name}_s{self.at}"):
            return getattr(self, f"step{self.at}")(needs)

    def step1(self, needs):
        self.sent = tie(self.theirs, *needs)
        self.got = cross(self.sent, self.core)
        return self.got

    def step2(self, needs):
        got = tie(self.got, *needs)
        self.sent = (self.mine[2:].astype(f32) + got[2:].astype(f32)).astype(bf16)
        self.got1 = cross(self.sent, self.first)
        return self.got1

    def step3(self, needs):
        got1 = tie(self.got1, *needs)
        send = self.mine[1].astype(f32) + self.got[1].astype(f32) + got1[1].astype(f32)
        self.sent = send.astype(bf16)
        self.got2 = cross(self.sent, self.second)
        return self.got2

    def own_half(self, got2, high):
        depth, wide = got2.shape[0] // 2, got2.shape[1]

        def cut(block):
            if block.ndim == 2:
                return lax.dynamic_slice(block, (high * depth, 0), (depth, wide)).astype(f32)
            return lax.dynamic_slice(block, (0, high * depth, 0), (1, depth, wide))[0].astype(f32)

        return cut(self.mine) + cut(self.got) + cut(self.got1) + cut(got2)

    def step4(self, needs):
        self.sent = self.own_half(tie(self.got2, *needs), 1 - self.odd).astype(bf16)
        self.h1 = lax.ppermute(self.sent, "seq", self.near)
        return self.h1

    def step5(self, needs):
        part = self.own_half(self.got2, self.odd) + tie(self.h1, *needs).astype(f32)
        self.part = self.sent = part.astype(bf16)
        self.h2 = lax.ppermute(self.part, "seq", [(i, i ^ 2) for i in range(4)])
        return self.h2

    def step6(self, needs):
        self.total = (self.part.astype(f32) + tie(self.h2, *needs).astype(f32)).astype(bf16)
        self.sent = self.total
        self.h3 = lax.ppermute(self.total, "seq", self.near)
        return self.h3

    def result(self):
        odd = self.odd == 1
        low = jnp.where(odd, self.h3, self.total)
        return jnp.concatenate([low, jnp.where(odd, self.total, self.h3)]).astype(f32)


class Total:
    steps = 5

    def __init__(self, flat, name):
        self.flat, self.name, self.at = flat, name, 0

    def step(self, *needs):
        axis, count, bit = (("dp", 8, 1), ("dp", 8, 2), ("dp", 8, 4), ("seq", 4, 1), ("seq", 4, 2))[self.at]
        self.at += 1
        with jax.named_scope(f"{self.name}_s{self.at}"):
            flat = self.sent = tie(self.flat, *needs)
            got = lax.ppermute(flat, axis, [(d, d ^ bit) for d in range(count)])
            self.flat = flat + got
        return got

    def result(self):
        return self.flat


def advance(last, *flows):
    for f in flows:
        f.step(last)
        last = f.sent
    return last


def local(
    hidden_in,
    seq_len,
    bucket,
    in_weight,
    in_bias,
    short_taps,
    cond_taps,
    mode_residue,
    mode_rate,
    out_weight,
    out_bias,
    norm1_gain,
    norm1_bias,
    gate_weight,
    up_weight,
    down_weight,
    down_bias,
    norm2_gain,
    norm2_bias,
    out_cotangent,
):
    rows, span, width = hidden_in.shape
    tokens, seg = rows * span, span // segs
    dp_count, seq_count = lax.axis_size("dp"), lax.axis_size("seq")
    me, place = lax.axis_index("dp"), lax.axis_index("seq")
    info = jnp.concatenate([seq_len, bucket, place[None]]).astype(jnp.int32)
    chips = dp_count == 8 and seq_count == 4
    up_line = [(i, i + 1) for i in range(seq_count - 1)]
    down_line = [(i + 1, i) for i in range(seq_count - 1)]

    def rims(low, high):
        return lax.ppermute(high, "seq", up_line), lax.ppermute(low, "seq", down_line)

    def dw_shapes(depth, wide):
        return ((4, depth, wide),) * 2 if chips else ((1, depth * dp_count, wide),)

    def line(vec):
        return vec[None]

    def states_of(block, sign):
        return [
            lax.ppermute(block, "seq", [(i, i + sign * k) for i in range(seq_count) if 0 <= i + sign * k < seq_count])
            for k in range(1, seq_count)
        ]

    depth, hidden = gate_weight.shape
    half = hidden // 2
    before, after = rims(
        hidden_in[:, :2].reshape(2 * rows, width), hidden_in[:, span - 2 :].reshape(2 * rows, width)
    )
    shards = (
        jnp.concatenate([in_weight, out_weight], axis=1),
        down_weight,
        jnp.concatenate([gate_weight, up_weight], axis=1),
    )
    if chips:
        w_io, w_d, w_f = (Gather(shard, name) for shard, name in zip(shards, ("w_in_out", "w_down", "w_feed")))
        w_io.one()
        w_io.two()
        w_io.three(w_io.p2, before, after, shards[2], info)
        io_parts = w_io.share((w_io.p1,))
        w_d.one(w_io.p3)
        w_d.two(w_io.p3)
    else:
        io_parts, d_parts, f_parts = ([lax.all_gather(shard, "dp", axis=0, tiled=True)] for shard in shards)
    one = jnp.zeros((1,), jnp.int32)
    where = shard_order(me) if chips else one
    slots = slot_order(me) if chips else one

    xp, xpt, cp, ext, q, keys, vals, ends, dev_end = mixer_enter(
        info, where, hidden_in, out_cotangent, before, after, line(in_bias), short_taps, cond_taps, mode_rate,
        io_parts, seq_count,
    )
    gath = states_of(tie(dev_end, w_d.p1, w_d.p2) if chips else dev_end, 1)
    wait = ()
    if chips:
        w_f.one(dev_end, w_d.p1, w_d.p2)
        w_f.two(dev_end, w_d.p1, w_d.p2)
    long_out, gated_t, carry, n1, s1, low, low_t = mixer_settle(
        tie(info, *wait), where, gath, ends, q, keys, vals, mode_rate, mode_residue, xp,
        line(out_bias), line(norm1_gain), line(norm1_bias), io_parts,
    )
    if chips:
        w_d.three(low)
        d_parts = w_d.share((low,), (low,))
        w_f.three(low, w_f.p2)
        f_parts = w_f.share((low,), (low,))
    layer_out, *grads, pre1, gg, back_ends, back_dev, sums_two, sums_one = feed_core(
        info, where, slots, f_parts, d_parts, io_parts, low, low_t, gated_t, n1, s1, cp, q, line(norm1_gain),
        line(norm1_bias), line(down_bias), line(norm2_gain), line(norm2_bias), mode_rate,
        dw_shapes(*down_weight.shape), dw_shapes(depth, hidden), dw_shapes(depth, width + hidden),
    )
    gg = gg.reshape(q.shape)
    back_gath = states_of(back_dev, -1)
    wait = ()
    if chips:
        s_d, s_a, s_b = (
            Scatter(*grads[2 * k : 2 * k + 2], name) for k, name in enumerate(("g_down", "g_feed", "g_out_feed"))
        )
        s_d.step()
        s_a.step()
        s_b.step()
        wait = advance(back_gath, s_d)
    gm, rim_low, rim_high, g_res, g_rate = mixer_source(
        tie(info, wait), back_gath, back_ends, carry, gg, q, long_out, keys, vals, mode_rate, mode_residue
    )
    before, after = rims(rim_low, rim_high)
    if chips:
        wait = advance(rim_low, s_d, s_a)
    grad_hidden, small, *g_in = mixer_taps(
        tie(info, wait), where, slots, gm, io_parts, before, after, ext, short_taps, cond_taps,
        xpt, pre1, g_res, g_rate, sums_one, sums_two, seq_count, dw_shapes(depth, 3 * width),
    )

    if chips:
        s_in = Scatter(*g_in, "g_in")
        s_small = Total(small, "g_small")
        s_in.step()
        order = (
            s_d, s_a, s_b, s_small, s_in, s_d, s_a, s_b, s_small, s_d, s_in, s_a, s_b, s_small, s_a, s_in,
            s_b, s_small, s_in, s_b, s_small, s_in,
        )
        advance(small, *order)
        flow = (s_in, s_small, s_d, s_a, s_b)
        share_in, small, share_down, share_a, share_b = (f.result() for f in flow)
    else:

        def share(grad):
            own = lax.psum_scatter(grad[0], "dp", scatter_dimension=0, tiled=True)
            return lax.psum(own, "seq").astype(f32)

        share_in, share_down, share_a, share_b = map(share, (*g_in, *grads))
        small = lax.psum(small, ("dp", "seq"))
    share_out = share_b[:, :width]
    share_gate = jnp.concatenate([share_a[:, :half], share_b[:, width : width + half]], axis=1)
    share_up = jnp.concatenate([share_a[:, half:], share_b[:, width + half :]], axis=1)
    modes = mode_rate.shape[0]
    return (
        layer_out, grad_hidden, share_in,
        small[row_bias : row_bias + 3].reshape(3 * width),
        small[row_short : row_short + 9].reshape(3, 3 * width),
        small[row_cond : row_cond + 3],
        small[row_res : row_res + modes],
        small[row_rate : row_rate + modes],
        share_out, small[row_one], small[row_one + 1], small[row_one + 2],
        share_gate, share_up, share_down, small[row_two], small[row_two + 1], small[row_two + 2],
    )


def solution(mesh):
    split, weight, full = P("dp", "seq", None), P("dp", None), P()
    in_specs = (
        split, P("dp"), P("dp"), weight, full, full, full, full, full, weight,
        full, full, full, weight, weight, weight, full, full, full, split,
    )
    out_specs = (
        split, split, weight, full, full, full, full, full, weight, full,
        full, full, weight, weight, weight, full, full, full,
    )
    return jax.shard_map(local, mesh=mesh, in_specs=in_specs, out_specs=out_specs, check_vma=False)
```

time: 464 us -> 350 us (0.75)
  waiting for transfers between devices: 196 us -> 129 us
  Pallas kernels: 158 us -> 104 us
  other arithmetic: 23.5 us -> 33.9 us
  starting transfers between devices: 65.4 us -> 59.4 us
    ppermute x80 -> x60, waiting for transfers between devices: 196 us -> 129 us  [the longest x33 59.1 us: cross(): return lax.ppermute(block, 'dp', pairs)]
    pallas_call x4 -> x1, Pallas kernels: 91.7 us -> 49.8 us  [feed_core(): pl.pallas_call(lambda *refs: core_kernel(rows, seg * segs, count, outs, *...]
    convert_element_type x27 -> x24, other arithmetic: 13.5 us -> 29.8 us  [the longest x4 9.64 us: step2(): self.sent = (self.mine[2:].astype(f32) + got[2:].astype(f32)).astype(bf16)]
    add x10 -> x5, other arithmetic: 7.6 us -> 1.01 us  [step(): self.flat = flat + got]
    ppermute x80 -> x60, starting transfers between devices: 65.4 us -> 59.4 us  [the longest x33 24.4 us: cross(): return lax.ppermute(block, 'dp', pairs)]
    pallas_call x1, Pallas kernels: 22.5 us -> 17 us  [mixer_taps(): pl.pallas_call(lambda *refs: taps_kernel(rows, seg * segs, seq_count, cou...]
  transfers between devices with their start and end apart: 80 -> 60, of which waited for: 37 -> 26; matrix products, arithmetic and copies ran while one was open for 8% -> 12% of each run, Pallas kernels for 16% -> 16%
where the time goes in v2:
time: 350 us; the launch traced here: 346 us
  waiting for transfers between devices  129 us (37%)
  Pallas kernels  104 us (30%)
  starting transfers between devices  59.4 us (17%)
  other arithmetic  33.9 us (10%)
  local copies, waits for them, and re-layouts  18.5 us (5%)
    ppermute x33, waiting for transfers between devices, cross(): return lax.ppermute(block, 'dp', pairs)  59.1 us
    pallas_call x1, Pallas kernels, feed_core(): pl.pallas_call(lambda *refs: core_kernel(rows, seg * segs, count, outs, *...  49.8 us
    ppermute x33, starting transfers between devices, cross(): return lax.ppermute(block, 'dp', pairs)  24.4 us
    ppermute x4, waiting for transfers between devices, step5(): self.h2 = lax.ppermute(self.part, 'seq', [(i, i ^ 2) for i in range(4)])  21.4 us
    pallas_call x1, Pallas kernels, mixer_taps(): pl.pallas_call(lambda *refs: taps_kernel(rows, seg * segs, seq_count, cou...  17 us
    ppermute x4, waiting for transfers between devices, step6(): self.h3 = lax.ppermute(self.total, 'seq', self.near)  15.3 us
    pallas_call x1, Pallas kernels, mixer_enter(): pl.pallas_call(lambda *refs: enter_kernel(rows, span, seq_count, len(part...  14.7 us
    ppermute x6, starting transfers between devices, states_of(): lax.ppermute(block, 'seq', [(i, i + sign * k) for i in range(seq_count) i...  14.1 us
  transfers between devices with their start and end apart: 60, of which 26 were waited for; matrix products, arithmetic and copies ran while one was open for 12% of the time, Pallas kernels for 16%

profile of v2, /device:TPU:0, one launch (start us, length us, event | category | flops | bytes accessed | tf_op | source)
XLA Modules:
  0.0 346.4 jit_solution(2201901819819213317)
XLA Ops:
  2.8 3.0 collective-permute-start.2
  8.1 3.5 %collective-permute-start = (bf16[4,768]{1,0:T(4,128)(2,1)S(1)}, bf16[4,768]{1,0:T(4,128)(2,1)S(1)}, u32[]{:S(2)}, u32[]{:S(2)}) collective-permute-start(bf16[4,768]{1,0:T(4,128)(2,1)S(1)} %reshape.115), channel_id=1, source_target_pairs={{0,1},{1,2},{2,3},{4,5},{5,6},{6,7},{8,9},{9,10},{10,11},{12,13},{... | collective-permute-start | bytes 18440 | tf_op jit(solution)/shard_map/ppermute | solution.py:1114
  17.1 2.3 collective-permute-done.2.refs_11_.refs_6_.refs_20_.refs_4_
  22.3 7.1 %collective-permute-done.4.refs_13_.refs_8_.refs_22_.refs_6_ = bf16[96,3072]{1,0:T(8,128)(2,1)S(1)} collective-permute-done((bf16[96,3072]{1,0:T(8,128)(2,1)S(1)}, bf16[96,3072]{1,0:T(8,128)(2,1)S(1)}, u32[]{:S(2)}, u32[]{:S(2)}) %collective-permute-start.4) | collective-permute-done | bytes 589856 | tf_op jit(solution)/shard_map/w_in_out_three/ppermute | solution.py:942
  34.6 14.7 %mixer_enter.1 = (bf16[512,768]{1,0:T(8,128)(2,1)}, bf16[768,512]{1,0:T(8,128)(2,1)}, bf16[512,768]{1,0:T(8,128)(2,1)}, f32[2,36,8,2304]{3,2,1,0:T(8,128)}, f32[...) custom-call(s32[5]{0:T(128)} %pad_add_fusion.refs_0_, ...), custom_call_target="tpu_custom_call" | custom-call | flops 1100000000 | bytes 1000000 | tf_op jit(solution)/shard_map/mixer_enter/pallas_call | solution.py:207
  50.8 3.9 %collective-permute-start.13 = (f32[2,4,768]{2,1,0:T(4,128)}, f32[2,4,768]{2,1,0:T(4,128)S(1)}, u32[]{:S(2)}, u32[]{:S(2)}) collective-permute-start(f32[2,4,768]{2,1,0:T(4,128)} %get-tuple-element.106), channel_id=1, source_target_pairs={{0,1},{1,2},{2,3},{4,5},{5,6},{6,7},{8,9},{9,10},{10,11},{12,13},{... | collective-permute-start | bytes 73736 | tf_op jit(solution)/shard_map/ppermute | solution.py:1124
  54.7 4.5 %collective-permute-start.14 = (f32[2,4,768]{2,1,0:T(4,128)}, f32[2,4,768]{2,1,0:T(4,128)S(1)}, u32[]{:S(2)}, u32[]{:S(2)}) collective-permute-start(f32[2,4,768]{2,1,0:T(4,128)} %get-tuple-element.106), channel_id=1, source_target_pairs={{0,2},{1,3},{4,6},{5,7},{8,10},{9,11},{12,14},{13,15},{16,18},{17,... | collective-permute-start | bytes 73736 | tf_op jit(solution)/shard_map/ppermute | solution.py:1124
  63.5 13.6 %mixer_settle.1 = (f32[2,32,8,768]{3,2,1,0:T(8,128)}, bf16[768,512]{1,0:T(8,128)(2,1)}, f32[2,4,8,768]{3,2,1,0:T(8,128)}, f32[512,768]{1,0:T(8,128)}, f32[512,12...) custom-call(s32[5]{0:T(128)} %pad_add_fusion.refs_0_, s32[8]{0:T(128)} %stack.46.refs_1_, ...), custom_call_target="tpu_custom_call" | custom-call | flops 1100000000 | bytes 1000000 | tf_op jit(solution)/shard_map/mixer_settle/pallas_call | solution.py:311
  81.0 13.8 %collective-permute-done.16.refs_6_ = bf16[96,6144]{1,0:T(8,128)(2,1)} collective-permute-done((bf16[96,6144]{1,0:T(8,128)(2,1)S(1)}, bf16[96,6144]{1,0:T(8,128)(2,1)}, u32[]{:S(2)}, u32[]{:S(2)}) %collective-permute-start.16) | collective-permute-done | bytes 1179680 | tf_op jit(solution)/shard_map/w_feed_three/ppermute | solution.py:942
  94.8 6.2 %collective-permute-done.21.refs_14_ = bf16[384,768]{1,0:T(8,128)(2,1)S(1)} collective-permute-done((bf16[384,768]{1,0:T(8,128)(2,1)}, bf16[384,768]{1,0:T(8,128)(2,1)S(1)}, u32[]{:S(2)}, u32[]{:S(2)}) %collective-permute-start.21) | collective-permute-done | bytes 589856 | tf_op jit(solution)/shard_map/w_down_three/ppermute | solution.py:942
  105.7 2.3 collective-permute-done.25.refs_18_
  108.9 49.8 %feed_core.1 = (bf16[2,256,768]{2,1,0:T(8,128)(2,1)}, bf16[4,384,768]{2,1,0:T(8,128)(2,1)}, bf16[4,384,768]{2,1,0:T(8,128)(2,1)}, bf16[4,96,3072]{2,1,0:T(8,128)...) custom-call(s32[5]{0:T(128)} %pad_add_fusion.refs_0_, ...), custom_call_target="tpu_custom_call" | custom-call | flops 1100000000 | bytes 1000000 | tf_op jit(solution)/shard_map/feed_core/pallas_call | solution.py:550
  165.2 2.3 collective-permute-done.29.refs_2_
  167.5 3.3 collective-permute-done.30.refs_3_
  170.7 3.4 add_convert_fusion.2
  174.6 9.3 %mixer_source.1 = (f32[2,36,8,2304]{3,2,1,0:T(8,128)}, bf16[4,2304]{1,0:T(4,128)(2,1)}, bf16[4,2304]{1,0:T(4,128)(2,1)}, f32[4,768]{1,0:T(4,128)}, f32[4,768]{1,0:T(4,128)}) custom-call(s32[5]{0:T(128)} %pad_add_fusion.refs_0_, f32[2,4,768]{2,1,0:T(4,128)} %copy-done.25, f32[2,4,768]{2,1,0:T(4,128)} %copy-done.26, f32[2,4,768]{2,1,0:T(4,128)} %copy-done.27, ...), custom_call_target="tpu_custom_call" | custom-call | flops 1100000000 | bytes 1000000 | tf_op jit(solution)/shard_map/mixer_source/pallas_call | solution.py:722
  183.9 6.9 %collective-permute-done.31 = bf16[2,384,768]{2,1,0:T(8,128)(2,1)} collective-permute-done((bf16[2,384,768]{2,1,0:T(8,128)(2,1)}, bf16[2,384,768]{2,1,0:T(8,128)(2,1)}, u32[]{:S(2)}, u32[]{:S(2)}) %collective-permute-start.31) | collective-permute-done | bytes 1179680 | tf_op jit(solution)/shard_map/g_down_s2/ppermute | solution.py:942
  198.1 4.2 %collective-permute-done.33.refs_16_ = bf16[4,2304]{1,0:T(4,128)(2,1)S(1)} collective-permute-done((bf16[4,2304]{1,0:T(4,128)(2,1)}, bf16[4,2304]{1,0:T(4,128)(2,1)S(1)}, u32[]{:S(2)}, u32[]{:S(2)}) %collective-permute-start.33) | collective-permute-done | bytes 18464 | tf_op jit(solution)/shard_map/ppermute | solution.py:1114
  202.9 17.0 %mixer_taps.1 = (bf16[2,256,768]{2,1,0:T(8,128)(2,1)}, f32[32,768]{1,0:T(8,128)}, bf16[4,96,2304]{2,1,0:T(8,128)(2,1)}, bf16[4,96,2304]{2,1,0:T(8,128)(2,1)}) custom-call(s32[5]{0:T(128)} %pad_add_fusion.refs_0_, s32[8]{0:T(128)} %stack.46.refs_1_, s32[8]{0:T(128)} %stack.47.refs_2_, bf16[96,3072]{1,0:T(8,128)(2,1)} %copy-done, bf16[96,3072]{1,0:T(8,128)(2,1)} %copy-done.1, ...), custom_call_target="tpu_custom_call" | custom-call | flops 1100000000 | bytes 1000000 | tf_op jit(solution)/shard_map/mixer_taps/pallas_call | solution.py:900
  222.2 2.5 fusion.5
  224.6 2.9 add_convert_fusion
  234.6 4.2 %collective-permute-done.39 = bf16[192,768]{1,0:T(8,128)(2,1)S(1)} collective-permute-done((bf16[192,768]{1,0:T(8,128)(2,1)}, bf16[192,768]{1,0:T(8,128)(2,1)S(1)}, u32[]{:S(2)}, u32[]{:S(2)}) %collective-permute-start.39) | collective-permute-done | bytes 294944 | tf_op jit(solution)/shard_map/g_down_s4/ppermute | solution.py:1035
  241.1 4.5 %collective-permute-done.43 = bf16[96,3072]{1,0:T(8,128)(2,1)S(1)} collective-permute-done((bf16[96,3072]{1,0:T(8,128)(2,1)}, bf16[96,3072]{1,0:T(8,128)(2,1)S(1)}, u32[]{:S(2)}, u32[]{:S(2)}) %collective-permute-start.43) | collective-permute-done | bytes 589856 | tf_op jit(solution)/shard_map/g_feed_s3/ppermute | solution.py:942
  249.0 4.5 %collective-permute-done.42 = bf16[2,96,3840]{2,1,0:T(8,128)(2,1)} collective-permute-done((bf16[2,96,3840]{2,1,0:T(8,128)(2,1)}, bf16[2,96,3840]{2,1,0:T(8,128)(2,1)}, u32[]{:S(2)}, u32[]{:S(2)}) %collective-permute-start.42) | collective-permute-done | bytes 1474592 | tf_op jit(solution)/shard_map/g_out_feed_s2/ppermute | solution.py:942
  258.2 10.1 %collective-permute-done.38 = bf16[2,96,2304]{2,1,0:T(8,128)(2,1)S(1)} collective-permute-done((bf16[2,96,2304]{2,1,0:T(8,128)(2,1)S(1)}, bf16[2,96,2304]{2,1,0:T(8,128)(2,1)S(1)}, u32[]{:S(2)}, u32[]{:S(2)}) %collective-permute-start.38) | collective-permute-done | bytes 884768 | tf_op jit(solution)/shard_map/g_in_s2/ppermute | solution.py:942
  276.5 9.2 %collective-permute-done.46 = bf16[48,3072]{1,0:T(8,128)(2,1)S(1)} collective-permute-done((bf16[48,3072]{1,0:T(8,128)(2,1)S(1)}, bf16[48,3072]{1,0:T(8,128)(2,1)S(1)}, u32[]{:S(2)}, u32[]{:S(2)}) %collective-permute-start.46) | collective-permute-done | bytes 294944 | tf_op jit(solution)/shard_map/g_feed_s5/ppermute | solution.py:1041
  289.1 10.2 %collective-permute-done.58 = bf16[48,3072]{1,0:T(8,128)(2,1)S(1)} collective-permute-done((bf16[48,3072]{1,0:T(8,128)(2,1)S(1)}, bf16[48,3072]{1,0:T(8,128)(2,1)S(1)}, u32[]{:S(2)}, u32[]{:S(2)}) %collective-permute-start.58) | collective-permute-done | bytes 294944 | tf_op jit(solution)/shard_map/g_feed_s6/ppermute | solution.py:1047
  305.8 6.9 %collective-permute-done.53 = f32[32,768]{1,0:T(8,128)S(1)} collective-permute-done((f32[32,768]{1,0:T(8,128)S(1)}, f32[32,768]{1,0:T(8,128)S(1)}, u32[]{:S(2)}, u32[]{:S(2)}) %collective-permute-start.53) | collective-permute-done | bytes 98336 | tf_op jit(solution)/shard_map/g_small_s4/ppermute | solution.py:1067
  312.7 10.3 %collective-permute-done.54 = bf16[48,3840]{1,0:T(8,128)(2,1)S(1)} collective-permute-done((bf16[48,3840]{1,0:T(8,128)(2,1)S(1)}, bf16[48,3840]{1,0:T(8,128)(2,1)S(1)}, u32[]{:S(2)}, u32[]{:S(2)}) %collective-permute-start.54) | collective-permute-done | bytes 368672 | tf_op jit(solution)/shard_map/g_out_feed_s5/ppermute | solution.py:1041
  323.2 2.8 collective-permute-start.56
  328.0 6.2 %collective-permute-done.56 = f32[32,768]{1,0:T(8,128)S(1)} collective-permute-done((f32[32,768]{1,0:T(8,128)S(1)}, f32[32,768]{1,0:T(8,128)S(1)}, u32[]{:S(2)}, u32[]{:S(2)}) %collective-permute-start.56) | collective-permute-done | bytes 98336 | tf_op jit(solution)/shard_map/g_small_s5/ppermute | solution.py:1067
  337.3 5.0 %collective-permute-done.55 = bf16[48,2304]{1,0:T(8,128)(2,1)S(1)} collective-permute-done((bf16[48,2304]{1,0:T(8,128)(2,1)S(1)}, bf16[48,2304]{1,0:T(8,128)(2,1)S(1)}, u32[]{:S(2)}, u32[]{:S(2)}) %collective-permute-start.55) | collective-permute-done | bytes 221216 | tf_op jit(solution)/shard_map/g_in_s6/ppermute | solution.py:1047
  (234 shorter events, 94.5 us)
Async XLA Ops:
  2.8 16.6 %collective-permute-start.2 = (bf16[96,3072]{1,0:T(8,128)(2,1)S(1)}, bf16[96,3072]{1,0:T(8,128)(2,1)S(1)}, u32[]{:S(2)}, u32[]{:S(2)}) collective-permute-start(bf16[96,3072]{1,0:T(8,128)(2,1)S(1)} %constant_dynamic-update-slice_fusion.2.refs_10_.refs_5_.refs_19_.refs_3_), channel_id=1, source_target_pairs={{0,8},{4,20},{8,0},{12,28},{16,24},{20,4},{24,16},{28,12},{1,9},{5... | collective-permute-start | bytes 1769480 | tf_op jit(solution)/shard_map/w_in_out_one/ppermute | solution.py:942
  5.8 13.6 %collective-permute-start.3 = (bf16[96,3072]{1,0:T(8,128)(2,1)S(1)}, bf16[96,3072]{1,0:T(8,128)(2,1)S(1)}, u32[]{:S(2)}, u32[]{:S(2)}) collective-permute-start(bf16[96,3072]{1,0:T(8,128)(2,1)S(1)} %constant_dynamic-update-slice_fusion.2.refs_10_.refs_5_.refs_19_.refs_3_), channel_id=1, source_target_pairs={{0,16},{4,12},{8,24},{12,4},{16,0},{20,28},{24,8},{28,20},{1,17},{... | collective-permute-start | bytes 1769480 | tf_op jit(solution)/shard_map/w_in_out_two/ppermute | solution.py:942
  29.4 19.9 %collective-permute-start.10 = (bf16[384,768]{1,0:T(8,128)(2,1)}, bf16[384,768]{1,0:T(8,128)(2,1)}, u32[]{:S(2)}, u32[]{:S(2)}) collective-permute-start(bf16[384,768]{1,0:T(8,128)(2,1)} %refs_11_.1), channel_id=1, source_target_pairs={{0,16},{4,12},{8,24},{12,4},{16,0},{20,28},{24,8},{28,20},{1,17},{... | collective-permute-start | bytes 1769480 | tf_op jit(solution)/shard_map/w_down_two/ppermute | solution.py:942
  30.9 18.4 %collective-permute-start.9 = (bf16[384,768]{1,0:T(8,128)(2,1)}, bf16[384,768]{1,0:T(8,128)(2,1)}, u32[]{:S(2)}, u32[]{:S(2)}) collective-permute-start(bf16[384,768]{1,0:T(8,128)(2,1)} %refs_11_.1), channel_id=1, source_target_pairs={{0,8},{4,20},{8,0},{12,28},{16,24},{20,4},{24,16},{28,12},{1,9},{5... | collective-permute-start | bytes 1769480 | tf_op jit(solution)/shard_map/w_down_one/ppermute | solution.py:942
  49.3 29.1 %collective-permute-start.11 = (bf16[96,6144]{1,0:T(8,128)(2,1)}, bf16[96,6144]{1,0:T(8,128)(2,1)S(1)}, u32[]{:S(2)}, u32[]{:S(2)}) collective-permute-start(bf16[96,6144]{1,0:T(8,128)(2,1)} %constant_dynamic-update-slice_fusion.refs_3_), channel_id=1, source_target_pairs={{0,8},{4,20},{8,0},{12,28},{16,24},{20,4},{24,16},{28,12},{1,9},{5... | collective-permute-start | bytes 3538952 | tf_op jit(solution)/shard_map/w_feed_one/ppermute | solution.py:942
  49.8 28.6 %collective-permute-start.12 = (bf16[96,6144]{1,0:T(8,128)(2,1)}, bf16[96,6144]{1,0:T(8,128)(2,1)S(1)}, u32[]{:S(2)}, u32[]{:S(2)}) collective-permute-start(bf16[96,6144]{1,0:T(8,128)(2,1)} %constant_dynamic-update-slice_fusion.refs_3_), channel_id=1, source_target_pairs={{0,16},{4,12},{8,24},{12,4},{16,0},{20,28},{24,8},{28,20},{1,17},{... | collective-permute-start | bytes 3538952 | tf_op jit(solution)/shard_map/w_feed_two/ppermute | solution.py:942
  78.4 16.4 %collective-permute-start.16 = (bf16[96,6144]{1,0:T(8,128)(2,1)S(1)}, bf16[96,6144]{1,0:T(8,128)(2,1)}, u32[]{:S(2)}, u32[]{:S(2)}) collective-permute-start(bf16[96,6144]{1,0:T(8,128)(2,1)S(1)} %collective-permute-done.11.refs_4_), channel_id=1, source_target_pairs={{0,16},{4,12},{8,24},{12,4},{16,0},{20,28},{24,8},{28,20},{1,17},{... | collective-permute-start | bytes 3538952 | tf_op jit(solution)/shard_map/w_feed_three/ppermute | solution.py:942
  79.2 21.8 %collective-permute-start.21 = (bf16[384,768]{1,0:T(8,128)(2,1)}, bf16[384,768]{1,0:T(8,128)(2,1)S(1)}, u32[]{:S(2)}, u32[]{:S(2)}) collective-permute-start(bf16[384,768]{1,0:T(8,128)(2,1)} %collective-permute-done.9.refs_12_), channel_id=1, source_target_pairs={{0,16},{4,12},{8,24},{12,4},{16,0},{20,28},{24,8},{28,20},{1,17},{... | collective-permute-start | bytes 1769480 | tf_op jit(solution)/shard_map/w_down_three/ppermute | solution.py:942
  80.5 20.5 %collective-permute-start.24 = (bf16[384,768]{1,0:T(8,128)(2,1)}, bf16[384,768]{1,0:T(8,128)(2,1)S(1)}, u32[]{:S(2)}, u32[]{:S(2)}) collective-permute-start(bf16[384,768]{1,0:T(8,128)(2,1)} %collective-permute-done.10.refs_13_), channel_id=1, source_target_pairs={{0,4},{4,0},{8,12},{12,8},{16,20},{20,16},{24,28},{28,24},{1,5},{5... | collective-permute-start | bytes 1769480 | tf_op jit(solution)/shard_map/w_down_core/ppermute | solution.py:942
  80.5 21.0 %collective-permute-start.23 = (bf16[384,768]{1,0:T(8,128)(2,1)}, bf16[384,768]{1,0:T(8,128)(2,1)S(1)}, u32[]{:S(2)}, u32[]{:S(2)}) collective-permute-start(bf16[384,768]{1,0:T(8,128)(2,1)} %collective-permute-done.9.refs_12_), channel_id=1, source_target_pairs={{0,4},{4,0},{8,12},{12,8},{16,20},{20,16},{24,28},{28,24},{1,5},{5... | collective-permute-start | bytes 1769480 | tf_op jit(solution)/shard_map/w_down_core/ppermute | solution.py:942
  81.0 24.7 %collective-permute-start.17 = (bf16[96,6144]{1,0:T(8,128)(2,1)}, bf16[96,6144]{1,0:T(8,128)(2,1)}, u32[]{:S(2)}, u32[]{:S(2)}) collective-permute-start(bf16[96,6144]{1,0:T(8,128)(2,1)} %constant_dynamic-update-slice_fusion.refs_3_), channel_id=1, source_target_pairs={{0,4},{4,0},{8,12},{12,8},{16,20},{20,16},{24,28},{28,24},{1,5},{5... | collective-permute-start | bytes 3538952 | tf_op jit(solution)/shard_map/w_feed_core/ppermute | solution.py:942
  158.9 33.4 %collective-permute-start.26 = (bf16[4,96,3072]{2,1,0:T(8,128)(2,1)}, bf16[4,96,3072]{2,1,0:T(8,128)(2,1)S(1)}, u32[]{:S(2)}, u32[]{:S(2)}) collective-permute-start(bf16[4,96,3072]{2,1,0:T(8,128)(2,1)} %get-tuple-element.129), channel_id=1, source_target_pairs={{0,4},{4,0},{8,12},{12,8},{16,20},{20,16},{24,28},{28,24},{1,5},{5... | collective-permute-start | bytes 7077896 | tf_op jit(solution)/shard_map/g_feed_s1/ppermute | solution.py:942
  174.2 16.6 %collective-permute-start.31 = (bf16[2,384,768]{2,1,0:T(8,128)(2,1)}, bf16[2,384,768]{2,1,0:T(8,128)(2,1)}, u32[]{:S(2)}, u32[]{:S(2)}) collective-permute-start(bf16[2,384,768]{2,1,0:T(8,128)(2,1)} %add_convert_fusion.2), channel_id=1, source_target_pairs={{0,8},{4,20},{8,0},{12,28},{16,24},{20,4},{24,16},{28,12},{1,9},{5... | collective-permute-start | bytes 3538952 | tf_op jit(solution)/shard_map/g_down_s2/ppermute | solution.py:942
  174.6 50.0 %collective-permute-start.35 = (bf16[4,96,3840]{2,1,0:T(8,128)(2,1)}, bf16[4,96,3840]{2,1,0:T(8,128)(2,1)}, u32[]{:S(2)}, u32[]{:S(2)}) collective-permute-start(bf16[4,96,3840]{2,1,0:T(8,128)(2,1)} %get-tuple-element.157), channel_id=1, source_target_pairs={{0,4},{4,0},{8,12},{12,8},{16,20},{20,16},{24,28},{28,24},{1,5},{5... | collective-permute-start | bytes 8847368 | tf_op jit(solution)/shard_map/g_out_feed_s1/ppermute | solution.py:942
  194.0 28.2 %collective-permute-start.36 = (bf16[2,96,3072]{2,1,0:T(8,128)(2,1)}, bf16[2,96,3072]{2,1,0:T(8,128)(2,1)}, u32[]{:S(2)}, u32[]{:S(2)}) collective-permute-start(bf16[2,96,3072]{2,1,0:T(8,128)(2,1)} %add_convert_fusion.1), channel_id=1, source_target_pairs={{0,8},{4,20},{8,0},{12,28},{16,24},{20,4},{24,16},{28,12},{1,9},{5... | collective-permute-start | bytes 3538952 | tf_op jit(solution)/shard_map/g_feed_s2/ppermute | solution.py:942
  194.4 25.6 %collective-permute-start.37 = (bf16[384,768]{1,0:T(8,128)(2,1)S(1)}, bf16[384,768]{1,0:T(8,128)(2,1)S(1)}, u32[]{:S(2)}, u32[]{:S(2)}) collective-permute-start(bf16[384,768]{1,0:T(8,128)(2,1)S(1)} %fusion.4), channel_id=1, source_target_pairs={{0,16},{4,12},{8,24},{12,4},{16,0},{20,28},{24,8},{28,20},{1,17},{... | collective-permute-start | bytes 1769480 | tf_op jit(solution)/shard_map/g_down_s3/ppermute | solution.py:942
  227.5 26.0 %collective-permute-start.42 = (bf16[2,96,3840]{2,1,0:T(8,128)(2,1)}, bf16[2,96,3840]{2,1,0:T(8,128)(2,1)}, u32[]{:S(2)}, u32[]{:S(2)}) collective-permute-start(bf16[2,96,3840]{2,1,0:T(8,128)(2,1)} %add_convert_fusion), channel_id=1, source_target_pairs={{0,8},{4,20},{8,0},{12,28},{16,24},{20,4},{24,16},{28,12},{1,9},{5... | collective-permute-start | bytes 4423688 | tf_op jit(solution)/shard_map/g_out_feed_s2/ppermute | solution.py:942
  229.1 16.5 %collective-permute-start.43 = (bf16[96,3072]{1,0:T(8,128)(2,1)}, bf16[96,3072]{1,0:T(8,128)(2,1)S(1)}, u32[]{:S(2)}, u32[]{:S(2)}) collective-permute-start(bf16[96,3072]{1,0:T(8,128)(2,1)} %fusion.5), channel_id=1, source_target_pairs={{0,16},{4,12},{8,24},{12,4},{16,0},{20,28},{24,8},{28,20},{1,17},{... | collective-permute-start | bytes 1769480 | tf_op jit(solution)/shard_map/g_feed_s3/ppermute | solution.py:942
  233.4 34.9 %collective-permute-start.38 = (bf16[2,96,2304]{2,1,0:T(8,128)(2,1)S(1)}, bf16[2,96,2304]{2,1,0:T(8,128)(2,1)S(1)}, u32[]{:S(2)}, u32[]{:S(2)}) collective-permute-start(bf16[2,96,2304]{2,1,0:T(8,128)(2,1)S(1)} %add_convert_fusion.3), channel_id=1, source_target_pairs={{0,8},{4,20},{8,0},{12,28},{16,24},{20,4},{24,16},{28,12},{1,9},{5... | collective-permute-start | bytes 2654216 | tf_op jit(solution)/shard_map/g_in_s2/ppermute | solution.py:942
  240.1 17.9 %collective-permute-start.40 = (bf16[192,768]{1,0:T(8,128)(2,1)S(1)}, bf16[192,768]{1,0:T(8,128)(2,1)S(1)}, u32[]{:S(2)}, u32[]{:S(2)}) collective-permute-start(bf16[192,768]{1,0:T(8,128)(2,1)S(1)} %fusion.10), channel_id=1, source_target_pairs={{0,2},{1,3},{2,0},{3,1},{4,6},{5,7},{6,4},{7,5},{8,10},{9,11},{10,... | collective-permute-start | bytes 884744 | tf_op jit(solution)/shard_map/g_down_s5/ppermute | solution.py:1041
  246.9 23.9 %collective-permute-start.45 = (bf16[48,3072]{1,0:T(8,128)(2,1)S(1)}, bf16[48,3072]{1,0:T(8,128)(2,1)S(1)}, u32[]{:S(2)}, u32[]{:S(2)}) collective-permute-start(bf16[48,3072]{1,0:T(8,128)(2,1)S(1)} %fusion.8), channel_id=1, source_target_pairs={{0,1},{1,0},{2,3},{3,2},{4,5},{5,4},{6,7},{7,6},{8,9},{9,8},{10,11... | collective-permute-start | bytes 884744 | tf_op jit(solution)/shard_map/g_feed_s4/ppermute | solution.py:1035
  255.1 19.2 %collective-permute-start.48 = (bf16[96,3840]{1,0:T(8,128)(2,1)S(1)}, bf16[96,3840]{1,0:T(8,128)(2,1)S(1)}, u32[]{:S(2)}, u32[]{:S(2)}) collective-permute-start(bf16[96,3840]{1,0:T(8,128)(2,1)S(1)} %fusion), channel_id=1, source_target_pairs={{0,16},{4,12},{8,24},{12,4},{16,0},{20,28},{24,8},{28,20},{1,17},{... | collective-permute-start | bytes 2211848 | tf_op jit(solution)/shard_map/g_out_feed_s3/ppermute | solution.py:942
  256.4 16.7 %collective-permute-start.47 = (f32[32,768]{1,0:T(8,128)S(1)}, f32[32,768]{1,0:T(8,128)S(1)}, u32[]{:S(2)}, u32[]{:S(2)}) collective-permute-start(f32[32,768]{1,0:T(8,128)S(1)} %add.251), channel_id=1, source_target_pairs={{0,8},{4,12},{8,0},{12,4},{16,24},{20,28},{24,16},{28,20},{1,9},{5... | collective-permute-start | bytes 294920 | tf_op jit(solution)/shard_map/g_small_s2/ppermute | solution.py:1067
  258.1 15.0 %collective-permute-start.59 = (bf16[192,768]{1,0:T(8,128)(2,1)S(1)}, bf16[192,768]{1,0:T(8,128)(2,1)S(1)}, u32[]{:S(2)}, u32[]{:S(2)}) collective-permute-start(bf16[192,768]{1,0:T(8,128)(2,1)S(1)} %add_convert_fusion.10), channel_id=1, source_target_pairs={{0,1},{1,0},{2,3},{3,2},{4,5},{5,4},{6,7},{7,6},{8,9},{9,8},{10,11... | collective-permute-start | bytes 884744 | tf_op jit(solution)/shard_map/g_down_s6/ppermute | solution.py:1047
  269.5 16.4 %collective-permute-start.44 = (bf16[96,2304]{1,0:T(8,128)(2,1)S(1)}, bf16[96,2304]{1,0:T(8,128)(2,1)S(1)}, u32[]{:S(2)}, u32[]{:S(2)}) collective-permute-start(bf16[96,2304]{1,0:T(8,128)(2,1)S(1)} %fusion.12), channel_id=1, source_target_pairs={{0,16},{4,12},{8,24},{12,4},{16,0},{20,28},{24,8},{28,20},{1,17},{... | collective-permute-start | bytes 1327112 | tf_op jit(solution)/shard_map/g_in_s3/ppermute | solution.py:942
  272.1 13.6 %collective-permute-start.46 = (bf16[48,3072]{1,0:T(8,128)(2,1)S(1)}, bf16[48,3072]{1,0:T(8,128)(2,1)S(1)}, u32[]{:S(2)}, u32[]{:S(2)}) collective-permute-start(bf16[48,3072]{1,0:T(8,128)(2,1)S(1)} %fusion.7), channel_id=1, source_target_pairs={{0,2},{1,3},{2,0},{3,1},{4,6},{5,7},{6,4},{7,5},{8,10},{9,11},{10,... | collective-permute-start | bytes 884744 | tf_op jit(solution)/shard_map/g_feed_s5/ppermute | solution.py:1041
  275.6 24.7 %collective-permute-start.51 = (bf16[48,3840]{1,0:T(8,128)(2,1)S(1)}, bf16[48,3840]{1,0:T(8,128)(2,1)S(1)}, u32[]{:S(2)}, u32[]{:S(2)}) collective-permute-start(bf16[48,3840]{1,0:T(8,128)(2,1)S(1)} %fusion.3), channel_id=1, source_target_pairs={{0,1},{1,0},{2,3},{3,2},{4,5},{5,4},{6,7},{7,6},{8,9},{9,8},{10,11... | collective-permute-start | bytes 1105928 | tf_op jit(solution)/shard_map/g_out_feed_s4/ppermute | solution.py:1035
  287.0 16.5 %collective-permute-start.49 = (bf16[48,2304]{1,0:T(8,128)(2,1)S(1)}, bf16[48,2304]{1,0:T(8,128)(2,1)S(1)}, u32[]{:S(2)}, u32[]{:S(2)}) collective-permute-start(bf16[48,2304]{1,0:T(8,128)(2,1)S(1)} %fusion.13), channel_id=1, source_target_pairs={{0,1},{1,0},{2,3},{3,2},{4,5},{5,4},{6,7},{7,6},{8,9},{9,8},{10,11... | collective-permute-start | bytes 663560 | tf_op jit(solution)/shard_map/g_in_s4/ppermute | solution.py:1035
  301.7 21.3 %collective-permute-start.54 = (bf16[48,3840]{1,0:T(8,128)(2,1)S(1)}, bf16[48,3840]{1,0:T(8,128)(2,1)S(1)}, u32[]{:S(2)}, u32[]{:S(2)}) collective-permute-start(bf16[48,3840]{1,0:T(8,128)(2,1)S(1)} %fusion.2), channel_id=1, source_target_pairs={{0,2},{1,3},{2,0},{3,1},{4,6},{5,7},{6,4},{7,5},{8,10},{9,11},{10,... | collective-permute-start | bytes 1105928 | tf_op jit(solution)/shard_map/g_out_feed_s5/ppermute | solution.py:1041
  304.5 23.3 %collective-permute-start.52 = (bf16[48,2304]{1,0:T(8,128)(2,1)S(1)}, bf16[48,2304]{1,0:T(8,128)(2,1)S(1)}, u32[]{:S(2)}, u32[]{:S(2)}) collective-permute-start(bf16[48,2304]{1,0:T(8,128)(2,1)S(1)} %fusion.15), channel_id=1, source_target_pairs={{0,2},{1,3},{2,0},{3,1},{4,6},{5,7},{6,4},{7,5},{8,10},{9,11},{10,... | collective-permute-start | bytes 663560 | tf_op jit(solution)/shard_map/g_in_s5/ppermute | solution.py:1041
  323.1 20.3 %collective-permute-start.57 = (bf16[48,3840]{1,0:T(8,128)(2,1)S(1)}, bf16[48,3840]{1,0:T(8,128)(2,1)S(1)}, u32[]{:S(2)}, u32[]{:S(2)}) collective-permute-start(bf16[48,3840]{1,0:T(8,128)(2,1)S(1)} %add_convert_fusion.8), channel_id=1, source_target_pairs={{0,1},{1,0},{2,3},{3,2},{4,5},{5,4},{6,7},{7,6},{8,9},{9,8},{10,11... | collective-permute-start | bytes 1105928 | tf_op jit(solution)/shard_map/g_out_feed_s6/ppermute | solution.py:1047
  327.9 14.5 %collective-permute-start.55 = (bf16[48,2304]{1,0:T(8,128)(2,1)S(1)}, bf16[48,2304]{1,0:T(8,128)(2,1)S(1)}, u32[]{:S(2)}, u32[]{:S(2)}) collective-permute-start(bf16[48,2304]{1,0:T(8,128)(2,1)S(1)} %add_convert_fusion.11), channel_id=1, source_target_pairs={{0,1},{1,0},{2,3},{3,2},{4,5},{5,4},{6,7},{7,6},{8,9},{9,8},{10,11... | collective-permute-start | bytes 663560 | tf_op jit(solution)/shard_map/g_in_s6/ppermute | solution.py:1047
  (69 other events, 782.4 us)
